TPU v7x, 128 devices: a whole 4x4x4 slice. The times are simulated.
128 devices in a mesh: scen: 8 (over z_hi, y), col: 16 (over x, z_lo, core).
Axes of the slice: x: 4, y: 4, z: 4 (z_hi: 2, z_lo: 2; z = z_hi * 2 + z_lo), core: 2. Of those that a mesh axis runs over, the one named last changes fastest.
Arguments:
- border: float32 [16, 2048, 16384], P('scen', None, 'col'), may hold values from -0.03314563 to 0.03314563
- pattern: int32 [16, 16, 128], P('scen', None, 'col'), may hold values 0 or 1
- slack: float32 [16, 2048], P('scen'), may hold values from 0.5 to 2
- first_diag: float32 [16384], P('col'), may hold values from 0.25 to 1.75
- rhs: float32 [16384, 256], P('col'), may hold values from -6 to 6
- scen_rhs: float32 [16, 2048, 256], P('scen', 'col'), may hold values from -6 to 6
Outputs:
- reduced: float32 [16, 1024, 256], P('col', 'scen')
- directions: float32 [16, 2048, 256], P('scen', 'col')
All inputs are finite; a program needn't handle non-finite values. No bound on the sum of `pattern` on one device may be relied on, other than what follows from the above.
Results may differ from a plain program's by a relative error of at most 0.0001.
Values sent between devices are 32-bit elements; how exact they have to be, the bound alone decides.
No kernel may reach another device: no remote copies, remote signals or barrier semaphores. Data moves between devices by JAX's collectives and lax.ppermute only.
A program may use at most 128 MiB of HBM per device.

v0:
```python
import jax
import jax.numpy as jnp
from jax import lax
from jax.sharding import PartitionSpec as P

PW = 512


def add_diagonal(rows, first_diag, col_index, pivot_width):
    row_count = rows.shape[0]
    local_rows = jnp.arange(row_count, dtype=jnp.int32)
    panel_cols = jnp.arange(rows.shape[1], dtype=jnp.int32)
    on_diag = (local_rows[:, None] < pivot_width) & (
        panel_cols[None, :] == col_index * pivot_width + local_rows[:, None]
    )
    return rows + jnp.where(on_diag, first_diag[:, None], jnp.zeros_like(rows))


def per_device(border, pattern, slack, first_diag, rhs, scen_rhs):
    col_count = lax.axis_size("col")
    col_index = lax.axis_index("col")
    scen_index = lax.axis_index("scen")
    scen_local, row_total, own_width = border.shape
    row_blocks = pattern.shape[1]
    width_blocks = pattern.shape[2]
    pivot_width = PW // col_count
    row_share = row_total // col_count
    own_share = own_width // lax.axis_size("scen")
    weights = pattern.astype(jnp.float32)[:, :, None, :, None]
    masked = border.reshape(
        scen_local, row_blocks, row_total // row_blocks, width_blocks, own_width // width_blocks
    )
    masked = (masked * weights).reshape(scen_local, row_total, own_width)
    own_panel = masked[:, :, :pivot_width]
    flat_masked = masked.reshape(scen_local * row_total, own_width)
    inverse_slack = (1.0 / slack).reshape(scen_local * row_total, 1)
    shard_cols = lax.all_gather(own_panel, "col", axis=2, tiled=True)
    scaled = shard_cols.reshape(scen_local * row_total, shard_cols.shape[2]) * inverse_slack
    schur_term = lax.dot_general(
        flat_masked,
        scaled,
        (((0,), (0,)), ((), ())),
        precision=lax.Precision.HIGHEST,
        preferred_element_type=jnp.float32,
    )
    my_panel = lax.all_to_all(own_panel, "col", split_axis=1, concat_axis=2, tiled=True)
    schur_rows = lax.psum(schur_term, "scen")
    row_count = schur_rows.shape[0]
    local_rows = jnp.arange(row_count, dtype=jnp.int32)
    schur_rows = add_diagonal(schur_rows, first_diag, col_index, pivot_width)
    pivot_source = schur_rows[:pivot_width]
    pivot_block, rhs_panel = (
        lax.all_gather(pivot_source, "col", axis=0, tiled=True),
        lax.all_gather(rhs[:pivot_width], "col", axis=0, tiled=True),
    )
    factor = jnp.linalg.cholesky(pivot_block)
    forward = lax.linalg.triangular_solve(factor, rhs_panel, left_side=True, lower=True)
    solved = lax.linalg.triangular_solve(
        factor, forward, left_side=True, lower=True, transpose_a=True
    )
    reduced = rhs - jnp.dot(
        schur_rows, solved, precision=lax.Precision.HIGHEST, preferred_element_type=jnp.float32
    )
    mine_forward = lax.dynamic_slice_in_dim(forward, col_index * pivot_width, pivot_width)
    padded = jnp.concatenate(
        [mine_forward, jnp.zeros((own_width - pivot_width, forward.shape[1]), jnp.float32)], axis=0
    )
    reduced = jnp.where((local_rows < pivot_width)[:, None], padded, reduced)
    reduced = lax.dynamic_slice_in_dim(reduced, scen_index * own_share, own_share)
    slack_rows = lax.dynamic_slice_in_dim(slack, col_index * row_share, row_share, 1)
    moved = jnp.dot(
        my_panel.reshape(scen_local * row_share, my_panel.shape[2]),
        solved,
        precision=lax.Precision.HIGHEST,
        preferred_element_type=jnp.float32,
    )
    moved = moved.reshape(scen_local, row_share, solved.shape[1])
    directions = (scen_rhs - moved) / slack_rows[:, :, None]
    return (reduced[None], directions)


def solution(mesh):
    return jax.shard_map(
        per_device,
        mesh=mesh,
        in_specs=(
            P("scen", None, "col"),
            P("scen", None, "col"),
            P("scen", None),
            P("col"),
            P("col", None),
            P("scen", "col", None),
        ),
        out_specs=(P("col", "scen", None), P("scen", "col", None)),
        check_vma=False,
    )
```

profile of v0, /device:TPU:1, one launch (start us, length us, event | category | flops | bytes accessed | tf_op | source)
XLA Modules:
  0.0 503.0 jit_solution(6819866523203971707)
XLA Ops:
  7.9 7.9 %mul.32 = f32[2,16,128,8,128]{2,1,0,4,3:T(8,128)} broadcast(f32[2,16,8]{1,0,2:T(2,128)S(1)} %copy.25), dimensions={0,1,3} | broadcast | bytes 16778240 | tf_op jit(solution)/shard_map/mul | solution.py:33
  15.8 20.7 %mul.33 = f32[2,2048,1024]{1,0,2:T(2,128)} reshape(f32[2,16,128,8,128]{2,1,0,4,3:T(8,128)} %mul.32) | data formatting | bytes 33554432 | tf_op jit(solution)/shard_map/mul | solution.py:33
  36.5 25.4 %copy.26 = f32[2,2048,1024]{1,0,2:T(2,128)} copy(f32[2,2048,1024]{2,1,0:T(8,128)} %param.6) | data formatting | bytes 33554432 | tf_op args[0]
  61.9 17.6 %mul.34 = f32[2,2048,1024]{1,0,2:T(2,128)} multiply(f32[2,2048,1024]{1,0,2:T(2,128)} %copy.26, f32[2,2048,1024]{1,0,2:T(2,128)} %mul.33) | non-fusion elementwise | flops 4194304 | bytes 50331648 | tf_op jit(solution)/shard_map/mul | solution.py:33
  81.9 55.3 %all-gather.3.cloned.1.call-done = f32[2,2048,512]{1,0,2:T(2,128)} async-done(((f32[2,2048,32]{1,0,2:T(2,128)}), f32[2,2048,512]{1,0,2:T(2,128)}) %all-gather.3.cloned.1.call-update) | async-done | bytes 8388624 | tf_op jit(solution)/shard_map/all_gather | solution.py:37
  137.3 9.4 %broadcast_multiply_fusion = f32[8,2048,128]{1,0,2:T(8,128)} fusion(f32[8,2048,128]{1,0,2:T(8,128)} %bitcast.82, f32[8,2048]{1,0:T(8,128)S(1)} %bitcast.85), kind=kLoop, calls=%fused_computation.5 | loop fusion | flops 2097152 | bytes 16842752 | tf_op jit(solution)/shard_map/mul | solution.py:38
  148.5 41.7 %fusion.4 = f32[1024,512]{1,0:T(8,128)} fusion(f32[2,2048,512]{1,0,2:T(2,128)} %bitcast.83, f32[2,2048,1024]{1,0,2:T(2,128)S(1)} %copy-done), kind=kOutput, calls=%fused_computation.9 | convolution fusion | flops 25769803776 | bytes 27262976 | tf_op jit(solution)/shard_map/dot_general | solution.py:39
  190.5 88.5 %all-reduce.4.cloned.1.call-done = f32[1024,512]{1,0:T(8,128)} async-done(((f32[1024,512]{1,0:T(8,128)}), f32[1024,512]{1,0:T(8,128)}) %all-reduce.4.cloned.1.call-update) | async-done | bytes 2097168 | tf_op jit(solution)/shard_map/psum | solution.py:47
  284.2 4.3 reshape.103
  288.5 9.5 %all-to-all-start = ((f32[16,1,8192]{2,1,0:T(1,128)}), f32[16,1,8192]{2,1,0:T(1,128)S(1)}, u32[]{:S(2)}, u32[]{:S(2)}) async-start(f32[16,1,8192]{2,1,0:T(1,128)} %reshape.103), calls=%async_computation | async-start | bytes 1048576 | tf_op jit(solution)/shard_map/all_to_all | solution.py:46
  298.1 26.4 %all_gather.11 = f32[512,256]{1,0:T(8,128)} all-gather(f32[32,256]{1,0:T(8,128)S(1)} %slice-done), channel_id=1, replica_groups=mesh['scen'=8,'col'=16] {'col'}, dimensions={0}, use_global_device_ids=true | all-gather | bytes 557056 | tf_op jit(solution)/shard_map/all_gather | solution.py:54
  326.8 3.1 reshape.104
  329.9 3.8 copy.36
  337.7 11.7 %cholesky.104 = f32[128,128]{1,0:T(8,128)S(1)} custom-call(f32[128,128]{1,0:T(8,128)S(1)} %cholesky.266), custom_call_target="Cholesky" | custom-call | tf_op jit(solution)/shard_map/jit(cholesky)/cholesky | solution.py:56
  349.5 9.8 %custom-call.32 = f32[1,128,128]{1,2,0:T(8,128)S(1)} custom-call(f32[1,128,128]{2,1,0:T(8,128)S(1)} %get-tuple-element.29), custom_call_target="InvertDiagBlocksLowerTriangular" | custom-call | tf_op jit(solution)/shard_map/jit(cholesky)/cholesky | solution.py:56
  362.0 11.7 %cholesky.217 = f32[128,128]{1,0:T(8,128)S(1)} custom-call(f32[128,128]{1,0:T(8,128)S(1)} %cholesky.270), custom_call_target="Cholesky" | custom-call | tf_op jit(solution)/shard_map/jit(cholesky)/cholesky | solution.py:56
  373.7 10.2 %custom-call.33 = f32[1,128,128]{1,2,0:T(8,128)S(1)} custom-call(f32[1,128,128]{2,1,0:T(8,128)S(1)} %get-tuple-element.26), custom_call_target="InvertDiagBlocksLowerTriangular" | custom-call | tf_op jit(solution)/shard_map/jit(cholesky)/cholesky | solution.py:56
  385.5 11.7 %cholesky.238 = f32[128,128]{1,0:T(8,128)S(1)} custom-call(f32[128,128]{1,0:T(8,128)S(1)} %cholesky.275), custom_call_target="Cholesky" | custom-call | tf_op jit(solution)/shard_map/jit(cholesky)/cholesky | solution.py:56
  397.9 9.8 %custom-call.34 = f32[1,128,128]{1,2,0:T(8,128)S(1)} custom-call(f32[1,128,128]{2,1,0:T(8,128)S(1)} %get-tuple-element.23), custom_call_target="InvertDiagBlocksLowerTriangular" | custom-call | tf_op jit(solution)/shard_map/jit(cholesky)/cholesky | solution.py:56
  409.2 11.7 %cholesky.255 = f32[128,128]{1,0:T(8,128)S(1)} custom-call(f32[128,128]{1,0:T(8,128)S(1)} %convolution_subtract_fusion.9), custom_call_target="Cholesky" | custom-call | tf_op jit(solution)/shard_map/jit(cholesky)/cholesky | solution.py:56
  426.2 14.5 %while.1 = (s32[]{:T(128)}, f32[512,512]{1,0:T(8,128)}, s32[4,2]{0,1:T(2,128)S(1)}, f32[4,128,128]{2,1,0:T(8,128)}, s32[]{:T(128)}) while((s32[]{:T(128)}, f32[512,512]{1,0:T(8,128)}, s32[4,2]{0,1:T(2,128)S(1)}, f32[4,128,128]{2,1,0:T(8,128)}, s32[]{:T(128)}) %tuple.31), condition=%wide.while_cond, body=%wide.while_body.sunk | while | flops 2 | bytes 132705 | solution.py:57
  426.8 3.0 bitcast_dynamic-update-slice_fusion.2
  430.5 3.0 bitcast_dynamic-update-slice_fusion.2
  440.7 40.1 %custom-call.35 = f32[4,128,128]{1,2,0:T(8,128)S(1)} custom-call(f32[4,128,128]{2,1,0:T(8,128)} %get-tuple-element.9), custom_call_target="InvertDiagBlocksLowerTriangular" | custom-call | tf_op jit(solution)/shard_map/triangular_solve | solution.py:57
  (91 shorter events, 49.7 us)
Async XLA Ops:
  7.2 130.1 %all-gather.3.cloned.1.call-start = ((), (), s32[]{:S(2)}) async-start(), calls=%async_computation.1 | async-start | bytes 8912896 | tf_op jit(solution)/shard_map/all_gather | solution.py:37
  61.9 20.0 %copy-start.5 = (f32[2,2048]{1,0:T(2,128)S(1)}, f32[2,2048]{1,0:T(2,128)}, u32[]{:S(2)}) copy-start(f32[2,2048]{1,0:T(2,128)} %param.8) | copy-start | bytes 49156
  81.3 197.7 %all-reduce.4.cloned.1.call-start = ((), (), s32[]{:S(2)}) async-start(), calls=%async_computation.2 | async-start | bytes 4194304 | tf_op jit(solution)/shard_map/psum | solution.py:47
  137.3 11.2 %copy-start = (f32[2,2048,1024]{1,0,2:T(2,128)S(1)}, f32[2,2048,1024]{1,0,2:T(2,128)}, u32[]{:S(2)}) copy-start(f32[2,2048,1024]{1,0,2:T(2,128)} %mul.34) | copy-start | bytes 50331652
  148.5 130.5 %copy-start.6 = (f32[1024]{0:T(1024)S(1)}, f32[1024]{0:T(1024)}, u32[]{:S(2)}) copy-start(f32[1024]{0:T(1024)} %param.9) | copy-start | bytes 12292
  148.5 133.4 %copy-start.1 = (f32[2,2048,32]{1,0,2:T(2,128)S(1)}, f32[2,2048,32]{1,0,2:T(2,128)}, u32[]{:S(2)}) copy-start(f32[2,2048,32]{1,0,2:T(2,128)} %slice.148) | copy-start | bytes 1572868
  190.2 107.9 %slice-start = ((f32[1024,256]{1,0:T(8,128)}), f32[32,256]{1,0:T(8,128)S(1)}, s32[]{:S(2)}) async-start(f32[1024,256]{1,0:T(8,128)} %param.10), calls=%async_computation.4 | async-start | bytes 65536 | tf_op jit(solution)/shard_map/slice | solution.py:54
  190.2 143.5 %all-gather.5.cloned.1.call-start = ((), (), s32[]{:S(2)}) async-start(), calls=%async_computation.3 | async-start | bytes 1114112 | tf_op jit(solution)/shard_map/all_gather | solution.py:53
  288.5 36.0 %all-to-all-start = ((f32[16,1,8192]{2,1,0:T(1,128)}), f32[16,1,8192]{2,1,0:T(1,128)S(1)}, u32[]{:S(2)}, u32[]{:S(2)}) async-start(f32[16,1,8192]{2,1,0:T(1,128)} %reshape.103), calls=%async_computation | async-start | bytes 1048576 | tf_op jit(solution)/shard_map/all_to_all | solution.py:46
  336.7 1.0 copy-start.2
  420.9 72.8 %copy-start.7 = (f32[2,128,256]{2,1,0:T(8,128)S(1)}, f32[2,128,256]{2,1,0:T(8,128)}, u32[]{:S(2)}) copy-start(f32[2,128,256]{2,1,0:T(8,128)} %param.11) | copy-start | bytes 786436
  426.2 67.6 %copy-start.3 = (f32[2,16,128,32]{2,3,1,0:T(8,128)S(1)}, f32[2,16,128,32]{2,3,1,0:T(8,128)}, u32[]{:S(2)}) copy-start(f32[2,16,128,32]{2,3,1,0:T(8,128)} %copy.36) | copy-start | bytes 1572868
  480.8 14.7 %copy-start.4 = (f32[1024,256]{1,0:T(8,128)S(1)}, f32[1024,256]{1,0:T(8,128)}, u32[]{:S(2)}) copy-start(f32[1024,256]{1,0:T(8,128)} %param.10) | copy-start | bytes 3145732
Sparse Core Ops, SparseCore 0:
  81.5 55.7 all-gather.2
  190.3 88.6 all-reduce.3
  282.0 40.6 all-gather.4
where the time goes:
time: 508 us; the launch traced here: 503 us
  other arithmetic  154 us (30%)
  waiting for transfers between devices  144 us (28%)
  local copies, waits for them, and re-layouts  89.5 us (18%)
  matrix products  61.7 us (12%)
  blocking collectives  26.4 us (5%)
  between operations  16.9 us (3%)
  starting transfers between devices  10.3 us (2%)
    psum x1, waiting for transfers between devices, per_device(): schur_rows = lax.psum(schur_term, 'scen')  88.5 us
    another operation x14, other arithmetic, per_device(): factor = jnp.linalg.cholesky(pivot_block)  78.9 us
    all_gather x1, waiting for transfers between devices, per_device(): shard_cols = lax.all_gather(own_panel, 'col', axis=2, tiled=True)  55.3 us
    dot_general x1, matrix products, per_device(): lax.dot_general(flat_masked, scaled, (((0,), (0,)), ((), ())), precision=...  41.7 us
    another operation x4, other arithmetic, per_device(): lax.linalg.triangular_solve(factor, rhs_panel, left_side=True, lower=True)  41.4 us
    unnamed x20, local copies, waits for them, and re-layouts  35.5 us
    mul x2, local copies, waits for them, and re-layouts, per_device(): masked = (masked * weights).reshape(scen_local, row_total, own_width)  28.6 us
    all_gather x1, blocking collectives, per_device(): lax.all_gather(rhs[:pivot_width], 'col', axis=0, tiled=True)  26.4 us
  transfers between devices with their start and end apart: 4, of which 2 were waited for; matrix products, arithmetic and copies ran while one was open for 3% of the time, Pallas kernels for 0%

commit v1 on v0

v1 whole, which is shorter than its diff:
```python
import jax
import jax.numpy as jnp
from jax import lax
from jax.experimental import pallas as pl
from jax.experimental.pallas import tpu as pltpu
from jax.sharding import Mesh, PartitionSpec as P

PW = 512
BLOCK = 128
SLAB = 8
F32 = jnp.float32
BF16 = jnp.bfloat16
COL = ("chip", "core")
ALL_CHIPS = ("scen", "chip")
VMEM = pl.BlockSpec(memory_space=pltpu.VMEM)
PARAMS = pltpu.CompilerParams(vmem_limit_bytes=48 << 20)


def dot(a, b, dims, precision=lax.Precision.HIGHEST):
    return lax.dot_general(a, b, (dims, ((), ())), precision=precision, preferred_element_type=F32)


def dot_nn(a, b):
    return dot(a, b, ((1,), (0,)))


def dot_tn(a, b):
    return dot(a, b, ((0,), (0,)))


def dot_nt(a, b):
    return dot(a, b, ((1,), (1,)))


def panel_kernel(pattern, border, rhs, row_out, all_out):
    scen = pl.program_id(0)
    width = rhs.shape[0]
    blocks = row_out.shape[0]
    for i in range(blocks):
        rows = border[0, i * BLOCK : (i + 1) * BLOCK, :].T[:width]
        rows = rows * pattern[scen, i, 0].astype(F32)
        row_out[i, 0] = rows
        all_out[scen * blocks + i] = rows

    @pl.when(scen == 0)
    def _():
        for h in range(2):
            all_out[2 * blocks + h] = rhs[:, h * BLOCK : (h + 1) * BLOCK]


def pivot_kernel(core, mine, slack, diag, out):
    size = diag.shape[1]
    parts = [mine[:, s].reshape(size, BLOCK) for s in range(2)]
    right = jnp.concatenate(parts, axis=1)
    left = jnp.concatenate([parts[s] / slack[s : s + 1, :] for s in range(2)], axis=1)
    rows = lax.broadcasted_iota(jnp.int32, (size, BLOCK), 0)
    cols = lax.broadcasted_iota(jnp.int32, (size, BLOCK), 1)
    for q in range(4):
        piece = dot_nt(left, right[q * BLOCK : (q + 1) * BLOCK])
        piece = piece + jnp.where(rows == cols + q * BLOCK, diag[:, q * BLOCK : (q + 1) * BLOCK], 0.0)
        out[lax.rem(q + 2 * core[0], 4)] = piece


def schur_kernel(border, panel, slack, mask, out, left, right):
    step = pl.program_id(0)
    size = out.shape[1]
    count = panel.shape[1]
    depth = count * BLOCK
    for e in range(count):
        index = step * count + e
        piece = panel[:, e].reshape(size, BLOCK) / slack[pl.ds(index, 1), :]
        high = piece.astype(BF16)
        low = (piece - high.astype(F32)).astype(BF16)
        at = e * BLOCK
        left[:, at : at + BLOCK] = high
        left[:, depth + at : depth + at + BLOCK] = high
        left[:, 2 * depth + at : 2 * depth + at + BLOCK] = low
        rows = border[0, at : at + BLOCK, :] * mask[pl.ds(index, 1), :]
        high = rows.astype(BF16)
        low = (rows - high.astype(F32)).astype(BF16)
        right[at : at + BLOCK, :] = high
        right[depth + at : depth + at + BLOCK, :] = low
        right[2 * depth + at : 2 * depth + at + BLOCK, :] = high

    @pl.when(step == 0)
    def _():
        out[...] = jnp.zeros_like(out)

    wide = 2 * BLOCK
    for n in range(right.shape[1] // wide):
        piece = dot(left[...], right[:, n * wide : (n + 1) * wide], ((1,), (0,)), lax.Precision.DEFAULT)
        out[2 * n] += piece[:, :BLOCK]
        out[2 * n + 1] += piece[:, BLOCK:]


def eliminate(w):
    for first in range(0, BLOCK, SLAB):
        height = BLOCK - first
        cols = [jnp.broadcast_to(w[first:, first + k : first + k + 1], (height, BLOCK)) for k in range(SLAB)]
        left, right = w[first : first + SLAB, :BLOCK], w[first : first + SLAB, BLOCK:]
        lower, upper = [], []
        for k in range(SLAB):
            scale = lax.rsqrt(cols[k][k : k + 1, :])
            square = scale * scale
            for m in range(k + 1, SLAB):
                cols[m] = cols[m] - cols[k] * (cols[k][m : m + 1, :] * square)
            low = cols[k] * scale
            u0 = left[k : k + 1, :] * scale
            u1 = right[k : k + 1, :] * scale
            if k + 1 < SLAB:
                left = left - low[:SLAB] * u0
                right = right - low[:SLAB] * u1
            w[first + k : first + k + 1, BLOCK:] = u1
            lower.append(low)
            upper.append((u0, u1))
        if height > SLAB:
            rest0, rest1 = w[first + SLAB :, :BLOCK], w[first + SLAB :, BLOCK:]
            for k in range(SLAB):
                rest0 = rest0 - lower[k][SLAB:] * upper[k][0]
                rest1 = rest1 - lower[k][SLAB:] * upper[k][1]
            w[first + SLAB :, :BLOCK] = rest0
            w[first + SLAB :, BLOCK:] = rest1


def solve_kernel(core, mine, other, rhs, fwd, sol, m, w, linv):
    size, width = fwd.shape
    steps = size // BLOCK
    for q in range(2):
        here = pl.ds(pl.multiple_of((q + 2 * core[0]) * BLOCK, BLOCK), BLOCK)
        m[:, here] = mine[q]
        here = pl.ds(pl.multiple_of((q + 2 * (1 - core[0])) * BLOCK, BLOCK), BLOCK)
        m[:, here] = other[q]
        m[:, size + q * BLOCK : size + (q + 1) * BLOCK] = rhs[:, q].reshape(size, BLOCK)
    shape = (BLOCK, BLOCK)
    eye = (lax.broadcasted_iota(jnp.int32, shape, 0) == lax.broadcasted_iota(jnp.int32, shape, 1)).astype(F32)

    def outer(step, carry):
        here = pl.ds(pl.multiple_of(step * BLOCK, BLOCK), BLOCK)
        w[:, :BLOCK] = m[here, here]
        w[:, BLOCK:] = eye
        eliminate(w)
        inverse = w[:, BLOCK:]
        linv[step] = inverse
        m[here, :] = dot_nn(inverse, m[here, :])

        def update(later, inner):
            there = pl.ds(pl.multiple_of(later * BLOCK, BLOCK), BLOCK)
            m[there, :] = m[there, :] - dot_tn(m[here, there], m[here, :])
            return inner

        lax.fori_loop(step + 1, steps, update, 0)
        return carry

    lax.fori_loop(0, steps, outer, 0)
    fwd[...] = m[:, size:]
    for step in reversed(range(steps)):
        rows = slice(step * BLOCK, (step + 1) * BLOCK)
        total = m[rows, size:]
        if step + 1 < steps:
            after = (step + 1) * BLOCK
            total = total - dot_nn(m[rows, after:size], sol[after:, :])
        sol[rows, :] = dot_tn(linv[step], total)


def finish_kernel(place, schur, sol, fwd, rhs, mine, slack, scen_rhs, reduced, directions):
    size = sol.shape[0]
    width = size // mine.shape[0]
    total = schur[0]
    for k in range(1, schur.shape[0]):
        total = total + schur[k]
    solved = sol[...]
    result = rhs[...] - dot_tn(total, solved)
    reduced[0] = result

    @pl.when(place[0] == 0)
    def _():
        reduced[0, :width] = fwd[pl.ds(pl.multiple_of(place[1] * width, width), width), :]

    for s in range(2):
        moved = dot_tn(mine[:, s].reshape(size, BLOCK), solved)
        divisor = jnp.broadcast_to(slack[s : s + 1, :], (BLOCK, BLOCK)).T
        for h in range(moved.shape[1] // BLOCK):
            lanes = slice(h * BLOCK, (h + 1) * BLOCK)
            directions[s, :, lanes] = (scen_rhs[s, :, lanes] - moved[:, lanes]) / divisor


def per_device(border, pattern, slack, first_diag, rhs, scen_rhs):
    scen_index = lax.axis_index("scen")
    core_index = lax.axis_index("core")
    col_index = lax.axis_index("chip") * 2 + core_index
    cols = lax.axis_size("chip") * 2
    scens = lax.axis_size("scen")
    chips = lax.axis_size("chip") * scens
    own, row_total, own_width = border.shape
    width = PW // cols
    nrhs = rhs.shape[1]
    blocks = row_total // BLOCK
    smem = pl.BlockSpec(memory_space=pltpu.SMEM)

    row_blocks, all_blocks = pl.pallas_call(
        panel_kernel,
        grid=(own,),
        in_specs=[
            smem,
            pl.BlockSpec((1, row_total, BLOCK), lambda s: (s, 0, 0)),
            pl.BlockSpec((width, nrhs), lambda s: (0, 0)),
        ],
        out_specs=[
            pl.BlockSpec((blocks, 1, width, BLOCK), lambda s: (0, s, 0, 0)),
            pl.BlockSpec((own * blocks + 2, width, BLOCK), lambda s: (0, 0, 0)),
        ],
        out_shape=[
            jax.ShapeDtypeStruct((blocks, own, width, BLOCK), F32),
            jax.ShapeDtypeStruct((own * blocks + 2, width, BLOCK), F32),
        ],
        compiler_params=PARAMS,
        name="panel",
    )(pattern, border, rhs)

    mine = lax.all_to_all(row_blocks, COL, 0, 0, tiled=True)
    gathered = lax.all_gather(all_blocks, COL)

    slack_mine = lax.dynamic_slice_in_dim(slack, col_index * BLOCK, BLOCK, 1)
    diag = jnp.where(scen_index == 0, first_diag[:width], 0.0)
    diag = lax.dynamic_update_slice_in_dim(jnp.zeros((PW,), F32), diag, col_index * width, 0).reshape(1, PW)
    core = core_index.reshape(1).astype(jnp.int32)
    pivots = pl.pallas_call(
        pivot_kernel,
        in_specs=[smem, VMEM, VMEM, VMEM],
        out_specs=VMEM,
        out_shape=jax.ShapeDtypeStruct((4, PW, BLOCK), F32),
        compiler_params=PARAMS,
        name="pivot",
    )(core, mine, slack_mine, diag)

    swap = [(0, 1), (1, 0)]
    pair = pivots[:2] + lax.ppermute(pivots[2:], "core", swap)
    pair = lax.all_to_all(pair.reshape(chips, 2 * PW // chips, BLOCK), ALL_CHIPS, 0, 0, tiled=True)
    share = jnp.sum(pair, axis=0)
    share = lax.all_to_all(jnp.broadcast_to(share[None], pair.shape), ALL_CHIPS, 0, 0, tiled=True)
    half = share.reshape(2, PW, BLOCK)
    other = lax.ppermute(half, "core", swap)

    steps = 8
    count = own * blocks // steps
    mask = jnp.repeat(pattern.reshape(own * blocks, -1).astype(F32), BLOCK, axis=1)
    per_scen = blocks // count
    schur = pl.pallas_call(
        schur_kernel,
        grid=(steps,),
        in_specs=[
            pl.BlockSpec((1, count * BLOCK, own_width), lambda t: (t // per_scen, t % per_scen, 0)),
            pl.BlockSpec((cols, count, width, BLOCK), lambda t: (0, t, 0, 0)),
            pl.BlockSpec((own * blocks, BLOCK), lambda t: (0, 0)),
            pl.BlockSpec((own * blocks, own_width), lambda t: (0, 0)),
        ],
        out_specs=pl.BlockSpec((scens, PW, own_width // scens), lambda t: (0, 0, 0)),
        out_shape=jax.ShapeDtypeStruct((scens, PW, own_width // scens), F32),
        scratch_shapes=[
            pltpu.VMEM((PW, 3 * count * BLOCK), BF16),
            pltpu.VMEM((3 * count * BLOCK, own_width), BF16),
        ],
        compiler_params=PARAMS,
        cost_estimate=pl.CostEstimate(
            flops=6 * own * row_total * own_width * PW, bytes_accessed=28 << 20, transcendentals=0
        ),
        name="schur",
    )(border, gathered, slack.reshape(own * blocks, BLOCK), mask)
    schur = lax.all_to_all(schur, "scen", 0, 0, tiled=True)

    fwd, sol = pl.pallas_call(
        solve_kernel,
        grid=(1,),
        in_specs=[
            smem,
            pl.BlockSpec((2, PW, BLOCK), lambda t: (0, 0, 0)),
            pl.BlockSpec((2, PW, BLOCK), lambda t: (0, 0, 0)),
            pl.BlockSpec((cols, 2, width, BLOCK), lambda t: (0, own * blocks // 2, 0, 0)),
        ],
        out_specs=[pl.BlockSpec((PW, nrhs), lambda t: (0, 0))] * 2,
        out_shape=[jax.ShapeDtypeStruct((PW, nrhs), F32)] * 2,
        scratch_shapes=[
            pltpu.VMEM((PW, PW + nrhs), F32),
            pltpu.VMEM((BLOCK, 2 * BLOCK), F32),
            pltpu.VMEM((PW // BLOCK, BLOCK, BLOCK), F32),
        ],
        compiler_params=PARAMS,
        cost_estimate=pl.CostEstimate(flops=20 << 30, bytes_accessed=3 << 20, transcendentals=0),
        name="solve",
    )(core, half, other, gathered)

    place = jnp.stack([scen_index, col_index]).astype(jnp.int32)
    own_share = own_width // scens
    reduced, directions = pl.pallas_call(
        finish_kernel,
        grid_spec=pltpu.PrefetchScalarGridSpec(
            num_scalar_prefetch=1,
            grid=(1,),
            in_specs=[
                pl.BlockSpec((scens, PW, own_share), lambda t, place: (0, 0, 0)),
                pl.BlockSpec((PW, nrhs), lambda t, place: (0, 0)),
                pl.BlockSpec((PW, nrhs), lambda t, place: (0, 0)),
                pl.BlockSpec((own_share, nrhs), lambda t, place: (place[0], 0)),
                pl.BlockSpec((cols, own, width, BLOCK), lambda t, place: (0, 0, 0, 0)),
                pl.BlockSpec((own, BLOCK), lambda t, place: (0, 0)),
                pl.BlockSpec((own, BLOCK, nrhs), lambda t, place: (0, 0, 0)),
            ],
            out_specs=[
                pl.BlockSpec((1, own_share, nrhs), lambda t, place: (0, 0, 0)),
                pl.BlockSpec((own, BLOCK, nrhs), lambda t, place: (0, 0, 0)),
            ],
        ),
        out_shape=[
            jax.ShapeDtypeStruct((1, own_share, nrhs), F32),
            jax.ShapeDtypeStruct((own, BLOCK, nrhs), F32),
        ],
        compiler_params=PARAMS,
        name="finish",
    )(place, schur, sol, fwd, rhs, mine, slack_mine, scen_rhs)
    return reduced, directions


def solution(mesh):
    scens, cols = mesh.devices.shape
    split = Mesh(mesh.devices.reshape(scens, cols // 2, 2), ("scen", "chip", "core"))
    return jax.shard_map(
        per_device,
        mesh=split,
        in_specs=(
            P("scen", None, COL),
            P("scen", None, COL),
            P("scen", None),
            P(COL),
            P(COL, None),
            P("scen", COL, None),
        ),
        out_specs=(P(COL, "scen", None), P("scen", COL, None)),
        check_vma=False,
    )
```

time: 508 us -> 157 us (0.31)
  other arithmetic: 154 us -> 0.9 us
  waiting for transfers between devices: 144 us -> 30.2 us
  local copies, waits for them, and re-layouts: 89.5 us -> 8.69 us
  matrix products: 61.7 us -> 0 us
  Pallas kernels: 0 us -> 53.2 us
  starting transfers between devices: 10.3 us -> 20.1 us
    another operation x18 -> x1, other arithmetic: 120 us -> 0.08 us  [per_device(): place = jnp.stack([scen_index, col_index]).astype(jnp.int32)]
    psum x1 -> x0, waiting for transfers between devices: 88.5 us -> none  [per_device(): schur_rows = lax.psum(schur_term, 'scen')]
    all_gather x2 -> x1, waiting for transfers between devices: 55.3 us -> 0.01 us  [per_device(): gathered = lax.all_gather(all_blocks, COL)]
    pallas_call x0 -> x5, Pallas kernels: none -> 53.2 us  [the longest x1 23.5 us: per_device(): pl.pallas_call(solve_kernel, grid=(1,), in_specs=[smem, pl.BlockSpec((2,...]
    dot_general x3 -> x0, matrix products: 45.2 us -> none  [the longest x1 41.7 us: per_device(): lax.dot_general(flat_masked, scaled, (((0,), (0,)), ((), ())), precision=...]
    all_to_all x1 -> x3, waiting for transfers between devices: 0.01 us -> 28.7 us  [the longest x1 16.3 us: per_device(): lax.all_to_all(jnp.broadcast_to(share[None], pair.shape), ALL_CHIPS, 0, 0...]
    mul x2 -> x0, local copies, waits for them, and re-layouts: 28.6 us -> none  [per_device(): masked = (masked * weights).reshape(scen_local, row_total, own_width)]
    unnamed x20 -> x22, local copies, waits for them, and re-layouts: 35.5 us -> 7.43 us
  transfers between devices with their start and end apart: 4 -> 6, of which waited for: 2 -> 4; matrix products, arithmetic and copies ran while one was open for 3% -> 1% of each run, Pallas kernels for 0% -> 31%
where the time goes in v1:
time: 157 us; the launch traced here: 155 us
  Pallas kernels  53.2 us (34%)
  waiting for transfers between devices  30.2 us (19%)
  blocking collectives  27.9 us (18%)
  starting transfers between devices  20.1 us (13%)
  between operations  14.2 us (9%)
  local copies, waits for them, and re-layouts  8.69 us (6%)
    all_to_all x1, blocking collectives, per_device(): lax.all_to_all(pair.reshape(chips, 2 * PW // chips, BLOCK), ALL_CHIPS, 0,...  27.9 us
    pallas_call x1, Pallas kernels, per_device(): pl.pallas_call(solve_kernel, grid=(1,), in_specs=[smem, pl.BlockSpec((2,...  23.5 us
    pallas_call x1, Pallas kernels, per_device(): pl.pallas_call(schur_kernel, grid=(steps,), in_specs=[pl.BlockSpec((1, co...  22.6 us
    all_to_all x1, waiting for transfers between devices, per_device(): lax.all_to_all(jnp.broadcast_to(share[None], pair.shape), ALL_CHIPS, 0, 0...  16.3 us
    all_to_all x1, waiting for transfers between devices, per_device(): mine = lax.all_to_all(row_blocks, COL, 0, 0, tiled=True)  9.3 us
    unnamed x22, local copies, waits for them, and re-layouts  7.43 us
    all_to_all x1, starting transfers between devices, per_device(): mine = lax.all_to_all(row_blocks, COL, 0, 0, tiled=True)  7.2 us
    all_to_all x1, starting transfers between devices, per_device(): lax.all_to_all(jnp.broadcast_to(share[None], pair.shape), ALL_CHIPS, 0, 0...  6.14 us
  transfers between devices with their start and end apart: 6, of which 4 were waited for; matrix products, arithmetic and copies ran while one was open for 1% of the time, Pallas kernels for 31%

profile of v1, /device:TPU:1, one launch (start us, length us, event | category | flops | bytes accessed | tf_op | source)
XLA Modules:
  0.0 155.3 jit_solution(1284650281300341186)
XLA Ops:
  7.2 0.8 copy.12.pattern
  8.0 1.2 copy-done
  9.2 2.8 %panel.1 = (f32[16,2,32,128]{3,2,1,0:T(8,128)}, f32[34,32,128]{2,1,0:T(8,128)}) custom-call(s32[2,16,8]{2,1,0:T(8,128)S(1)} %copy.12.pattern, f32[2,2048,1024]{2,1,0:T(8,128)} %border.3, f32[1024,256]{1,0:T(8,128)S(1)} %copy-done), custom_call_target="tpu_custom_call" | custom-call | tf_op jit(solution)/shard_map/panel/pallas_call | solution.py:200
  12.1 7.2 %all-to-all-start.1 = ((f32[16,2,32,128]{3,2,1,0:T(8,128)}), f32[16,2,32,128]{3,2,1,0:T(8,128)S(1)}, u32[]{:S(2)}, u32[]{:S(2)}) async-start(f32[16,2,32,128]{3,2,1,0:T(8,128)} %get-tuple-element.7), calls=%async_computation.1 | async-start | bytes 1048576 | tf_op jit(solution)/shard_map/all_to_all | solution.py:220
  19.3 0.7 fusion
  20.2 9.3 %all-to-all-done.1.mine = f32[16,2,32,128]{3,2,1,0:T(8,128)S(1)} async-done(((f32[16,2,32,128]{3,2,1,0:T(8,128)}), f32[16,2,32,128]{3,2,1,0:T(8,128)S(1)}, u32[]{:S(2)}, u32[]{:S(2)}) %all-to-all-start.1) | async-done | bytes 524320 | tf_op jit(solution)/shard_map/all_to_all | solution.py:220
  29.5 1.8 %pivot.1 = f32[4,512,128]{2,1,0:T(8,128)S(1)} custom-call(s32[1]{0:T(128)} %bitcast.4.core, f32[16,2,32,128]{3,2,1,0:T(8,128)S(1)} %all-to-all-done.1.mine, f32[2,128]{1,0:T(2,128)S(1)} %constant_dynamic-slice_fusion.slack, f32[1,512]{1,0:T(1,128)S(1)} %dynamic_update_slice.4.diag), custom_call_target="tpu_custom_call" | custom-call | tf_op jit(solution)/shard_map/pivot/pallas_call | solution.py:227
  31.3 0.7 collective-permute-start
  32.0 1.5 collective-permute-done
  33.6 27.9 %all_to_all.20 = f32[64,16,128]{2,1,0:T(8,128)S(1)} all-to-all(f32[64,16,128]{2,1,0:T(8,128)S(1)} %bitcast.16), channel_id=1, replica_groups=mesh['scen'=8,'chip'=8,'core'=2] {'scen','chip'}, dimensions={0} | all-to-all | bytes 1048576 | tf_op jit(solution)/shard_map/all_to_all | solution.py:238
  61.6 0.8 broadcast_in_dim.19
  62.5 6.1 %all-to-all-start.3 = ((f32[64,16,128]{2,1,0:T(8,128)}), f32[64,16,128]{2,1,0:T(8,128)S(1)}, u32[]{:S(2)}, u32[]{:S(2)}) async-start(f32[64,16,128]{2,1,0:T(8,128)} %broadcast_in_dim.19), calls=%async_computation.3 | async-start | bytes 1048576 | tf_op jit(solution)/shard_map/all_to_all | solution.py:240
  68.9 16.3 %all-to-all-done.3 = f32[64,16,128]{2,1,0:T(8,128)S(1)} async-done(((f32[64,16,128]{2,1,0:T(8,128)}), f32[64,16,128]{2,1,0:T(8,128)S(1)}, u32[]{:S(2)}, u32[]{:S(2)}) %all-to-all-start.3) | async-done | bytes 524320 | tf_op jit(solution)/shard_map/all_to_all | solution.py:240
  85.2 2.3 %collective-permute-start.1 = (f32[2,512,128]{2,1,0:T(8,128)S(1)}, f32[2,512,128]{2,1,0:T(8,128)}, u32[]{:S(2)}, u32[]{:S(2)}) collective-permute-start(f32[2,512,128]{2,1,0:T(8,128)S(1)} %bitcast.13), channel_id=1, source_target_pairs={{0,1},{1,0},{2,3},{3,2},{4,5},{5,4},{6,7},{7,6},{8,9},{9,8},{10,11... | collective-permute-start | bytes 1572872 | tf_op jit(solution)/shard_map/ppermute | solution.py:242
  87.6 22.6 %schur.1 = f32[8,512,128]{2,1,0:T(8,128)S(1)} custom-call(f32[2,2048,1024]{2,1,0:T(8,128)} %border.3, f32[16,34,32,128]{3,2,1,0:T(8,128)} %bitcast.19, f32[32,128]{1,0:T(8,128)S(1)} %reshape.27.slack, f32[32,1024]{1,0:T(8,128)S(1)} %bitcast.15), custom_call_target="tpu_custom_call" | custom-call | flops 12884901888 | bytes 29360128 | tf_op jit(solution)/shard_map/schur/pallas_call | solution.py:248
  110.2 1.3 copy-done.2
  111.5 3.8 %all-to-all-start = ((f32[8,512,128]{2,1,0:T(8,128)}), f32[8,512,128]{2,1,0:T(8,128)S(1)}, u32[]{:S(2)}, u32[]{:S(2)}) async-start(f32[8,512,128]{2,1,0:T(8,128)} %copy-done.2), calls=%async_computation | async-start | bytes 4194304 | tf_op jit(solution)/shard_map/all_to_all | solution.py:269
  115.3 1.0 copy-done.6
  116.3 23.5 %solve.1 = (f32[512,256]{1,0:T(8,128)S(1)}, f32[512,256]{1,0:T(8,128)S(1)}) custom-call(s32[1]{0:T(128)} %bitcast.4.core, f32[2,512,128]{2,1,0:T(8,128)S(1)} %bitcast.14, f32[2,512,128]{2,1,0:T(8,128)} %collective-permute-done.1.other, f32[16,34,32,128]{3,2,1,0:T(8,128)} %bitcast.20), custom_call_target="tpu_custom_call" | custom-call | flops 21474836480 | bytes 3145728 | tf_op jit(solution)/shard_map/solve/pallas_call | solution.py:271
  139.9 0.8 copy-done.3
  140.6 3.1 %all-to-all-done.schur = f32[8,512,128]{2,1,0:T(8,128)S(1)} async-done(((f32[8,512,128]{2,1,0:T(8,128)}), f32[8,512,128]{2,1,0:T(8,128)S(1)}, u32[]{:S(2)}, u32[]{:S(2)}) %all-to-all-start) | async-done | bytes 2097184 | tf_op jit(solution)/shard_map/all_to_all | solution.py:269
  143.7 1.2 copy-done.1
  144.9 1.0 copy-done.4
  146.0 2.5 %finish.1 = (f32[1,128,256]{2,1,0:T(8,128)}, f32[2,128,256]{2,1,0:T(8,128)}) custom-call(s32[2]{0:T(128)S(1)} %pad_add_fusion.place, f32[8,512,128]{2,1,0:T(8,128)S(1)} %all-to-all-done.schur, f32[512,256]{1,0:T(8,128)S(1)} %copy-done.4, f32[512,256]{1,0:T(8,128)S(1)} %get-tuple-element.9.fwd, f32[1024,256]{1,0:T(8,128)S(1)} %copy-done.1, ...), custom_call_target="tpu_custom_call" | custom-call | tf_op jit(solution)/shard_map/finish/pallas_call | solution.py:294
  (30 shorter events, 0.7 us)
Async XLA Ops:
  7.2 80.4 %all-gather.3.cloned.1.call-start = ((), (), s32[]{:S(2)}) async-start(), calls=%async_computation.4 | async-start | bytes 9469952 | tf_op jit(solution)/shard_map/all_gather | solution.py:221
  8.0 1.2 copy-start
  9.2 10.9 %copy-start.9 = (f32[2,2048]{1,0:T(2,128)S(1)}, f32[2,2048]{1,0:T(2,128)}, u32[]{:S(2)}) copy-start(f32[2,2048]{1,0:T(2,128)} %param.8) | copy-start | bytes 49156
  12.0 56.6 %copy-start.8 = (s32[2,16,8]{1,2,0:T(8,128)S(1)}, s32[2,16,8]{1,2,0:T(8,128)}, u32[]{:S(2)}) copy-start(s32[2,16,8]{1,2,0:T(8,128)} %param.7) | copy-start | bytes 3076
  12.1 17.4 %all-to-all-start.1 = ((f32[16,2,32,128]{3,2,1,0:T(8,128)}), f32[16,2,32,128]{3,2,1,0:T(8,128)S(1)}, u32[]{:S(2)}, u32[]{:S(2)}) async-start(f32[16,2,32,128]{3,2,1,0:T(8,128)} %get-tuple-element.7), calls=%async_computation.1 | async-start | bytes 1048576 | tf_op jit(solution)/shard_map/all_to_all | solution.py:220
  31.3 2.2 %collective-permute-start = (f32[2,512,128]{2,1,0:T(8,128)S(1)}, f32[2,512,128]{2,1,0:T(8,128)S(1)}, u32[]{:S(2)}, u32[]{:S(2)}) collective-permute-start(f32[2,512,128]{2,1,0:T(8,128)S(1)} %slice.13), channel_id=1, source_target_pairs={{0,1},{1,0},{2,3},{3,2},{4,5},{5,4},{6,7},{7,6},{8,9},{9,8},{10,11... | collective-permute-start | bytes 1572872 | tf_op jit(solution)/shard_map/ppermute | solution.py:237
  62.5 22.8 %all-to-all-start.3 = ((f32[64,16,128]{2,1,0:T(8,128)}), f32[64,16,128]{2,1,0:T(8,128)S(1)}, u32[]{:S(2)}, u32[]{:S(2)}) async-start(f32[64,16,128]{2,1,0:T(8,128)} %broadcast_in_dim.19), calls=%async_computation.3 | async-start | bytes 1048576 | tf_op jit(solution)/shard_map/all_to_all | solution.py:240
  85.2 24.9 %copy-start.5 = (f32[64,16,128]{2,1,0:T(8,128)}, f32[64,16,128]{2,1,0:T(8,128)S(1)}, u32[]{:S(2)}) copy-start(f32[64,16,128]{2,1,0:T(8,128)S(1)} %all-to-all-done.3) | copy-start | bytes 1572868
  85.2 30.1 %collective-permute-start.1 = (f32[2,512,128]{2,1,0:T(8,128)S(1)}, f32[2,512,128]{2,1,0:T(8,128)}, u32[]{:S(2)}, u32[]{:S(2)}) collective-permute-start(f32[2,512,128]{2,1,0:T(8,128)S(1)} %bitcast.13), channel_id=1, source_target_pairs={{0,1},{1,0},{2,3},{3,2},{4,5},{5,4},{6,7},{7,6},{8,9},{9,8},{10,11... | collective-permute-start | bytes 1572872 | tf_op jit(solution)/shard_map/ppermute | solution.py:242
  110.2 1.3 copy-start.2
  111.5 32.2 %all-to-all-start = ((f32[8,512,128]{2,1,0:T(8,128)}), f32[8,512,128]{2,1,0:T(8,128)S(1)}, u32[]{:S(2)}, u32[]{:S(2)}) async-start(f32[8,512,128]{2,1,0:T(8,128)} %copy-done.2), calls=%async_computation | async-start | bytes 4194304 | tf_op jit(solution)/shard_map/all_to_all | solution.py:269
  115.3 1.0 copy-start.6
  116.3 27.4 %copy-start.7 = (f32[2,128,256]{2,1,0:T(8,128)S(1)}, f32[2,128,256]{2,1,0:T(8,128)}, u32[]{:S(2)}) copy-start(f32[2,128,256]{2,1,0:T(8,128)} %scen_rhs.1) | copy-start | bytes 786436
  139.8 0.8 copy-start.3
  143.7 1.2 copy-start.1
  144.9 1.0 copy-start.4
Sparse Core Ops, SparseCore 0:
  12.2 70.8 all-gather.2

commit v2 on v1

v2 whole, which is shorter than its diff:
```python
import jax
import jax.numpy as jnp
from jax import lax
from jax.experimental import pallas as pl
from jax.experimental.pallas import tpu as pltpu
from jax.sharding import Mesh, PartitionSpec as P

PW = 512
BLOCK = 128
SLAB = 8
STEPS = 8
F32 = jnp.float32
BF16 = jnp.bfloat16
COL = ("x", "z", "core")
SWAP = [(0, 1), (1, 0)]
ALL_CHIPS = ("scen", "x", "z")
DONE = jax.ShapeDtypeStruct((8, 128), F32)
DONE_SPEC = pl.BlockSpec((8, 128), lambda t: (0, 0))
ANY = pl.BlockSpec(memory_space=pl.ANY)
VMEM = pl.BlockSpec(memory_space=pltpu.VMEM)
LIMIT = 60 << 20
PARAMS = pltpu.CompilerParams(vmem_limit_bytes=LIMIT)


def dot(a, b, dims, precision=lax.Precision.HIGHEST):
    return lax.dot_general(a, b, (dims, ((), ())), precision=precision, preferred_element_type=F32)


def dot_nn(a, b):
    return dot(a, b, ((1,), (0,)))


def dot_tn(a, b):
    return dot(a, b, ((0,), (0,)))


def dot_nt(a, b):
    return dot(a, b, ((1,), (1,)))


def panel_kernel(pattern, border, rhs, row_out, all_out):
    scen = pl.program_id(0)
    width = rhs.shape[0]
    blocks = row_out.shape[0]
    for i in range(blocks):
        rows = border[0, i * BLOCK : (i + 1) * BLOCK, :].T[:width]
        rows = rows * pattern[scen, i, 0].astype(F32)
        row_out[i, 0] = rows
        all_out[scen * blocks + i] = rows

    @pl.when(scen == 0)
    def _():
        for h in range(2):
            all_out[2 * blocks + h] = rhs[:, h * BLOCK : (h + 1) * BLOCK]


def pivot_kernel(core, mine, slack, diag, *refs):
    kept, sent = refs[4], refs[5]
    size = diag.shape[1]
    parts = [mine[:, s].reshape(size, BLOCK) for s in range(2)]
    right = jnp.concatenate(parts, axis=1)
    left = jnp.concatenate([parts[s] / slack[s : s + 1, :] for s in range(2)], axis=1)
    rows = lax.broadcasted_iota(jnp.int32, (size, BLOCK), 0)
    cols = lax.broadcasted_iota(jnp.int32, (size, BLOCK), 1)
    for q in range(4):
        piece = dot_nt(left, right[q * BLOCK : (q + 1) * BLOCK])
        piece = piece + jnp.where(rows == cols + q * BLOCK, diag[:, q * BLOCK : (q + 1) * BLOCK], 0.0)

        @pl.when(core[0] == q // 2)
        def _():
            kept[q % 2] = piece

        @pl.when(core[0] != q // 2)
        def _():
            sent[q % 2] = piece


def total_kernel(pair, *refs):
    shared = refs[5]
    total = pair[0]
    for k in range(1, pair.shape[0]):
        total = total + pair[k]
    for k in range(pair.shape[0]):
        shared[k] = total


def split(values):
    high = values.astype(BF16)
    return high, (values - high.astype(F32)).astype(BF16)


def mask_kernel(pattern, border, _, out, done):
    step = pl.program_id(0)
    done[...] = jnp.zeros_like(done)
    depth, width = border.shape[1:]
    count = depth // BLOCK
    for e in range(count):
        index = step * count + e
        at = e * BLOCK
        for c in range(width // BLOCK):
            lanes = slice(c * BLOCK, (c + 1) * BLOCK)
            weight = pattern[index, c].astype(F32)
            high, low = split(border[0, at : at + BLOCK, lanes] * weight)
            out[0, at : at + BLOCK, lanes] = high
            out[0, depth + at : depth + at + BLOCK, lanes] = low


def mask_parts(pattern, border, after):
    scenarios, row_total, own_width = border.shape
    depth = scenarios * row_total // STEPS
    per_scen = row_total // depth
    return pl.pallas_call(
        mask_kernel,
        grid=(STEPS,),
        in_specs=[
            pl.BlockSpec(memory_space=pltpu.SMEM),
            pl.BlockSpec((1, depth, own_width), lambda t: (t // per_scen, t % per_scen, 0)),
            ANY,
        ],
        out_specs=[pl.BlockSpec((1, 2 * depth, own_width), lambda t: (t, 0, 0)), DONE_SPEC],
        out_shape=[jax.ShapeDtypeStruct((STEPS, 2 * depth, own_width), BF16), DONE],
        compiler_params=pltpu.CompilerParams(vmem_limit_bytes=LIMIT),
        cost_estimate=pl.CostEstimate(flops=0, bytes_accessed=40 << 20, transcendentals=0),
        name="mask",
    )(pattern, border, after)


def follow_kernel(*refs):
    del refs


def schur_kernel(*refs):
    masked, slack, _, _, *pieces, out, done, left = refs
    step = pl.program_id(0)
    done[...] = jnp.zeros_like(done)
    count, width = pieces[0].shape[:2]
    depth = count * BLOCK
    for e in range(count):
        inverse = 1.0 / slack[pl.ds(step * count + e, 1), :]
        at = e * BLOCK
        for k, piece in enumerate(pieces):
            high, low = split(piece[e] * inverse)
            rows = slice(k * width, (k + 1) * width)
            left[rows, at : at + BLOCK] = high
            left[rows, depth + at : depth + at + BLOCK] = high
            left[rows, 2 * depth + at : 2 * depth + at + BLOCK] = low

    @pl.when(step == 0)
    def _():
        out[...] = jnp.zeros_like(out)

    wide = 2 * BLOCK
    for n in range(masked.shape[2] // wide):
        lanes = slice(n * wide, (n + 1) * wide)
        dims = ((1,), (0,))
        product = dot(left[:, : 2 * depth], masked[0, :, lanes], dims, lax.Precision.DEFAULT)
        product += dot(left[:, 2 * depth :], masked[0, :depth, lanes], dims, lax.Precision.DEFAULT)
        out[2 * n] += product[:, :BLOCK]
        out[2 * n + 1] += product[:, BLOCK:]


def schur_product(masked, slack, pieces, scens, part, earlier, after):
    steps, depth, own_width = masked.shape
    depth //= 2
    width = pieces[0].shape[1]
    count = depth // BLOCK
    shape = (scens, len(pieces) * width, own_width // scens)
    whole = (scens, 2 * shape[1], shape[2])
    return pl.pallas_call(
        schur_kernel,
        grid=(steps,),
        in_specs=[
            pl.BlockSpec((1, 2 * depth, own_width), lambda t: (t, 0, 0)),
            pl.BlockSpec(slack.shape, lambda t: (0, 0)),
            ANY,
            ANY,
        ]
        + [pl.BlockSpec((count, width, BLOCK), lambda t: (t, 0, 0))] * len(pieces),
        out_specs=[pl.BlockSpec(shape, lambda t: (0, part, 0)), DONE_SPEC],
        out_shape=[jax.ShapeDtypeStruct(whole, F32), DONE],
        input_output_aliases={2: 0} if part else {},
        scratch_shapes=[pltpu.VMEM((shape[1], 3 * depth), BF16)],
        compiler_params=pltpu.CompilerParams(vmem_limit_bytes=LIMIT),
        cost_estimate=pl.CostEstimate(
            flops=6 * steps * depth * own_width * shape[1], bytes_accessed=20 << 20, transcendentals=0
        ),
        name="schur",
    )(masked, slack, earlier, after, *pieces)


def eliminate(w):
    for first in range(0, BLOCK, SLAB):
        height = BLOCK - first
        cols = [jnp.broadcast_to(w[first:, first + k : first + k + 1], (height, BLOCK)) for k in range(SLAB)]
        left, right = w[first : first + SLAB, :BLOCK], w[first : first + SLAB, BLOCK:]
        lower, upper = [], []
        for k in range(SLAB):
            scale = lax.rsqrt(cols[k][k : k + 1, :])
            square = scale * scale
            for m in range(k + 1, SLAB):
                cols[m] = cols[m] - cols[k] * (cols[k][m : m + 1, :] * square)
            low = cols[k] * scale
            u0 = left[k : k + 1, :] * scale
            u1 = right[k : k + 1, :] * scale
            if k + 1 < SLAB:
                left = left - low[:SLAB] * u0
                right = right - low[:SLAB] * u1
            w[first + k : first + k + 1, BLOCK:] = u1
            lower.append(low)
            upper.append((u0, u1))
        if height > SLAB:
            rest0, rest1 = w[first + SLAB :, :BLOCK], w[first + SLAB :, BLOCK:]
            for k in range(SLAB):
                rest0 = rest0 - lower[k][SLAB:] * upper[k][0]
                rest1 = rest1 - lower[k][SLAB:] * upper[k][1]
            w[first + SLAB :, :BLOCK] = rest0
            w[first + SLAB :, BLOCK:] = rest1


def row_of(order, core, k, width):
    place = core[0] if k % 2 == 0 else 1 - core[0]
    return pl.multiple_of((2 * order[k // 2] + place) * width, width)


def solve_kernel(core, order, mine, other, *refs):
    *pieces, _, fwd, sol, m, w, linv = refs
    size = fwd.shape[0]
    steps = size // BLOCK
    width = pieces[0].shape[1]
    for q in range(2):
        here = pl.ds(pl.multiple_of((q + 2 * core[0]) * BLOCK, BLOCK), BLOCK)
        m[:, here] = mine[q]
        here = pl.ds(pl.multiple_of((q + 2 * (1 - core[0])) * BLOCK, BLOCK), BLOCK)
        m[:, here] = other[q]
        for k, piece in enumerate(pieces):
            m[pl.ds(row_of(order, core, k, width), width), size + q * BLOCK : size + (q + 1) * BLOCK] = piece[q]
    shape = (BLOCK, BLOCK)
    eye = (lax.broadcasted_iota(jnp.int32, shape, 0) == lax.broadcasted_iota(jnp.int32, shape, 1)).astype(F32)

    def outer(step, carry):
        here = pl.ds(pl.multiple_of(step * BLOCK, BLOCK), BLOCK)
        w[:, :BLOCK] = m[here, here]
        w[:, BLOCK:] = eye
        eliminate(w)
        inverse = w[:, BLOCK:]
        linv[step] = inverse
        m[here, :] = dot_nn(inverse, m[here, :])

        def update(later, inner):
            there = pl.ds(pl.multiple_of(later * BLOCK, BLOCK), BLOCK)
            m[there, :] = m[there, :] - dot_tn(m[here, there], m[here, :])
            return inner

        lax.fori_loop(step + 1, steps, update, 0)
        return carry

    lax.fori_loop(0, steps, outer, 0)
    fwd[...] = m[:, size:]
    for step in reversed(range(steps)):
        rows = slice(step * BLOCK, (step + 1) * BLOCK)
        total = m[rows, size:]
        if step + 1 < steps:
            after = (step + 1) * BLOCK
            total = total - dot_nn(m[rows, after:size], sol[after:, :])
        sol[rows, :] = dot_tn(linv[step], total)


def finish_kernel(place, core, order, schur, sol, fwd, rhs, mine, slack, scen_rhs, reduced, directions, moved_sol):
    size = sol.shape[0]
    width = size // mine.shape[0]
    for k in range(mine.shape[0]):
        moved_sol[k * width : (k + 1) * width, :] = sol[pl.ds(row_of(order, core, k, width), width), :]
    solved = sol[...]
    total = schur[0]
    for k in range(1, schur.shape[0]):
        total = total + schur[k]
    result = rhs[...] - dot_tn(total, moved_sol[...])
    reduced[0] = result

    @pl.when(place[0] == 0)
    def _():
        reduced[0, :width] = fwd[pl.ds(pl.multiple_of(place[1] * width, width), width), :]

    for s in range(2):
        moved = dot_tn(mine[:, s].reshape(size, BLOCK), solved)
        divisor = jnp.broadcast_to(slack[s : s + 1, :], (BLOCK, BLOCK)).T
        for h in range(moved.shape[1] // BLOCK):
            lanes = slice(h * BLOCK, (h + 1) * BLOCK)
            directions[s, :, lanes] = (scen_rhs[s, :, lanes] - moved[:, lanes]) / divisor


def shape_of(value):
    return jax.ShapeDtypeStruct(value.shape, value.dtype)


def with_other_core(pieces):
    return [value for piece in pieces for value in (piece, lax.ppermute(piece, "core", SWAP))]


def per_device(border, pattern, slack, first_diag, rhs, scen_rhs):
    scen_index = lax.axis_index("scen")
    core_index = lax.axis_index("core")
    col_index = lax.axis_index(COL)
    cols = lax.axis_size(COL)
    scens = lax.axis_size("scen")
    chips = lax.axis_size(ALL_CHIPS)
    own, row_total, own_width = border.shape
    width = PW // cols
    nrhs = rhs.shape[1]
    blocks = row_total // BLOCK
    smem = pl.BlockSpec(memory_space=pltpu.SMEM)

    row_blocks, piece = pl.pallas_call(
        panel_kernel,
        grid=(own,),
        in_specs=[
            smem,
            pl.BlockSpec((1, row_total, BLOCK), lambda s: (s, 0, 0)),
            pl.BlockSpec((width, nrhs), lambda s: (0, 0)),
        ],
        out_specs=[
            pl.BlockSpec((blocks, 1, width, BLOCK), lambda s: (0, s, 0, 0)),
            pl.BlockSpec((own * blocks + 2, width, BLOCK), lambda s: (0, 0, 0)),
        ],
        out_shape=[
            jax.ShapeDtypeStruct((blocks, own, width, BLOCK), F32),
            jax.ShapeDtypeStruct((own * blocks + 2, width, BLOCK), F32),
        ],
        compiler_params=pltpu.CompilerParams(vmem_limit_bytes=LIMIT),
        name="panel",
    )(pattern, border, rhs)

    mine = lax.all_to_all(row_blocks, COL, 0, 0, tiled=True)
    along = lax.axis_size("x")
    up = [(a, (a + 1) % along) for a in range(along)]
    down = [(a, (a - 1) % along) for a in range(along)]
    below = lax.ppermute(piece, "x", up)
    above = lax.ppermute(piece, "x", down)
    beside = lax.ppermute(piece, "z", SWAP)
    masked, masked_done = mask_parts(pattern.reshape(own * blocks, -1), border, row_blocks)

    slack_mine = lax.dynamic_slice_in_dim(slack, col_index * BLOCK, BLOCK, 1)
    diag = jnp.where(scen_index == 0, first_diag[:width], 0.0)
    diag = lax.dynamic_update_slice_in_dim(jnp.zeros((PW,), F32), diag, col_index * width, 0).reshape(1, PW)
    core = core_index.reshape(1).astype(jnp.int32)
    half_shape = jax.ShapeDtypeStruct((2, PW, BLOCK), F32)
    kept, sent, below, above, beside = pl.pallas_call(
        pivot_kernel,
        in_specs=[smem, VMEM, VMEM, VMEM, ANY, ANY, ANY, ANY],
        out_specs=[VMEM, VMEM, ANY, ANY, ANY],
        out_shape=[half_shape, half_shape] + [shape_of(below)] * 3,
        input_output_aliases={5: 2, 6: 3, 7: 4},
        compiler_params=PARAMS,
        name="pivot",
    )(core, mine, slack_mine, diag, masked_done, below, above, beside)

    pair = kept + lax.ppermute(sent, "core", SWAP)
    pair = lax.all_to_all(pair.reshape(chips, 2 * PW // chips, BLOCK), ALL_CHIPS, 0, 0, tiled=True)
    middle = piece.shape[0] // 2
    far_up = lax.ppermute(below[:middle], "x", up)
    far_down = lax.ppermute(above[middle:], "x", down)
    below_beside = lax.ppermute(beside, "x", up)
    above_beside = lax.ppermute(beside, "x", down)
    slack_rows = slack.reshape(own * blocks, BLOCK)
    near_pieces = with_other_core([piece, below, above, beside])
    schur, near_done = schur_product(masked, slack_rows, near_pieces, scens, 0, masked_done, masked_done)

    share, far_up, far_down, below_beside, above_beside = pl.pallas_call(
        total_kernel,
        in_specs=[VMEM] + [ANY] * 5,
        out_specs=[VMEM] + [ANY] * 4,
        out_shape=[shape_of(v) for v in (pair, far_up, far_down, below_beside, above_beside)],
        input_output_aliases={2: 1, 3: 2, 4: 3, 5: 4},
        compiler_params=PARAMS,
        name="total",
    )(pair, near_done, far_up, far_down, below_beside, above_beside)
    half = lax.all_to_all(share, ALL_CHIPS, 0, 0, tiled=True).reshape(2, PW, BLOCK)
    other = lax.ppermute(half, "core", SWAP)
    opposite = jnp.concatenate([far_up, far_down])
    opposite_beside = lax.ppermute(opposite, "z", SWAP)
    opposite_beside = pl.pallas_call(
        follow_kernel,
        in_specs=[ANY, ANY],
        out_specs=ANY,
        out_shape=shape_of(opposite_beside),
        input_output_aliases={1: 0},
        compiler_params=PARAMS,
        name="follow",
    )(half, opposite_beside)
    far_pieces = with_other_core([below_beside, above_beside, opposite, opposite_beside])
    schur, far_done = schur_product(masked, slack_rows, far_pieces, scens, 1, schur, half)

    x, z = lax.axis_index("x"), lax.axis_index("z")
    steps = [(along - 1, z), (1, z), (along - 1, 1 - z), (1, 1 - z), (2, z), (2, 1 - z)]
    order = [x * 2 + z] + [lax.rem(x + step, along) * 2 + side for step, side in steps[:2]] + [x * 2 + 1 - z]
    order += [lax.rem(x + step, along) * 2 + side for step, side in steps[2:]]
    order = jnp.stack(order).astype(jnp.int32)
    pieces = near_pieces + far_pieces
    fwd, sol = pl.pallas_call(
        solve_kernel,
        grid=(1,),
        in_specs=[
            smem,
            smem,
            pl.BlockSpec((2, PW, BLOCK), lambda t: (0, 0, 0)),
            pl.BlockSpec((2, PW, BLOCK), lambda t: (0, 0, 0)),
        ]
        + [pl.BlockSpec((2, width, BLOCK), lambda t: (own * blocks // 2, 0, 0))] * len(pieces)
        + [ANY],
        out_specs=[pl.BlockSpec((PW, nrhs), lambda t: (0, 0))] * 2,
        out_shape=[jax.ShapeDtypeStruct((PW, nrhs), F32)] * 2,
        scratch_shapes=[
            pltpu.VMEM((PW, PW + nrhs), F32),
            pltpu.VMEM((BLOCK, 2 * BLOCK), F32),
            pltpu.VMEM((PW // BLOCK, BLOCK, BLOCK), F32),
        ],
        compiler_params=PARAMS,
        cost_estimate=pl.CostEstimate(flops=20 << 30, bytes_accessed=3 << 20, transcendentals=0),
        name="solve",
    )(core, order, half, other, *pieces, far_done)
    schur = lax.all_to_all(schur, "scen", 0, 0, tiled=True)

    place = jnp.stack([scen_index, col_index]).astype(jnp.int32)
    own_share = own_width // scens
    reduced, directions = pl.pallas_call(
        finish_kernel,
        grid_spec=pltpu.PrefetchScalarGridSpec(
            num_scalar_prefetch=3,
            grid=(1,),
            in_specs=[
                pl.BlockSpec(schur.shape, lambda t, *_: (0, 0, 0)),
                pl.BlockSpec((PW, nrhs), lambda t, *_: (0, 0)),
                pl.BlockSpec((PW, nrhs), lambda t, *_: (0, 0)),
                pl.BlockSpec((own_share, nrhs), lambda t, place, *_: (place[0], 0)),
                pl.BlockSpec((cols, own, width, BLOCK), lambda t, *_: (0, 0, 0, 0)),
                pl.BlockSpec((own, BLOCK), lambda t, *_: (0, 0)),
                pl.BlockSpec((own, BLOCK, nrhs), lambda t, *_: (0, 0, 0)),
            ],
            out_specs=[
                pl.BlockSpec((1, own_share, nrhs), lambda t, *_: (0, 0, 0)),
                pl.BlockSpec((own, BLOCK, nrhs), lambda t, *_: (0, 0, 0)),
            ],
            scratch_shapes=[pltpu.VMEM((PW, nrhs), F32)],
        ),
        out_shape=[
            jax.ShapeDtypeStruct((1, own_share, nrhs), F32),
            jax.ShapeDtypeStruct((own, BLOCK, nrhs), F32),
        ],
        compiler_params=PARAMS,
        name="finish",
    )(place, core, order, schur, sol, fwd, rhs, mine, slack_mine, scen_rhs)
    return reduced, directions


def solution(mesh):
    scens, cols = mesh.devices.shape
    parts = Mesh(mesh.devices.reshape(scens, cols // 4, 2, 2), ("scen", "x", "z", "core"))
    return jax.shard_map(
        per_device,
        mesh=parts,
        in_specs=(
            P("scen", None, COL),
            P("scen", None, COL),
            P("scen", None),
            P(COL),
            P(COL, None),
            P("scen", COL, None),
        ),
        out_specs=(P(COL, "scen", None), P("scen", COL, None)),
        check_vma=False,
    )
```

time: 157 us -> 169 us (1.076)
  Pallas kernels: 53.2 us -> 82.2 us
  starting transfers between devices: 20.1 us -> 49 us
  blocking collectives: 27.9 us -> 0 us
  between operations: 14.2 us -> 0.87 us
  waiting for transfers between devices: 30.2 us -> 17.6 us
  local copies, waits for them, and re-layouts: 8.69 us -> 13.9 us
  other arithmetic: 0.9 us -> 3.25 us
    all_to_all x1 -> x0, blocking collectives: 27.9 us -> none  [per_device(): lax.all_to_all(pair.reshape(chips, 2 * PW // chips, BLOCK), ALL_CHIPS, 0,...]
    pallas_call x3 -> x7, Pallas kernels: 47.9 us -> 74.6 us  [the longest x2 27 us: schur_product(): pl.pallas_call(schur_kernel, grid=(steps,), in_specs=[pl.BlockSpec((1, 2...]
    ppermute x2 -> x18, starting transfers between devices: 2.99 us -> 20.6 us  [the longest x8 7.39 us: with_other_core(): lax.ppermute(piece, 'core', SWAP)]
    all_to_all x1 -> x2, starting transfers between devices: 6.14 us -> 19.9 us  [the longest x1 10.5 us: per_device(): lax.all_to_all(pair.reshape(chips, 2 * PW // chips, BLOCK), ALL_CHIPS, 0,...]
    all_to_all x1, waiting for transfers between devices: 9.3 us -> 0.01 us  [per_device(): mine = lax.all_to_all(row_blocks, COL, 0, 0, tiled=True)]
    all_to_all x1 -> x2, waiting for transfers between devices: 16.3 us -> 7.5 us  [the longest x1 7.5 us: per_device(): lax.all_to_all(share, ALL_CHIPS, 0, 0, tiled=True).reshape(2, PW, BLOCK)]
    ppermute x2 -> x18, waiting for transfers between devices: 1.54 us -> 6.75 us  [the longest x1 5.62 us: per_device(): far_down = lax.ppermute(above[middle:], 'x', down)]
    all_to_all x1, starting transfers between devices: 7.2 us -> 4.87 us  [per_device(): mine = lax.all_to_all(row_blocks, COL, 0, 0, tiled=True)]
  transfers between devices with their start and end apart: 6 -> 22, of which waited for: 4 -> 5; matrix products, arithmetic and copies ran while one was open for 1% -> 4% of each run, Pallas kernels for 31% -> 44%
where the time goes in v2:
time: 169 us; the launch traced here: 167 us
  Pallas kernels  82.2 us (49%)
  starting transfers between devices  49 us (29%)
  waiting for transfers between devices  17.6 us (10%)
  local copies, waits for them, and re-layouts  13.9 us (8%)
  other arithmetic  3.25 us (2%)
    pallas_call x2, Pallas kernels, schur_product(): pl.pallas_call(schur_kernel, grid=(steps,), in_specs=[pl.BlockSpec((1, 2...  27 us
    pallas_call x1, Pallas kernels, per_device(): pl.pallas_call(solve_kernel, grid=(1,), in_specs=[smem, smem, pl.BlockSpe...  24.5 us
    pallas_call x1, Pallas kernels, mask_parts(): pl.pallas_call(mask_kernel, grid=(STEPS,), in_specs=[pl.BlockSpec(memory_...  15.3 us
    all_to_all x1, starting transfers between devices, per_device(): lax.all_to_all(pair.reshape(chips, 2 * PW // chips, BLOCK), ALL_CHIPS, 0,...  10.5 us
    all_to_all x1, starting transfers between devices, per_device(): lax.all_to_all(share, ALL_CHIPS, 0, 0, tiled=True).reshape(2, PW, BLOCK)  9.45 us
    unnamed x44, local copies, waits for them, and re-layouts  9.01 us
    all_to_all x1, waiting for transfers between devices, per_device(): lax.all_to_all(share, ALL_CHIPS, 0, 0, tiled=True).reshape(2, PW, BLOCK)  7.5 us
    ppermute x8, starting transfers between devices, with_other_core(): lax.ppermute(piece, 'core', SWAP)  7.39 us
  transfers between devices with their start and end apart: 22, of which 5 were waited for; matrix products, arithmetic and copies ran while one was open for 4% of the time, Pallas kernels for 44%

profile of v2, /device:TPU:1, one launch (start us, length us, event | category | flops | bytes accessed | tf_op | source)
XLA Modules:
  0.0 166.8 jit_solution(16251219556992906501)
XLA Ops:
  0.6 1.4 copy.17.pattern
  2.0 2.8 %panel.1 = (f32[16,2,32,128]{3,2,1,0:T(8,128)}, f32[34,32,128]{2,1,0:T(8,128)}) custom-call(s32[2,16,8]{2,1,0:T(8,128)} %copy.17.pattern, f32[2,2048,1024]{2,1,0:T(8,128)} %border.3, f32[1024,256]{1,0:T(8,128)} %rhs.3), custom_call_target="tpu_custom_call" | custom-call | tf_op jit(solution)/shard_map/panel/pallas_call | solution.py:313
  4.8 2.0 %collective-permute-start.1 = (f32[34,32,128]{2,1,0:T(8,128)}, f32[34,32,128]{2,1,0:T(8,128)S(1)}, u32[]{:S(2)}, u32[]{:S(2)}) collective-permute-start(f32[34,32,128]{2,1,0:T(8,128)} %get-tuple-element.25.refs_4_.refs_0_), channel_id=1, source_target_pairs={{0,4},{4,8},{8,12},{12,0},{1,5},{5,9},{9,13},{13,1},{2,6},{6,10},{... | collective-permute-start | bytes 1671176 | tf_op jit(solution)/shard_map/ppermute | solution.py:337
  8.2 1.8 %collective-permute-start.3 = (f32[34,32,128]{2,1,0:T(8,128)}, f32[34,32,128]{2,1,0:T(8,128)S(1)}, u32[]{:S(2)}, u32[]{:S(2)}) collective-permute-start(f32[34,32,128]{2,1,0:T(8,128)} %get-tuple-element.25.refs_4_.refs_0_), channel_id=1, source_target_pairs={{0,2},{2,0},{1,3},{3,1},{4,6},{6,4},{5,7},{7,5},{8,10},{10,8},{9,1... | collective-permute-start | bytes 1671176 | tf_op jit(solution)/shard_map/ppermute | solution.py:339
  10.0 4.9 %all-to-all-start = ((f32[16,2,32,128]{3,2,1,0:T(8,128)}), f32[16,2,32,128]{3,2,1,0:T(8,128)S(1)}, u32[]{:S(2)}, u32[]{:S(2)}) async-start(f32[16,2,32,128]{3,2,1,0:T(8,128)} %get-tuple-element.22._), calls=%async_computation | async-start | bytes 1048576 | tf_op jit(solution)/shard_map/all_to_all | solution.py:333
  15.1 15.3 %mask.1 = (bf16[8,1024,1024]{2,1,0:T(8,128)(2,1)}, f32[8,128]{1,0:T(8,128)}) custom-call(s32[32,8]{1,0:T(8,128)} %bitcast.20, f32[2,2048,1024]{2,1,0:T(8,128)} %border.3, f32[16,2,32,128]{3,2,1,0:T(8,128)} %get-tuple-element.22._), custom_call_target="tpu_custom_call" | custom-call | bytes 41943040 | tf_op jit(solution)/shard_map/mask/pallas_call | solution.py:112
  33.3 5.9 %pivot.1 = (f32[2,512,128]{2,1,0:T(8,128)}, f32[2,512,128]{2,1,0:T(8,128)}, f32[34,32,128]{2,1,0:T(8,128)}, f32[34,32,128]{2,1,0:T(8,128)}, f32[34,32,128]{2,1,0:T(8,128)}) custom-call(s32[1]{0:T(128)} %bitcast.2.core, f32[16,2,32,128]{3,2,1,0:T(8,128)} %copy-done.2, ...), custom_call_target="tpu_custom_call", output_to_operand_aliasing={{2}: (5, {}), {3}: (6, {}), {4}: (7, {})} | custom-call | tf_op jit(solution)/shard_map/pivot/pallas_call | solution.py:347
  43.4 1.4 collective-permute-start.10
  44.8 1.9 %add.66 = f32[2,512,128]{2,1,0:T(8,128)} add(f32[2,512,128]{2,1,0:T(8,128)} %get-tuple-element.30, f32[2,512,128]{2,1,0:T(8,128)S(1)} %collective-permute-done.7) | non-fusion elementwise | flops 131072 | bytes 1572864 | tf_op jit(solution)/shard_map/add | solution.py:357
  46.7 10.5 %all-to-all-start.1 = ((f32[64,16,128]{2,1,0:T(8,128)}), f32[64,16,128]{2,1,0:T(8,128)S(1)}, u32[]{:S(2)}, u32[]{:S(2)}) async-start(f32[64,16,128]{2,1,0:T(8,128)} %bitcast.13), calls=%async_computation.1 | async-start | bytes 1048576 | tf_op jit(solution)/shard_map/all_to_all | solution.py:358
  57.2 2.3 %collective-permute-start.11 = (f32[34,32,128]{2,1,0:T(8,128)S(1)}, f32[34,32,128]{2,1,0:T(8,128)S(1)}, u32[]{:S(2)}, u32[]{:S(2)}) collective-permute-start(f32[34,32,128]{2,1,0:T(8,128)S(1)} %copy-done.17), channel_id=1, source_target_pairs={{0,12},{4,0},{8,4},{12,8},{1,13},{5,1},{9,5},{13,9},{2,14},{6,2},{... | collective-permute-start | bytes 1671176 | tf_op jit(solution)/shard_map/ppermute | solution.py:363
  59.5 2.7 %collective-permute-start.9 = (f32[17,32,128]{2,1,0:T(8,128)S(1)}, f32[17,32,128]{2,1,0:T(8,128)S(1)}, u32[]{:S(2)}, u32[]{:S(2)}) collective-permute-start(f32[17,32,128]{2,1,0:T(8,128)S(1)} %slice.11), channel_id=1, source_target_pairs={{0,12},{4,0},{8,4},{12,8},{1,13},{5,1},{9,5},{13,9},{2,14},{6,2},{... | collective-permute-start | bytes 835592 | tf_op jit(solution)/shard_map/ppermute | solution.py:361
  62.2 13.5 %schur.2 = (f32[8,512,128]{2,1,0:T(8,128)}, f32[8,128]{1,0:T(8,128)}) custom-call(bf16[8,1024,1024]{2,1,0:T(8,128)(2,1)} %get-tuple-element.23.refs_0_, f32[32,128]{1,0:T(8,128)} %reshape.26.refs_1_, f32[8,128]{1,0:T(8,128)} %get-tuple-element.24.refs_0_.refs_2_.refs_3_, f32[8,128]{1,0:T(8,128)} %get-tuple-element.24.refs_0_.refs_2_.refs_3_, ...), custom_call_target="tpu_custom_call" | custom-call | flops 6442450944 | bytes 20971520 | tf_op jit(solution)/shard_map/schur/pallas_call | solution.py:169
  75.7 5.6 %collective-permute-done.9.refs_2_ = f32[17,32,128]{2,1,0:T(8,128)S(1)} collective-permute-done((f32[17,32,128]{2,1,0:T(8,128)S(1)}, f32[17,32,128]{2,1,0:T(8,128)S(1)}, u32[]{:S(2)}, u32[]{:S(2)}) %collective-permute-start.9) | collective-permute-done | bytes 278560 | tf_op jit(solution)/shard_map/ppermute | solution.py:361
  82.7 1.9 %total.1 = (f32[64,16,128]{2,1,0:T(8,128)}, f32[17,32,128]{2,1,0:T(8,128)}, f32[17,32,128]{2,1,0:T(8,128)}, f32[34,32,128]{2,1,0:T(8,128)}, f32[34,32,128]{2,1,0:T(8,128)}) custom-call(f32[64,16,128]{2,1,0:T(8,128)} %copy-done.8, f32[8,128]{1,0:T(8,128)} %get-tuple-element.32.refs_0_, ...), custom_call_target="tpu_custom_call", output_to_operand_aliasing={{1}: (2, {}), {2}: (3, {}), {3}: (4, {}), {4}: (5, {})} | custom-call | tf_op jit(solution)/shard_map/total/pallas_call | solution.py:368
  88.0 9.4 %all-to-all-start.2 = ((f32[64,16,128]{2,1,0:T(8,128)}), f32[64,16,128]{2,1,0:T(8,128)S(1)}, u32[]{:S(2)}, u32[]{:S(2)}) async-start(f32[64,16,128]{2,1,0:T(8,128)} %get-tuple-element.33), calls=%async_computation.2 | async-start | bytes 1048576 | tf_op jit(solution)/shard_map/all_to_all | solution.py:377
  97.4 2.5 %collective-permute-start.14 = (f32[34,32,128]{2,1,0:T(8,128)S(1)}, f32[34,32,128]{2,1,0:T(8,128)S(1)}, u32[]{:S(2)}, u32[]{:S(2)}) collective-permute-start(f32[34,32,128]{2,1,0:T(8,128)S(1)} %constant_dynamic-update-slice_fusion.refs_8_.refs_12_), channel_id=1, source_target_pairs={{0,1},{1,0},{2,3},{3,2},{4,5},{5,4},{6,7},{7,6},{8,9},{9,8},{10,11... | collective-permute-start | bytes 1671176 | tf_op jit(solution)/shard_map/ppermute | solution.py:297
  100.4 7.5 %all-to-all-done.2 = f32[64,16,128]{2,1,0:T(8,128)S(1)} async-done(((f32[64,16,128]{2,1,0:T(8,128)}), f32[64,16,128]{2,1,0:T(8,128)S(1)}, u32[]{:S(2)}, u32[]{:S(2)}) %all-to-all-start.2) | async-done | bytes 524320 | tf_op jit(solution)/shard_map/all_to_all | solution.py:377
  108.9 3.5 %collective-permute-start.16 = (f32[34,32,128]{2,1,0:T(8,128)}, f32[34,32,128]{2,1,0:T(8,128)S(1)}, u32[]{:S(2)}, u32[]{:S(2)}) collective-permute-start(f32[34,32,128]{2,1,0:T(8,128)} %follow.1.refs_10_.refs_14_), channel_id=1, source_target_pairs={{0,1},{1,0},{2,3},{3,2},{4,5},{5,4},{6,7},{7,6},{8,9},{9,8},{10,11... | collective-permute-start | bytes 1671176 | tf_op jit(solution)/shard_map/ppermute | solution.py:297
  115.0 13.5 %schur.3 = (f32[8,512,128]{2,1,0:T(8,128)}, f32[8,128]{1,0:T(8,128)}) custom-call(bf16[8,1024,1024]{2,1,0:T(8,128)(2,1)} %get-tuple-element.23.refs_0_, f32[32,128]{1,0:T(8,128)} %reshape.26.refs_1_, f32[8,512,128]{2,1,0:T(8,128)} %get-tuple-element.29.refs_2_, f32[2,512,128]{2,1,0:T(8,128)} %bitcast.18, ...), custom_call_target="tpu_custom_call", output_to_operand_aliasing={{0}: (2, {})} | custom-call | flops 6442450944 | bytes 20971520 | tf_op jit(solution)/shard_map/schur/pallas_call | solution.py:169
  128.5 3.6 %all-to-all-start.3 = ((f32[8,512,128]{2,1,0:T(8,128)}), f32[8,512,128]{2,1,0:T(8,128)S(1)}, u32[]{:S(2)}, u32[]{:S(2)}) async-start(f32[8,512,128]{2,1,0:T(8,128)} %get-tuple-element.38), calls=%async_computation.3 | async-start | bytes 4194304 | tf_op jit(solution)/shard_map/all_to_all | solution.py:421
  132.9 24.5 %solve.1 = (f32[512,256]{1,0:T(8,128)}, f32[512,256]{1,0:T(8,128)}) custom-call(s32[1]{0:T(128)} %bitcast.2.core, s32[8]{0:T(128)} %stack.47.order, f32[2,512,128]{2,1,0:T(8,128)} %bitcast.19, f32[2,512,128]{2,1,0:T(8,128)} %copy-done.20, f32[34,32,128]{2,1,0:T(8,128)} %get-tuple-element.25.refs_4_.refs_0_, ...), custom_call_target="tpu_custom_call" | custom-call | flops 21474836480 | bytes 3145728 | tf_op jit(solution)/shard_map/solve/pallas_call | solution.py:399
  157.4 3.3 %all-to-all-done.3.schur = f32[8,512,128]{2,1,0:T(8,128)S(1)} async-done(((f32[8,512,128]{2,1,0:T(8,128)}), f32[8,512,128]{2,1,0:T(8,128)S(1)}, u32[]{:S(2)}, u32[]{:S(2)}) %all-to-all-start.3) | async-done | bytes 2097184 | tf_op jit(solution)/shard_map/all_to_all | solution.py:421
  162.0 4.7 %finish.1 = (f32[1,128,256]{2,1,0:T(8,128)}, f32[2,128,256]{2,1,0:T(8,128)}) custom-call(s32[2]{0:T(128)} %pad_add_fusion.place, s32[1]{0:T(128)} %bitcast.2.core, s32[8]{0:T(128)} %stack.47.order, f32[8,512,128]{2,1,0:T(8,128)} %copy-done, f32[512,256]{1,0:T(8,128)} %get-tuple-element.40.sol, f32[512,256]{1,0:T(8,128)} %get-tuple-element.41.fwd, ...), custom_call_target="tpu_custom_call" | custom-call | tf_op jit(solution)/shard_map/finish/pallas_call | solution.py:425
  (84 shorter events, 19.5 us)
Async XLA Ops:
  4.8 27.1 %collective-permute-start.1 = (f32[34,32,128]{2,1,0:T(8,128)}, f32[34,32,128]{2,1,0:T(8,128)S(1)}, u32[]{:S(2)}, u32[]{:S(2)}) collective-permute-start(f32[34,32,128]{2,1,0:T(8,128)} %get-tuple-element.25.refs_4_.refs_0_), channel_id=1, source_target_pairs={{0,4},{4,8},{8,12},{12,0},{1,5},{5,9},{9,13},{13,1},{2,6},{6,10},{... | collective-permute-start | bytes 1671176 | tf_op jit(solution)/shard_map/ppermute | solution.py:337
  6.9 25.1 %collective-permute-start.2 = (f32[34,32,128]{2,1,0:T(8,128)}, f32[34,32,128]{2,1,0:T(8,128)S(1)}, u32[]{:S(2)}, u32[]{:S(2)}) collective-permute-start(f32[34,32,128]{2,1,0:T(8,128)} %get-tuple-element.25.refs_4_.refs_0_), channel_id=1, source_target_pairs={{0,12},{4,0},{8,4},{12,8},{1,13},{5,1},{9,5},{13,9},{2,14},{6,2},{... | collective-permute-start | bytes 1671176 | tf_op jit(solution)/shard_map/ppermute | solution.py:338
  8.2 23.8 %collective-permute-start.3 = (f32[34,32,128]{2,1,0:T(8,128)}, f32[34,32,128]{2,1,0:T(8,128)S(1)}, u32[]{:S(2)}, u32[]{:S(2)}) collective-permute-start(f32[34,32,128]{2,1,0:T(8,128)} %get-tuple-element.25.refs_4_.refs_0_), channel_id=1, source_target_pairs={{0,2},{2,0},{1,3},{3,1},{4,6},{6,4},{5,7},{7,5},{8,10},{10,8},{9,1... | collective-permute-start | bytes 1671176 | tf_op jit(solution)/shard_map/ppermute | solution.py:339
  10.0 22.0 %all-to-all-start = ((f32[16,2,32,128]{3,2,1,0:T(8,128)}), f32[16,2,32,128]{3,2,1,0:T(8,128)S(1)}, u32[]{:S(2)}, u32[]{:S(2)}) async-start(f32[16,2,32,128]{3,2,1,0:T(8,128)} %get-tuple-element.22._), calls=%async_computation | async-start | bytes 1048576 | tf_op jit(solution)/shard_map/all_to_all | solution.py:333
  14.8 42.4 %collective-permute-start = (f32[34,32,128]{2,1,0:T(8,128)}, f32[34,32,128]{2,1,0:T(8,128)}, u32[]{:S(2)}, u32[]{:S(2)}) collective-permute-start(f32[34,32,128]{2,1,0:T(8,128)} %get-tuple-element.25.refs_4_.refs_0_), channel_id=1, source_target_pairs={{0,1},{1,0},{2,3},{3,2},{4,5},{5,4},{6,7},{7,6},{8,9},{9,8},{10,11... | collective-permute-start | bytes 1671176 | tf_op jit(solution)/shard_map/ppermute | solution.py:297
  39.2 18.0 %copy-start.17 = (f32[34,32,128]{2,1,0:T(8,128)S(1)}, f32[34,32,128]{2,1,0:T(8,128)}, u32[]{:S(2)}) copy-start(f32[34,32,128]{2,1,0:T(8,128)} %get-tuple-element.28.refs_10_.refs_6_) | copy-start | bytes 1671172
  39.2 20.3 %collective-permute-start.4 = (f32[34,32,128]{2,1,0:T(8,128)}, f32[34,32,128]{2,1,0:T(8,128)}, u32[]{:S(2)}, u32[]{:S(2)}) collective-permute-start(f32[34,32,128]{2,1,0:T(8,128)} %get-tuple-element.26.refs_6_.refs_2_), channel_id=1, source_target_pairs={{0,1},{1,0},{2,3},{3,2},{4,5},{5,4},{6,7},{7,6},{8,9},{9,8},{10,11... | collective-permute-start | bytes 1671176 | tf_op jit(solution)/shard_map/ppermute | solution.py:297
  39.3 20.2 %collective-permute-start.5 = (f32[34,32,128]{2,1,0:T(8,128)}, f32[34,32,128]{2,1,0:T(8,128)}, u32[]{:S(2)}, u32[]{:S(2)}) collective-permute-start(f32[34,32,128]{2,1,0:T(8,128)} %get-tuple-element.27.refs_8_.refs_4_), channel_id=1, source_target_pairs={{0,1},{1,0},{2,3},{3,2},{4,5},{5,4},{6,7},{7,6},{8,9},{9,8},{10,11... | collective-permute-start | bytes 1671176 | tf_op jit(solution)/shard_map/ppermute | solution.py:297
  39.7 22.5 %collective-permute-start.6 = (f32[34,32,128]{2,1,0:T(8,128)}, f32[34,32,128]{2,1,0:T(8,128)}, u32[]{:S(2)}, u32[]{:S(2)}) collective-permute-start(f32[34,32,128]{2,1,0:T(8,128)} %get-tuple-element.28.refs_10_.refs_6_), channel_id=1, source_target_pairs={{0,1},{1,0},{2,3},{3,2},{4,5},{5,4},{6,7},{7,6},{8,9},{9,8},{10,11... | collective-permute-start | bytes 1671176 | tf_op jit(solution)/shard_map/ppermute | solution.py:297
  39.8 3.6 %collective-permute-start.7 = (f32[2,512,128]{2,1,0:T(8,128)}, f32[2,512,128]{2,1,0:T(8,128)S(1)}, u32[]{:S(2)}, u32[]{:S(2)}) collective-permute-start(f32[2,512,128]{2,1,0:T(8,128)} %get-tuple-element.31), channel_id=1, source_target_pairs={{0,1},{1,0},{2,3},{3,2},{4,5},{5,4},{6,7},{7,6},{8,9},{9,8},{10,11... | collective-permute-start | bytes 1572872 | tf_op jit(solution)/shard_map/ppermute | solution.py:357
  43.4 38.0 %collective-permute-start.10 = (f32[34,32,128]{2,1,0:T(8,128)}, f32[34,32,128]{2,1,0:T(8,128)S(1)}, u32[]{:S(2)}, u32[]{:S(2)}) collective-permute-start(f32[34,32,128]{2,1,0:T(8,128)} %get-tuple-element.28.refs_10_.refs_6_), channel_id=1, source_target_pairs={{0,4},{4,8},{8,12},{12,0},{1,5},{5,9},{9,13},{13,1},{2,6},{6,10},{... | collective-permute-start | bytes 1671176 | tf_op jit(solution)/shard_map/ppermute | solution.py:362
  46.7 34.7 %all-to-all-start.1 = ((f32[64,16,128]{2,1,0:T(8,128)}), f32[64,16,128]{2,1,0:T(8,128)S(1)}, u32[]{:S(2)}, u32[]{:S(2)}) async-start(f32[64,16,128]{2,1,0:T(8,128)} %bitcast.13), calls=%async_computation.1 | async-start | bytes 1048576 | tf_op jit(solution)/shard_map/all_to_all | solution.py:358
  57.2 24.2 %collective-permute-start.11 = (f32[34,32,128]{2,1,0:T(8,128)S(1)}, f32[34,32,128]{2,1,0:T(8,128)S(1)}, u32[]{:S(2)}, u32[]{:S(2)}) collective-permute-start(f32[34,32,128]{2,1,0:T(8,128)S(1)} %copy-done.17), channel_id=1, source_target_pairs={{0,12},{4,0},{8,4},{12,8},{1,13},{5,1},{9,5},{13,9},{2,14},{6,2},{... | collective-permute-start | bytes 1671176 | tf_op jit(solution)/shard_map/ppermute | solution.py:363
  59.5 16.2 %collective-permute-start.8 = (f32[17,32,128]{2,1,0:T(8,128)S(1)}, f32[17,32,128]{2,1,0:T(8,128)S(1)}, u32[]{:S(2)}, u32[]{:S(2)}) collective-permute-start(f32[17,32,128]{2,1,0:T(8,128)S(1)} %slice.10), channel_id=1, source_target_pairs={{0,4},{4,8},{8,12},{12,0},{1,5},{5,9},{9,13},{13,1},{2,6},{6,10},{... | collective-permute-start | bytes 835592 | tf_op jit(solution)/shard_map/ppermute | solution.py:360
  59.5 21.8 %collective-permute-start.9 = (f32[17,32,128]{2,1,0:T(8,128)S(1)}, f32[17,32,128]{2,1,0:T(8,128)S(1)}, u32[]{:S(2)}, u32[]{:S(2)}) collective-permute-start(f32[17,32,128]{2,1,0:T(8,128)S(1)} %slice.11), channel_id=1, source_target_pairs={{0,12},{4,0},{8,4},{12,8},{1,13},{5,1},{9,5},{13,9},{2,14},{6,2},{... | collective-permute-start | bytes 835592 | tf_op jit(solution)/shard_map/ppermute | solution.py:361
  86.7 27.5 %copy-start.9 = (f32[34,32,128]{2,1,0:T(8,128)}, f32[34,32,128]{2,1,0:T(8,128)S(1)}, u32[]{:S(2)}) copy-start(f32[34,32,128]{2,1,0:T(8,128)S(1)} %constant_dynamic-update-slice_fusion.refs_8_.refs_12_) | copy-start | bytes 1671172
  86.7 21.2 %collective-permute-start.15 = (f32[34,32,128]{2,1,0:T(8,128)S(1)}, f32[34,32,128]{2,1,0:T(8,128)S(1)}, u32[]{:S(2)}, u32[]{:S(2)}) collective-permute-start(f32[34,32,128]{2,1,0:T(8,128)S(1)} %constant_dynamic-update-slice_fusion.refs_8_.refs_12_), channel_id=1, source_target_pairs={{0,2},{2,0},{1,3},{3,1},{4,6},{6,4},{5,7},{7,5},{8,10},{10,8},{9,1... | collective-permute-start | bytes 1671176 | tf_op jit(solution)/shard_map/ppermute | solution.py:380
  88.0 20.0 %all-to-all-start.2 = ((f32[64,16,128]{2,1,0:T(8,128)}), f32[64,16,128]{2,1,0:T(8,128)S(1)}, u32[]{:S(2)}, u32[]{:S(2)}) async-start(f32[64,16,128]{2,1,0:T(8,128)} %get-tuple-element.33), calls=%async_computation.2 | async-start | bytes 1048576 | tf_op jit(solution)/shard_map/all_to_all | solution.py:377
  97.4 16.3 %collective-permute-start.14 = (f32[34,32,128]{2,1,0:T(8,128)S(1)}, f32[34,32,128]{2,1,0:T(8,128)S(1)}, u32[]{:S(2)}, u32[]{:S(2)}) collective-permute-start(f32[34,32,128]{2,1,0:T(8,128)S(1)} %constant_dynamic-update-slice_fusion.refs_8_.refs_12_), channel_id=1, source_target_pairs={{0,1},{1,0},{2,3},{3,2},{4,5},{5,4},{6,7},{7,6},{8,9},{9,8},{10,11... | collective-permute-start | bytes 1671176 | tf_op jit(solution)/shard_map/ppermute | solution.py:297
  99.9 13.8 %collective-permute-start.12 = (f32[34,32,128]{2,1,0:T(8,128)S(1)}, f32[34,32,128]{2,1,0:T(8,128)}, u32[]{:S(2)}, u32[]{:S(2)}) collective-permute-start(f32[34,32,128]{2,1,0:T(8,128)S(1)} %copy-done.4), channel_id=1, source_target_pairs={{0,1},{1,0},{2,3},{3,2},{4,5},{5,4},{6,7},{7,6},{8,9},{9,8},{10,11... | collective-permute-start | bytes 1671176 | tf_op jit(solution)/shard_map/ppermute | solution.py:297
  100.2 13.5 %collective-permute-start.13 = (f32[34,32,128]{2,1,0:T(8,128)S(1)}, f32[34,32,128]{2,1,0:T(8,128)}, u32[]{:S(2)}, u32[]{:S(2)}) collective-permute-start(f32[34,32,128]{2,1,0:T(8,128)S(1)} %copy-done.6), channel_id=1, source_target_pairs={{0,1},{1,0},{2,3},{3,2},{4,5},{5,4},{6,7},{7,6},{8,9},{9,8},{10,11... | collective-permute-start | bytes 1671176 | tf_op jit(solution)/shard_map/ppermute | solution.py:297
  108.9 5.3 %collective-permute-start.16 = (f32[34,32,128]{2,1,0:T(8,128)}, f32[34,32,128]{2,1,0:T(8,128)S(1)}, u32[]{:S(2)}, u32[]{:S(2)}) collective-permute-start(f32[34,32,128]{2,1,0:T(8,128)} %follow.1.refs_10_.refs_14_), channel_id=1, source_target_pairs={{0,1},{1,0},{2,3},{3,2},{4,5},{5,4},{6,7},{7,6},{8,9},{9,8},{10,11... | collective-permute-start | bytes 1671176 | tf_op jit(solution)/shard_map/ppermute | solution.py:297
  113.7 18.4 %collective-permute-start.17 = (f32[2,512,128]{2,1,0:T(8,128)}, f32[2,512,128]{2,1,0:T(8,128)S(1)}, u32[]{:S(2)}, u32[]{:S(2)}) collective-permute-start(f32[2,512,128]{2,1,0:T(8,128)} %bitcast.17), channel_id=1, source_target_pairs={{0,1},{1,0},{2,3},{3,2},{4,5},{5,4},{6,7},{7,6},{8,9},{9,8},{10,11... | collective-permute-start | bytes 1572872 | tf_op jit(solution)/shard_map/ppermute | solution.py:378
  128.5 32.2 %all-to-all-start.3 = ((f32[8,512,128]{2,1,0:T(8,128)}), f32[8,512,128]{2,1,0:T(8,128)S(1)}, u32[]{:S(2)}, u32[]{:S(2)}) async-start(f32[8,512,128]{2,1,0:T(8,128)} %get-tuple-element.38), calls=%async_computation.3 | async-start | bytes 4194304 | tf_op jit(solution)/shard_map/all_to_all | solution.py:421
  (19 other events, 67.3 us)

commit v3 on v2

v3 whole, which is shorter than its diff:
```python
import functools

import jax
import jax.numpy as jnp
from jax import lax
from jax.experimental import pallas as pl
from jax.experimental.pallas import tpu as pltpu
from jax.sharding import Mesh, PartitionSpec as P

PW = 512
BLOCK = 128
SLAB = 8
STEPS = 8
F32 = jnp.float32
BF16 = jnp.bfloat16
COL = ("x", "z", "core")
SWAP = [(0, 1), (1, 0)]
ALL_CHIPS = ("scen", "x", "z")
DONE = jax.ShapeDtypeStruct((8, 128), F32)
DONE_SPEC = pl.BlockSpec((8, 128), lambda t: (0, 0))
ANY = pl.BlockSpec(memory_space=pl.ANY)
VMEM = pl.BlockSpec(memory_space=pltpu.VMEM)
PARAMS = pltpu.CompilerParams(vmem_limit_bytes=20 << 20)
SHORT = pl.CostEstimate(flops=1 << 20, bytes_accessed=1 << 16, transcendentals=0)
WIDE_PARAMS = pltpu.CompilerParams(vmem_limit_bytes=56 << 20)


def dot(a, b, dims, precision=lax.Precision.HIGHEST):
    return lax.dot_general(a, b, (dims, ((), ())), precision=precision, preferred_element_type=F32)


def dot_nn(a, b):
    return dot(a, b, ((1,), (0,)))


def dot_tn(a, b):
    return dot(a, b, ((0,), (0,)))


def dot_nt(a, b):
    return dot(a, b, ((1,), (1,)))


def panel_kernel(pattern, border, rhs, row_out, all_out):
    scen = pl.program_id(0)
    width = rhs.shape[0]
    blocks = row_out.shape[0]
    for i in range(blocks):
        rows = border[0, i * BLOCK : (i + 1) * BLOCK, :].T[:width]
        rows = rows * pattern[scen, 0, i].astype(F32)
        row_out[i, 0] = rows
        all_out[scen * blocks + i] = rows

    @pl.when(scen == 0)
    def _():
        for h in range(2):
            all_out[2 * blocks + h] = rhs[:, h * BLOCK : (h + 1) * BLOCK]


def pivot_kernel(core, mine, slack, diag, *refs):
    kept, sent, right = refs[3], refs[4], refs[-1]
    size = diag.shape[1]
    for s in range(2):
        right[:, s * BLOCK : (s + 1) * BLOCK] = mine[:, s].reshape(size, BLOCK)
    left = jnp.concatenate([right[:, s * BLOCK : (s + 1) * BLOCK] / slack[s : s + 1, :] for s in range(2)], axis=1)
    rows = lax.broadcasted_iota(jnp.int32, (size, BLOCK), 0)
    cols = lax.broadcasted_iota(jnp.int32, (size, BLOCK), 1)
    for out, place in ((kept, core[0]), (sent, 1 - core[0])):
        for q in range(2):
            first = pl.multiple_of((q + 2 * place) * BLOCK, BLOCK)
            piece = dot_nt(left, right[pl.ds(first, BLOCK), :])
            out[q] = piece + jnp.where(rows == cols + first, diag[:, pl.ds(first, BLOCK)], 0.0)


def total_kernel(pair, *refs):
    shared = refs[4]
    total = pair[0]
    for k in range(1, pair.shape[0]):
        total = total + pair[k]
    for k in range(pair.shape[0]):
        shared[k] = total


def split(values):
    high = values.astype(BF16)
    return high, (values - high.astype(F32)).astype(BF16)


def mask_kernel(half, pattern, border, _, out, done):
    step = pl.program_id(0)
    done[...] = jnp.zeros_like(done)
    depth = border.shape[1]
    chunks, _, _, wide = out.shape
    per_scen = STEPS // pattern.shape[0]
    for e in range(depth // BLOCK):
        rows = slice(e * BLOCK, (e + 1) * BLOCK)
        block = lax.rem(step, per_scen) * (depth // BLOCK) + e
        for n in range(chunks):
            for c in range(wide // BLOCK):
                col = n * (wide // BLOCK) + c
                weight = pattern[lax.div(step, per_scen), half * chunks * (wide // BLOCK) + col, block].astype(F32)
                high, low = split(border[0, rows, col * BLOCK : (col + 1) * BLOCK] * weight)
                lanes = slice(c * BLOCK, (c + 1) * BLOCK)
                out[n, 0, rows, lanes] = high
                out[n, 1, rows, lanes] = low


def mask_parts(half, pattern, border, after):
    scenarios, row_total, own_width = border.shape
    rows = scenarios * row_total
    depth = rows // STEPS
    per_scen = row_total // depth
    wide = 2 * BLOCK
    chunks = own_width // 2 // wide
    return pl.pallas_call(
        functools.partial(mask_kernel, half),
        grid=(STEPS,),
        in_specs=[
            pl.BlockSpec(memory_space=pltpu.SMEM),
            pl.BlockSpec((1, depth, own_width // 2), lambda t: (t // per_scen, t % per_scen, half)),
            ANY,
        ],
        out_specs=[pl.BlockSpec((chunks, 2, depth, wide), lambda t: (0, 0, t, 0)), DONE_SPEC],
        out_shape=[jax.ShapeDtypeStruct((chunks, 2, rows, wide), BF16), DONE],
        compiler_params=WIDE_PARAMS,
        cost_estimate=SHORT,
        name="mask",
    )(pattern, border, after)


def follow_kernel(*refs):
    del refs


def follow(first, value):
    return pl.pallas_call(
        follow_kernel,
        in_specs=[ANY, ANY],
        out_specs=ANY,
        out_shape=shape_of(value),
        input_output_aliases={1: 0},
        compiler_params=PARAMS,
        cost_estimate=SHORT,
        name="follow",
    )(first, value)


def schur_kernel(part, masked_left, masked_right, slack, earlier, *refs):
    count = len(refs) - 10
    pieces, out, done = refs[:count], refs[count], refs[count + 1]
    high, low, held, right, result, sems, right_sems, out_sem = refs[count + 2 :]
    done[...] = jnp.zeros_like(done)
    blocks, width = held.shape[1:3]
    sources = [half.at[n] for half in (masked_left, masked_right) for n in range(half.shape[0])]
    loads = [
        pltpu.make_async_copy(source, right.at[n % 2], right_sems.at[n % 2]) for n, source in enumerate(sources)
    ]
    copies = [
        pltpu.make_async_copy(piece.at[pl.ds(0, blocks)], held.at[k], sems.at[k]) for k, piece in enumerate(pieces)
    ]
    for copy in copies:
        copy.start()
    loads[0].start()
    for k, copy in enumerate(copies):
        copy.wait()

        def prepare(e, carry):
            inverse = 1.0 / slack[pl.ds(e, 1), :]
            lanes = pl.ds(pl.multiple_of(e * BLOCK, BLOCK), BLOCK)
            rows = slice(k * width, (k + 1) * width)
            high[rows, lanes], low[rows, lanes] = split(held[k, e] * inverse)
            return carry

        lax.fori_loop(0, blocks, prepare, 0, unroll=4)
    dims = ((1,), (0,))
    for n, load in enumerate(loads):
        if n + 1 < len(loads):
            loads[n + 1].start()
        load.wait()
        product = dot(high[...], right[n % 2, 0], dims, lax.Precision.DEFAULT)
        product += dot(high[...], right[n % 2, 1], dims, lax.Precision.DEFAULT)
        product += dot(low[...], right[n % 2, 0], dims, lax.Precision.DEFAULT)
        result[2 * n] = product[:, :BLOCK]
        result[2 * n + 1] = product[:, BLOCK:]
    rows = result.shape[1]
    copy = pltpu.make_async_copy(result, out.at[:, pl.ds(part * rows, rows)], out_sem)
    copy.start()
    copy.wait()


def schur_product(masked, slack, pieces, scens, part, earlier):
    chunks, _, depth, wide = masked[0].shape
    own_width = 2 * chunks * wide
    width = pieces[0].shape[1]
    rows = len(pieces) * width
    whole = (scens, 2 * rows, own_width // scens)
    return pl.pallas_call(
        functools.partial(schur_kernel, part),
        in_specs=[ANY, ANY, VMEM, ANY] + [ANY] * len(pieces),
        out_specs=[ANY, VMEM],
        out_shape=[jax.ShapeDtypeStruct(whole, F32), DONE],
        input_output_aliases={3: 0} if part else {},
        scratch_shapes=[
            pltpu.VMEM((rows, depth), BF16),
            pltpu.VMEM((rows, depth), BF16),
            pltpu.VMEM((len(pieces), depth // BLOCK, width, BLOCK), F32),
            pltpu.VMEM((2, 2, depth, wide), BF16),
            pltpu.VMEM((scens, rows, own_width // scens), F32),
            pltpu.SemaphoreType.DMA((len(pieces),)),
            pltpu.SemaphoreType.DMA((2,)),
            pltpu.SemaphoreType.DMA,
        ],
        compiler_params=WIDE_PARAMS,
        cost_estimate=SHORT,
        name="schur",
    )(*masked, slack, earlier, *pieces)


def eliminate(w):
    for first in range(0, BLOCK, SLAB):
        height = BLOCK - first
        cols = [jnp.broadcast_to(w[first:, first + k : first + k + 1], (height, BLOCK)) for k in range(SLAB)]
        left, right = w[first : first + SLAB, :BLOCK], w[first : first + SLAB, BLOCK:]
        lower, upper = [], []
        for k in range(SLAB):
            scale = lax.rsqrt(cols[k][k : k + 1, :])
            square = scale * scale
            for m in range(k + 1, SLAB):
                cols[m] = cols[m] - cols[k] * (cols[k][m : m + 1, :] * square)
            low = cols[k] * scale
            u0 = left[k : k + 1, :] * scale
            u1 = right[k : k + 1, :] * scale
            if k + 1 < SLAB:
                left = left - low[:SLAB] * u0
                right = right - low[:SLAB] * u1
            w[first + k : first + k + 1, BLOCK:] = u1
            lower.append(low)
            upper.append((u0, u1))
        if height > SLAB:
            rest0, rest1 = w[first + SLAB :, :BLOCK], w[first + SLAB :, BLOCK:]
            for k in range(SLAB):
                rest0 = rest0 - lower[k][SLAB:] * upper[k][0]
                rest1 = rest1 - lower[k][SLAB:] * upper[k][1]
            w[first + SLAB :, :BLOCK] = rest0
            w[first + SLAB :, BLOCK:] = rest1


def rows_of(order, k, width):
    return pl.ds(pl.multiple_of(order[k] * width, width), width)


def solve_kernel(core, order, mine, other, *refs):
    *pieces, _, fwd, sol, m, w, linv = refs
    size = fwd.shape[0]
    steps = size // BLOCK
    width = pieces[0].shape[1]
    for q in range(2):
        here = pl.ds(pl.multiple_of((q + 2 * core[0]) * BLOCK, BLOCK), BLOCK)
        m[:, here] = mine[q]
        here = pl.ds(pl.multiple_of((q + 2 * (1 - core[0])) * BLOCK, BLOCK), BLOCK)
        m[:, here] = other[q]
        for k, piece in enumerate(pieces):
            m[rows_of(order, k, width), size + q * BLOCK : size + (q + 1) * BLOCK] = piece[q]
    shape = (BLOCK, BLOCK)
    eye = (lax.broadcasted_iota(jnp.int32, shape, 0) == lax.broadcasted_iota(jnp.int32, shape, 1)).astype(F32)

    def outer(step, carry):
        here = pl.ds(pl.multiple_of(step * BLOCK, BLOCK), BLOCK)
        w[:, :BLOCK] = m[here, here]
        w[:, BLOCK:] = eye
        eliminate(w)
        inverse = w[:, BLOCK:]
        linv[step] = inverse
        m[here, :] = dot_nn(inverse, m[here, :])

        def update(later, inner):
            there = pl.ds(pl.multiple_of(later * BLOCK, BLOCK), BLOCK)
            m[there, :] = m[there, :] - dot_tn(m[here, there], m[here, :])
            return inner

        lax.fori_loop(step + 1, steps, update, 0)
        return carry

    lax.fori_loop(0, steps, outer, 0)
    fwd[...] = m[:, size:]
    for step in reversed(range(steps)):
        rows = slice(step * BLOCK, (step + 1) * BLOCK)
        total = m[rows, size:]
        if step + 1 < steps:
            after = (step + 1) * BLOCK
            total = total - dot_nn(m[rows, after:size], sol[after:, :])
        sol[rows, :] = dot_tn(linv[step], total)


def directions_kernel(sol, mine, slack, scen_rhs, directions):
    size = sol.shape[0]
    solved = sol[...]
    for s in range(2):
        moved = dot_tn(mine[:, s].reshape(size, BLOCK), solved)
        divisor = jnp.broadcast_to(slack[s : s + 1, :], (BLOCK, BLOCK)).T
        for h in range(moved.shape[1] // BLOCK):
            lanes = slice(h * BLOCK, (h + 1) * BLOCK)
            directions[s, :, lanes] = (scen_rhs[s, :, lanes] - moved[:, lanes]) / divisor


def reduced_kernel(place, order, schur, sol, fwd, rhs, reduced, moved_sol):
    pieces = order.shape[0]
    width = sol.shape[0] // pieces
    for k in range(pieces):
        moved_sol[k * width : (k + 1) * width, :] = sol[rows_of(order, k, width), :]
    total = schur[0]
    for k in range(1, schur.shape[0]):
        total = total + schur[k]
    reduced[0] = rhs[...] - dot_tn(total, moved_sol[...])

    @pl.when(place[0] == 0)
    def _():
        reduced[0, :width] = fwd[rows_of(place, 1, width), :]


def shape_of(value):
    return jax.ShapeDtypeStruct(value.shape, value.dtype)


def with_other_core(pieces):
    return [value for piece in pieces for value in (piece, lax.ppermute(piece, "core", SWAP))]


def per_device(border, pattern, slack, first_diag, rhs, scen_rhs):
    scen_index = lax.axis_index("scen")
    core_index = lax.axis_index("core")
    pattern = jnp.transpose(pattern, (0, 2, 1))
    col_index = lax.axis_index(COL)
    cols = lax.axis_size(COL)
    scens = lax.axis_size("scen")
    chips = lax.axis_size(ALL_CHIPS)
    own, row_total, own_width = border.shape
    width = PW // cols
    nrhs = rhs.shape[1]
    blocks = row_total // BLOCK
    smem = pl.BlockSpec(memory_space=pltpu.SMEM)

    row_blocks, piece = pl.pallas_call(
        panel_kernel,
        grid=(own,),
        in_specs=[
            smem,
            pl.BlockSpec((1, row_total, BLOCK), lambda s: (s, 0, 0)),
            pl.BlockSpec((width, nrhs), lambda s: (0, 0)),
        ],
        out_specs=[
            pl.BlockSpec((blocks, 1, width, BLOCK), lambda s: (0, s, 0, 0)),
            pl.BlockSpec((own * blocks + 2, width, BLOCK), lambda s: (0, 0, 0)),
        ],
        out_shape=[
            jax.ShapeDtypeStruct((blocks, own, width, BLOCK), F32),
            jax.ShapeDtypeStruct((own * blocks + 2, width, BLOCK), F32),
        ],
        compiler_params=WIDE_PARAMS,
        name="panel",
    )(pattern, border, rhs)

    mine = lax.all_to_all(row_blocks, COL, 0, 0, tiled=True)
    along = lax.axis_size("x")
    first_way = [(2 * a + c, 2 * ((a + 1 - 2 * c) % along) + c) for a in range(along) for c in range(2)]
    second_way = [(target, source) for source, target in first_way]
    first = lax.ppermute(piece, ("x", "core"), first_way)
    second = lax.ppermute(piece, ("x", "core"), second_way)
    beside = lax.ppermute(piece, "z", SWAP)
    masked_left, masked_done = mask_parts(0, pattern, border, row_blocks)
    masked_right, masked_done = mask_parts(1, pattern, border, masked_done)
    masked = (masked_left, masked_right)
    first = follow(masked_done, first)
    opposite = lax.ppermute(first, ("x", "core"), first_way)

    slack_mine = lax.dynamic_slice_in_dim(slack, col_index * BLOCK, BLOCK, 1)
    diag = jnp.where(scen_index == 0, first_diag[:width], 0.0)
    diag = lax.dynamic_update_slice_in_dim(jnp.zeros((PW,), F32), diag, col_index * width, 0).reshape(1, PW)
    core = core_index.reshape(1).astype(jnp.int32)
    half_shape = jax.ShapeDtypeStruct((2, PW, BLOCK), F32)
    kept, sent, second, beside = pl.pallas_call(
        pivot_kernel,
        in_specs=[smem, VMEM, VMEM, VMEM, ANY, ANY, ANY],
        out_specs=[VMEM, VMEM, ANY, ANY],
        out_shape=[half_shape, half_shape] + [shape_of(first)] * 2,
        scratch_shapes=[pltpu.VMEM((PW, own * BLOCK), F32)],
        input_output_aliases={5: 2, 6: 3},
        compiler_params=PARAMS,
        cost_estimate=SHORT,
        name="pivot",
    )(core, mine, slack_mine, diag, masked_done, second, beside)

    pair = kept + lax.ppermute(sent, "core", SWAP)
    pair = lax.all_to_all(pair.reshape(chips, 2 * PW // chips, BLOCK), ALL_CHIPS, 0, 0, tiled=True)
    opposite_beside = lax.ppermute(opposite, "z", SWAP)
    first_beside = lax.ppermute(beside, ("x", "core"), first_way)
    second_beside = lax.ppermute(beside, ("x", "core"), second_way)
    slack_rows = slack.reshape(own * blocks, BLOCK)
    near_pieces = with_other_core([piece, first, second, beside])
    schur, near_done = schur_product(masked, slack_rows, near_pieces, scens, 0, masked_done)

    share, first_beside, second_beside, opposite_beside = pl.pallas_call(
        total_kernel,
        in_specs=[VMEM] + [ANY] * 4,
        out_specs=[VMEM] + [ANY] * 3,
        out_shape=[shape_of(v) for v in (pair, first_beside, second_beside, opposite_beside)],
        input_output_aliases={2: 1, 3: 2, 4: 3},
        compiler_params=PARAMS,
        cost_estimate=SHORT,
        name="total",
    )(pair, near_done, first_beside, second_beside, opposite_beside)
    half = lax.all_to_all(share, ALL_CHIPS, 0, 0, tiled=True).reshape(2, PW, BLOCK)
    far_pieces = with_other_core([first_beside, second_beside, opposite, opposite_beside])
    schur, far_done = schur_product(masked, slack_rows, far_pieces, scens, 1, schur)
    half = follow(far_done, half)
    other = lax.ppermute(half, "core", SWAP)

    x, z = lax.axis_index("x"), lax.axis_index("z")
    order = []
    for step, side in ((0, 0), (-1, 0), (1, 0), (0, 1), (-1, 1), (1, 1), (2, 0), (2, 1)):
        for other_core in range(2):
            c = core_index if other_core == 0 else 1 - core_index
            chip_x = lax.rem(x + along + step * (1 - 2 * c), along)
            order.append((chip_x * 2 + lax.rem(z + side, 2)) * 2 + c)
    order = jnp.stack(order).astype(jnp.int32)
    pieces = near_pieces + far_pieces
    fwd, sol = pl.pallas_call(
        solve_kernel,
        grid=(1,),
        in_specs=[
            smem,
            smem,
            pl.BlockSpec((2, PW, BLOCK), lambda t: (0, 0, 0)),
            pl.BlockSpec((2, PW, BLOCK), lambda t: (0, 0, 0)),
        ]
        + [pl.BlockSpec((2, width, BLOCK), lambda t: (own * blocks // 2, 0, 0))] * len(pieces)
        + [ANY],
        out_specs=[pl.BlockSpec((PW, nrhs), lambda t: (0, 0))] * 2,
        out_shape=[jax.ShapeDtypeStruct((PW, nrhs), F32)] * 2,
        scratch_shapes=[
            pltpu.VMEM((PW, PW + nrhs), F32),
            pltpu.VMEM((BLOCK, 2 * BLOCK), F32),
            pltpu.VMEM((PW // BLOCK, BLOCK, BLOCK), F32),
        ],
        compiler_params=WIDE_PARAMS,
        cost_estimate=SHORT,
        name="solve",
    )(core, order, half, other, *pieces, far_done)
    schur = lax.all_to_all(schur, "scen", 0, 0, tiled=True)

    directions = pl.pallas_call(
        directions_kernel,
        in_specs=[VMEM] * 4,
        out_specs=VMEM,
        out_shape=shape_of(scen_rhs),
        compiler_params=WIDE_PARAMS,
        cost_estimate=SHORT,
        name="directions",
    )(sol, mine, slack_mine, scen_rhs)

    place = jnp.stack([scen_index, col_index]).astype(jnp.int32)
    own_share = own_width // scens
    reduced = pl.pallas_call(
        reduced_kernel,
        grid_spec=pltpu.PrefetchScalarGridSpec(
            num_scalar_prefetch=2,
            grid=(1,),
            in_specs=[
                pl.BlockSpec(schur.shape, lambda t, *_: (0, 0, 0)),
                pl.BlockSpec((PW, nrhs), lambda t, *_: (0, 0)),
                pl.BlockSpec((PW, nrhs), lambda t, *_: (0, 0)),
                pl.BlockSpec((own_share, nrhs), lambda t, place, *_: (place[0], 0)),
            ],
            out_specs=pl.BlockSpec((1, own_share, nrhs), lambda t, *_: (0, 0, 0)),
            scratch_shapes=[pltpu.VMEM((PW, nrhs), F32)],
        ),
        out_shape=jax.ShapeDtypeStruct((1, own_share, nrhs), F32),
        compiler_params=WIDE_PARAMS,
        cost_estimate=SHORT,
        name="reduced",
    )(place, order, schur, sol, fwd, rhs)
    return reduced, directions


def solution(mesh):
    scens, cols = mesh.devices.shape
    parts = Mesh(mesh.devices.reshape(scens, cols // 4, 2, 2), ("scen", "x", "z", "core"))
    return jax.shard_map(
        per_device,
        mesh=parts,
        in_specs=(
            P("scen", None, COL),
            P("scen", None, COL),
            P("scen", None),
            P(COL),
            P(COL, None),
            P("scen", COL, None),
        ),
        out_specs=(P(COL, "scen", None), P("scen", COL, None)),
        check_vma=False,
    )
```

time: 169 us -> 158 us (0.935)
  waiting for transfers between devices: 17.6 us -> 2.57 us
  Pallas kernels: 82.2 us -> 95.4 us
  local copies, waits for them, and re-layouts: 13.9 us -> 7.42 us
    pallas_call x6 -> x9, Pallas kernels: 49 us -> 66.3 us  [the longest x2 38.8 us: schur_product(): pl.pallas_call(functools.partial(schur_kernel, part), in_specs=[ANY, ANY,...]
    all_to_all x1, waiting for transfers between devices: 7.5 us -> 0.01 us  [per_device(): lax.all_to_all(share, ALL_CHIPS, 0, 0, tiled=True).reshape(2, PW, BLOCK)]
    ppermute x6 -> x5, waiting for transfers between devices: 5.64 us -> 1.23 us  [the longest x1 1.22 us: per_device(): opposite = lax.ppermute(first, ('x', 'core'), first_way)]
    pallas_call x1, Pallas kernels: 5.89 us -> 1.82 us  [per_device(): pl.pallas_call(pivot_kernel, in_specs=[smem, VMEM, VMEM, VMEM, ANY, ANY,...]
    all_to_all x1, waiting for transfers between devices: 3.32 us -> 0.01 us  [per_device(): schur = lax.all_to_all(schur, 'scen', 0, 0, tiled=True)]
    ppermute x8, starting transfers between devices: 7.39 us -> 4.19 us  [with_other_core(): lax.ppermute(piece, 'core', SWAP)]
    unnamed x44 -> x38, local copies, waits for them, and re-layouts: 9.01 us -> 5.93 us
    all_to_all x1, starting transfers between devices: 3.6 us -> 6.2 us  [per_device(): schur = lax.all_to_all(schur, 'scen', 0, 0, tiled=True)]
  transfers between devices with their start and end apart: 22 -> 21, of which waited for: 5 -> 3; matrix products, arithmetic and copies ran while one was open for 4% -> 2% of each run, Pallas kernels for 44% -> 57%
where the time goes in v3:
time: 158 us; the launch traced here: 157 us
  Pallas kernels  95.4 us (60%)
  starting transfers between devices  48.4 us (31%)
  local copies, waits for them, and re-layouts  7.42 us (5%)
  waiting for transfers between devices  2.57 us (2%)
  other arithmetic  2.23 us (1%)
    pallas_call x2, Pallas kernels, schur_product(): pl.pallas_call(functools.partial(schur_kernel, part), in_specs=[ANY, ANY,...  38.8 us
    pallas_call x1, Pallas kernels, per_device(): pl.pallas_call(solve_kernel, grid=(1,), in_specs=[smem, smem, pl.BlockSpe...  24.5 us
    pallas_call x2, Pallas kernels, mask_parts(): pl.pallas_call(functools.partial(mask_kernel, half), grid=(STEPS,), in_sp...  19.2 us
    all_to_all x1, starting transfers between devices, per_device(): lax.all_to_all(share, ALL_CHIPS, 0, 0, tiled=True).reshape(2, PW, BLOCK)  10.3 us
    all_to_all x1, starting transfers between devices, per_device(): lax.all_to_all(pair.reshape(chips, 2 * PW // chips, BLOCK), ALL_CHIPS, 0,...  8.48 us
    all_to_all x1, starting transfers between devices, per_device(): schur = lax.all_to_all(schur, 'scen', 0, 0, tiled=True)  6.2 us
    unnamed x38, local copies, waits for them, and re-layouts  5.93 us
    all_to_all x1, starting transfers between devices, per_device(): mine = lax.all_to_all(row_blocks, COL, 0, 0, tiled=True)  5.07 us
  transfers between devices with their start and end apart: 21, of which 3 were waited for; matrix products, arithmetic and copies ran while one was open for 2% of the time, Pallas kernels for 57%

profile of v3, /device:TPU:1, one launch (start us, length us, event | category | flops | bytes accessed | tf_op | source)
XLA Modules:
  0.0 156.9 jit_solution(3968348885657308196)
XLA Ops:
  0.6 2.8 %panel.1 = (f32[16,2,32,128]{3,2,1,0:T(8,128)}, f32[34,32,128]{2,1,0:T(8,128)}) custom-call(s32[2,8,16]{2,1,0:T(8,128)} %bitcast.26, f32[2,2048,1024]{2,1,0:T(8,128)} %border.5, f32[1024,256]{1,0:T(8,128)} %rhs.3), custom_call_target="tpu_custom_call" | custom-call | tf_op jit(solution)/shard_map/panel/pallas_call | solution.py:343
  3.5 3.3 %collective-permute-start.1 = (f32[34,32,128]{2,1,0:T(8,128)}, f32[34,32,128]{2,1,0:T(8,128)S(1)}, u32[]{:S(2)}, u32[]{:S(2)}) collective-permute-start(f32[34,32,128]{2,1,0:T(8,128)} %get-tuple-element.27.refs_0_), channel_id=1, source_target_pairs={{0,4},{1,13},{4,8},{5,1},{8,12},{9,5},{12,0},{13,9},{2,6},{3,15},{... | collective-permute-start | bytes 1671176 | tf_op jit(solution)/shard_map/ppermute | solution.py:367
  6.8 1.6 %collective-permute-start.4 = (f32[34,32,128]{2,1,0:T(8,128)}, f32[34,32,128]{2,1,0:T(8,128)S(1)}, u32[]{:S(2)}, u32[]{:S(2)}) collective-permute-start(f32[34,32,128]{2,1,0:T(8,128)} %get-tuple-element.27.refs_0_), channel_id=1, source_target_pairs={{0,2},{2,0},{1,3},{3,1},{4,6},{6,4},{5,7},{7,5},{8,10},{10,8},{9,1... | collective-permute-start | bytes 1671176 | tf_op jit(solution)/shard_map/ppermute | solution.py:369
  8.4 5.1 %all-to-all-start = ((f32[16,2,32,128]{3,2,1,0:T(8,128)}), f32[16,2,32,128]{3,2,1,0:T(8,128)S(1)}, u32[]{:S(2)}, u32[]{:S(2)}) async-start(f32[16,2,32,128]{3,2,1,0:T(8,128)} %get-tuple-element.22._), calls=%async_computation | async-start | bytes 1048576 | tf_op jit(solution)/shard_map/all_to_all | solution.py:363
  13.8 9.6 %mask.2 = (bf16[2,2,4096,256]{3,2,1,0:T(8,128)(2,1)}, f32[8,128]{1,0:T(8,128)}) custom-call(s32[2,8,16]{2,1,0:T(8,128)} %bitcast.27, f32[2,2048,1024]{2,1,0:T(8,128)} %border.5, f32[16,2,32,128]{3,2,1,0:T(8,128)} %get-tuple-element.22._), custom_call_target="tpu_custom_call" | custom-call | flops 1048576 | bytes 65536 | tf_op jit(solution)/shard_map/mask/pallas_call | solution.py:115
  23.4 9.6 %mask.3 = (bf16[2,2,4096,256]{3,2,1,0:T(8,128)(2,1)}, f32[8,128]{1,0:T(8,128)}) custom-call(s32[2,8,16]{2,1,0:T(8,128)} %bitcast.28, f32[2,2048,1024]{2,1,0:T(8,128)} %border.5, f32[8,128]{1,0:T(8,128)} %get-tuple-element.24._), custom_call_target="tpu_custom_call" | custom-call | flops 1048576 | bytes 65536 | tf_op jit(solution)/shard_map/mask/pallas_call | solution.py:115
  34.3 2.7 %collective-permute-start.10 = (f32[34,32,128]{2,1,0:T(8,128)S(1)}, f32[34,32,128]{2,1,0:T(8,128)}, u32[]{:S(2)}, u32[]{:S(2)}) collective-permute-start(f32[34,32,128]{2,1,0:T(8,128)S(1)} %follow.2.refs_2_), channel_id=1, source_target_pairs={{0,4},{1,13},{4,8},{5,1},{8,12},{9,5},{12,0},{13,9},{2,6},{3,15},{... | collective-permute-start | bytes 1671176 | tf_op jit(solution)/shard_map/ppermute | solution.py:374
  38.1 1.8 %pivot.1 = (f32[2,512,128]{2,1,0:T(8,128)S(1)}, f32[2,512,128]{2,1,0:T(8,128)S(1)}, f32[34,32,128]{2,1,0:T(8,128)S(1)}, f32[34,32,128]{2,1,0:T(8,128)S(1)}) custom-call(s32[1]{0:T(128)} %bitcast.19.core, f32[16,2,32,128]{3,2,1,0:T(8,128)S(1)} %all-to-all-done.mine, ...), custom_call_target="tpu_custom_call", output_to_operand_aliasing={{2}: (5, {}), {3}: (6, {})} | custom-call | flops 1048576 | bytes 65536 | tf_op jit(solution)/shard_map/pivot/pallas_call | solution.py:381
  41.0 1.0 collective-permute-done.7
  42.3 1.2 collective-permute-done.10.refs_4_.refs_12_
  43.5 3.2 %collective-permute-start.8 = (f32[34,32,128]{2,1,0:T(8,128)S(1)}, f32[34,32,128]{2,1,0:T(8,128)S(1)}, u32[]{:S(2)}, u32[]{:S(2)}) collective-permute-start(f32[34,32,128]{2,1,0:T(8,128)S(1)} %get-tuple-element.29.refs_6_), channel_id=1, source_target_pairs={{0,4},{1,13},{4,8},{5,1},{8,12},{9,5},{12,0},{13,9},{2,6},{3,15},{... | collective-permute-start | bytes 1671176 | tf_op jit(solution)/shard_map/ppermute | solution.py:396
  46.8 1.2 collective-permute-start.11
  48.9 8.5 %all-to-all-start.1 = ((f32[64,16,128]{2,1,0:T(8,128)}), f32[64,16,128]{2,1,0:T(8,128)}, u32[]{:S(2)}, u32[]{:S(2)}) async-start(f32[64,16,128]{2,1,0:T(8,128)} %bitcast.25), calls=%async_computation.1 | async-start | bytes 1048576 | tf_op jit(solution)/shard_map/all_to_all | solution.py:394
  58.0 2.8 %collective-permute-start.14 = (f32[34,32,128]{2,1,0:T(8,128)}, f32[34,32,128]{2,1,0:T(8,128)}, u32[]{:S(2)}, u32[]{:S(2)}) collective-permute-start(f32[34,32,128]{2,1,0:T(8,128)} %collective-permute-done.10.refs_4_.refs_12_), channel_id=1, source_target_pairs={{0,1},{1,0},{2,3},{3,2},{4,5},{5,4},{6,7},{7,6},{8,9},{9,8},{10,11... | collective-permute-start | bytes 1671176 | tf_op jit(solution)/shard_map/ppermute | solution.py:326
  60.8 19.4 %schur.2 = (f32[8,512,128]{2,1,0:T(8,128)}, f32[8,128]{1,0:T(8,128)}) custom-call(bf16[2,2,4096,256]{3,2,1,0:T(8,128)(2,1)} %get-tuple-element.23.masked_left, bf16[2,2,4096,256]{3,2,1,0:T(8,128)(2,1)} %get-tuple-element.25.masked_right, f32[32,128]{1,0:T(8,128)} %reshape.21.slack, f32[8,128]{1,0:T(8,128)} %get-tuple-element.26.refs_0_.earlier, ...), custom_call_target="tpu_custom_call" | custom-call | flops 1048576 | bytes 65536 | tf_op jit(solution)/shard_map/schur/pallas_call | solution.py:197
  80.9 1.9 %total.1 = (f32[64,16,128]{2,1,0:T(8,128)}, f32[34,32,128]{2,1,0:T(8,128)S(1)}, f32[34,32,128]{2,1,0:T(8,128)S(1)}, f32[34,32,128]{2,1,0:T(8,128)S(1)}) custom-call(f32[64,16,128]{2,1,0:T(8,128)} %all-to-all-done.1.pair, f32[8,128]{1,0:T(8,128)S(1)} %copy-done.12, ...), custom_call_target="tpu_custom_call", output_to_operand_aliasing={{1}: (2, {}), {2}: (3, {}), {3}: (4, {})} | custom-call | flops 1048576 | bytes 65536 | tf_op jit(solution)/shard_map/total/pallas_call | solution.py:402
  83.5 10.3 %all-to-all-start.3 = ((f32[64,16,128]{2,1,0:T(8,128)}), f32[64,16,128]{2,1,0:T(8,128)S(1)}, u32[]{:S(2)}, u32[]{:S(2)}) async-start(f32[64,16,128]{2,1,0:T(8,128)} %get-tuple-element.39), calls=%async_computation.3 | async-start | bytes 1048576 | tf_op jit(solution)/shard_map/all_to_all | solution.py:412
  94.8 19.4 %schur.3 = (f32[8,512,128]{2,1,0:T(8,128)}, f32[8,128]{1,0:T(8,128)}) custom-call(bf16[2,2,4096,256]{3,2,1,0:T(8,128)(2,1)} %get-tuple-element.23.masked_left, bf16[2,2,4096,256]{3,2,1,0:T(8,128)(2,1)} %get-tuple-element.25.masked_right, f32[32,128]{1,0:T(8,128)} %reshape.21.slack, ...), custom_call_target="tpu_custom_call", output_to_operand_aliasing={{0}: (3, {})} | custom-call | flops 1048576 | bytes 65536 | tf_op jit(solution)/shard_map/schur/pallas_call | solution.py:197
  114.2 6.2 %all-to-all-start.2 = ((f32[8,512,128]{2,1,0:T(8,128)}), f32[8,512,128]{2,1,0:T(8,128)S(1)}, u32[]{:S(2)}, u32[]{:S(2)}) async-start(f32[8,512,128]{2,1,0:T(8,128)} %get-tuple-element.37), calls=%async_computation.2 | async-start | bytes 4194304 | tf_op jit(solution)/shard_map/all_to_all | solution.py:449
  121.1 1.3 collective-permute-start.16
  124.7 24.5 %solve.1 = (f32[512,256]{1,0:T(8,128)}, f32[512,256]{1,0:T(8,128)}) custom-call(s32[1]{0:T(128)} %bitcast.19.core, s32[16]{0:T(128)} %stack.79.order, f32[2,512,128]{2,1,0:T(8,128)} %copy-done.6, f32[2,512,128]{2,1,0:T(8,128)} %copy-done.17, f32[34,32,128]{2,1,0:T(8,128)} %get-tuple-element.27.refs_0_, f32[34,32,128]{2,1,0:T(8,128)} %copy-done.14, ...), custom_call_target="tpu_custom_call" | custom-call | flops 1048576 | bytes 65536 | tf_op jit(solution)/shard_map/solve/pallas_call | solution.py:427
  149.2 2.7 %directions.1 = f32[2,128,256]{2,1,0:T(8,128)} custom-call(f32[512,256]{1,0:T(8,128)} %get-tuple-element.40.sol, f32[16,2,32,128]{3,2,1,0:T(8,128)} %copy-done.7, f32[2,128]{1,0:T(2,128)} %copy-done.11, f32[2,128,256]{2,1,0:T(8,128)} %scen_rhs.1), custom_call_target="tpu_custom_call" | custom-call | flops 1048576 | bytes 65536 | tf_op jit(solution)/shard_map/directions/pallas_call | solution.py:451
  151.9 1.3 copy-done.13
  153.2 3.7 %reduced.1 = f32[1,128,256]{2,1,0:T(8,128)} custom-call(s32[2]{0:T(128)} %pad_add_fusion.place, s32[16]{0:T(128)} %stack.79.order, f32[8,512,128]{2,1,0:T(8,128)} %copy-done.13, f32[512,256]{1,0:T(8,128)} %get-tuple-element.40.sol, f32[512,256]{1,0:T(8,128)} %get-tuple-element.41.fwd, f32[1024,256]{1,0:T(8,128)} %rhs.3), custom_call_target="tpu_custom_call" | custom-call | flops 1048576 | bytes 65536 | tf_op jit(solution)/shard_map/reduced/pallas_call | solution.py:463
  (76 shorter events, 10.9 us)
Async XLA Ops:
  3.5 30.2 %collective-permute-start.1 = (f32[34,32,128]{2,1,0:T(8,128)}, f32[34,32,128]{2,1,0:T(8,128)S(1)}, u32[]{:S(2)}, u32[]{:S(2)}) collective-permute-start(f32[34,32,128]{2,1,0:T(8,128)} %get-tuple-element.27.refs_0_), channel_id=1, source_target_pairs={{0,4},{1,13},{4,8},{5,1},{8,12},{9,5},{12,0},{13,9},{2,6},{3,15},{... | collective-permute-start | bytes 1671176 | tf_op jit(solution)/shard_map/ppermute | solution.py:367
  6.8 30.6 %collective-permute-start.4 = (f32[34,32,128]{2,1,0:T(8,128)}, f32[34,32,128]{2,1,0:T(8,128)S(1)}, u32[]{:S(2)}, u32[]{:S(2)}) collective-permute-start(f32[34,32,128]{2,1,0:T(8,128)} %get-tuple-element.27.refs_0_), channel_id=1, source_target_pairs={{0,2},{2,0},{1,3},{3,1},{4,6},{6,4},{5,7},{7,5},{8,10},{10,8},{9,1... | collective-permute-start | bytes 1671176 | tf_op jit(solution)/shard_map/ppermute | solution.py:369
  8.4 29.0 %collective-permute-start.3 = (f32[34,32,128]{2,1,0:T(8,128)}, f32[34,32,128]{2,1,0:T(8,128)S(1)}, u32[]{:S(2)}, u32[]{:S(2)}) collective-permute-start(f32[34,32,128]{2,1,0:T(8,128)} %get-tuple-element.27.refs_0_), channel_id=1, source_target_pairs={{4,0},{13,1},{8,4},{1,5},{12,8},{5,9},{0,12},{9,13},{6,2},{15,3},{... | collective-permute-start | bytes 1671176 | tf_op jit(solution)/shard_map/ppermute | solution.py:368
  8.4 28.9 %all-to-all-start = ((f32[16,2,32,128]{3,2,1,0:T(8,128)}), f32[16,2,32,128]{3,2,1,0:T(8,128)S(1)}, u32[]{:S(2)}, u32[]{:S(2)}) async-start(f32[16,2,32,128]{3,2,1,0:T(8,128)} %get-tuple-element.22._), calls=%async_computation | async-start | bytes 1048576 | tf_op jit(solution)/shard_map/all_to_all | solution.py:363
  13.5 27.1 %collective-permute-start = (f32[34,32,128]{2,1,0:T(8,128)}, f32[34,32,128]{2,1,0:T(8,128)S(1)}, u32[]{:S(2)}, u32[]{:S(2)}) collective-permute-start(f32[34,32,128]{2,1,0:T(8,128)} %get-tuple-element.27.refs_0_), channel_id=1, source_target_pairs={{0,1},{1,0},{2,3},{3,2},{4,5},{5,4},{6,7},{7,6},{8,9},{9,8},{10,11... | collective-permute-start | bytes 1671176 | tf_op jit(solution)/shard_map/ppermute | solution.py:326
  34.3 26.4 %copy-start.2 = (f32[34,32,128]{2,1,0:T(8,128)}, f32[34,32,128]{2,1,0:T(8,128)S(1)}, u32[]{:S(2)}) copy-start(f32[34,32,128]{2,1,0:T(8,128)S(1)} %follow.2.refs_2_) | copy-start | bytes 1671172
  34.3 9.2 %collective-permute-start.10 = (f32[34,32,128]{2,1,0:T(8,128)S(1)}, f32[34,32,128]{2,1,0:T(8,128)}, u32[]{:S(2)}, u32[]{:S(2)}) collective-permute-start(f32[34,32,128]{2,1,0:T(8,128)S(1)} %follow.2.refs_2_), channel_id=1, source_target_pairs={{0,4},{1,13},{4,8},{5,1},{8,12},{9,5},{12,0},{13,9},{2,6},{3,15},{... | collective-permute-start | bytes 1671176 | tf_op jit(solution)/shard_map/ppermute | solution.py:374
  37.1 9.7 %collective-permute-start.2 = (f32[34,32,128]{2,1,0:T(8,128)S(1)}, f32[34,32,128]{2,1,0:T(8,128)}, u32[]{:S(2)}, u32[]{:S(2)}) collective-permute-start(f32[34,32,128]{2,1,0:T(8,128)S(1)} %follow.2.refs_2_), channel_id=1, source_target_pairs={{0,1},{1,0},{2,3},{3,2},{4,5},{5,4},{6,7},{7,6},{8,9},{9,8},{10,11... | collective-permute-start | bytes 1671176 | tf_op jit(solution)/shard_map/ppermute | solution.py:326
  37.1 43.1 %copy-start.11 = (f32[2,128]{1,0:T(2,128)}, f32[2,128]{1,0:T(2,128)S(1)}, u32[]{:S(2)}) copy-start(f32[2,128]{1,0:T(2,128)S(1)} %constant_dynamic-slice_fusion.slack) | copy-start | bytes 3076
  40.0 20.8 %copy-start = (f32[34,32,128]{2,1,0:T(8,128)}, f32[34,32,128]{2,1,0:T(8,128)S(1)}, u32[]{:S(2)}) copy-start(f32[34,32,128]{2,1,0:T(8,128)S(1)} %get-tuple-element.29.refs_6_) | copy-start | bytes 1671172
  40.0 2.0 %collective-permute-start.7 = (f32[2,512,128]{2,1,0:T(8,128)S(1)}, f32[2,512,128]{2,1,0:T(8,128)S(1)}, u32[]{:S(2)}, u32[]{:S(2)}) collective-permute-start(f32[2,512,128]{2,1,0:T(8,128)S(1)} %get-tuple-element.32), channel_id=1, source_target_pairs={{0,1},{1,0},{2,3},{3,2},{4,5},{5,4},{6,7},{7,6},{8,9},{9,8},{10,11... | collective-permute-start | bytes 1572872 | tf_op jit(solution)/shard_map/ppermute | solution.py:393
  40.5 17.5 %collective-permute-start.5 = (f32[34,32,128]{2,1,0:T(8,128)S(1)}, f32[34,32,128]{2,1,0:T(8,128)}, u32[]{:S(2)}, u32[]{:S(2)}) collective-permute-start(f32[34,32,128]{2,1,0:T(8,128)S(1)} %get-tuple-element.28.refs_4_), channel_id=1, source_target_pairs={{0,1},{1,0},{2,3},{3,2},{4,5},{5,4},{6,7},{7,6},{8,9},{9,8},{10,11... | collective-permute-start | bytes 1671176 | tf_op jit(solution)/shard_map/ppermute | solution.py:326
  40.6 20.2 %collective-permute-start.6 = (f32[34,32,128]{2,1,0:T(8,128)S(1)}, f32[34,32,128]{2,1,0:T(8,128)}, u32[]{:S(2)}, u32[]{:S(2)}) collective-permute-start(f32[34,32,128]{2,1,0:T(8,128)S(1)} %get-tuple-element.29.refs_6_), channel_id=1, source_target_pairs={{0,1},{1,0},{2,3},{3,2},{4,5},{5,4},{6,7},{7,6},{8,9},{9,8},{10,11... | collective-permute-start | bytes 1671176 | tf_op jit(solution)/shard_map/ppermute | solution.py:326
  42.0 38.2 %collective-permute-start.9 = (f32[34,32,128]{2,1,0:T(8,128)S(1)}, f32[34,32,128]{2,1,0:T(8,128)S(1)}, u32[]{:S(2)}, u32[]{:S(2)}) collective-permute-start(f32[34,32,128]{2,1,0:T(8,128)S(1)} %get-tuple-element.29.refs_6_), channel_id=1, source_target_pairs={{4,0},{13,1},{8,4},{1,5},{12,8},{5,9},{0,12},{9,13},{6,2},{15,3},{... | collective-permute-start | bytes 1671176 | tf_op jit(solution)/shard_map/ppermute | solution.py:397
  43.5 36.7 %collective-permute-start.8 = (f32[34,32,128]{2,1,0:T(8,128)S(1)}, f32[34,32,128]{2,1,0:T(8,128)S(1)}, u32[]{:S(2)}, u32[]{:S(2)}) collective-permute-start(f32[34,32,128]{2,1,0:T(8,128)S(1)} %get-tuple-element.29.refs_6_), channel_id=1, source_target_pairs={{0,4},{1,13},{4,8},{5,1},{8,12},{9,5},{12,0},{13,9},{2,6},{3,15},{... | collective-permute-start | bytes 1671176 | tf_op jit(solution)/shard_map/ppermute | solution.py:396
  46.8 33.5 %collective-permute-start.11 = (f32[34,32,128]{2,1,0:T(8,128)}, f32[34,32,128]{2,1,0:T(8,128)S(1)}, u32[]{:S(2)}, u32[]{:S(2)}) collective-permute-start(f32[34,32,128]{2,1,0:T(8,128)} %collective-permute-done.10.refs_4_.refs_12_), channel_id=1, source_target_pairs={{0,2},{2,0},{1,3},{3,1},{4,6},{6,4},{5,7},{7,5},{8,10},{10,8},{9,1... | collective-permute-start | bytes 1671176 | tf_op jit(solution)/shard_map/ppermute | solution.py:395
  48.9 31.4 %all-to-all-start.1 = ((f32[64,16,128]{2,1,0:T(8,128)}), f32[64,16,128]{2,1,0:T(8,128)}, u32[]{:S(2)}, u32[]{:S(2)}) async-start(f32[64,16,128]{2,1,0:T(8,128)} %bitcast.25), calls=%async_computation.1 | async-start | bytes 1048576 | tf_op jit(solution)/shard_map/all_to_all | solution.py:394
  58.0 35.8 %collective-permute-start.14 = (f32[34,32,128]{2,1,0:T(8,128)}, f32[34,32,128]{2,1,0:T(8,128)}, u32[]{:S(2)}, u32[]{:S(2)}) collective-permute-start(f32[34,32,128]{2,1,0:T(8,128)} %collective-permute-done.10.refs_4_.refs_12_), channel_id=1, source_target_pairs={{0,1},{1,0},{2,3},{3,2},{4,5},{5,4},{6,7},{7,6},{8,9},{9,8},{10,11... | collective-permute-start | bytes 1671176 | tf_op jit(solution)/shard_map/ppermute | solution.py:326
  82.9 10.9 %collective-permute-start.12 = (f32[34,32,128]{2,1,0:T(8,128)S(1)}, f32[34,32,128]{2,1,0:T(8,128)S(1)}, u32[]{:S(2)}, u32[]{:S(2)}) collective-permute-start(f32[34,32,128]{2,1,0:T(8,128)S(1)} %get-tuple-element.34.refs_0_.refs_8_), channel_id=1, source_target_pairs={{0,1},{1,0},{2,3},{3,2},{4,5},{5,4},{6,7},{7,6},{8,9},{9,8},{10,11... | collective-permute-start | bytes 1671176 | tf_op jit(solution)/shard_map/ppermute | solution.py:326
  82.9 10.9 %collective-permute-start.13 = (f32[34,32,128]{2,1,0:T(8,128)S(1)}, f32[34,32,128]{2,1,0:T(8,128)S(1)}, u32[]{:S(2)}, u32[]{:S(2)}) collective-permute-start(f32[34,32,128]{2,1,0:T(8,128)S(1)} %get-tuple-element.35.refs_2_.refs_10_), channel_id=1, source_target_pairs={{0,1},{1,0},{2,3},{3,2},{4,5},{5,4},{6,7},{7,6},{8,9},{9,8},{10,11... | collective-permute-start | bytes 1671176 | tf_op jit(solution)/shard_map/ppermute | solution.py:326
  83.4 10.4 %collective-permute-start.15 = (f32[34,32,128]{2,1,0:T(8,128)S(1)}, f32[34,32,128]{2,1,0:T(8,128)}, u32[]{:S(2)}, u32[]{:S(2)}) collective-permute-start(f32[34,32,128]{2,1,0:T(8,128)S(1)} %get-tuple-element.36.refs_6_.refs_14_), channel_id=1, source_target_pairs={{0,1},{1,0},{2,3},{3,2},{4,5},{5,4},{6,7},{7,6},{8,9},{9,8},{10,11... | collective-permute-start | bytes 1671176 | tf_op jit(solution)/shard_map/ppermute | solution.py:326
  83.5 30.7 %all-to-all-start.3 = ((f32[64,16,128]{2,1,0:T(8,128)}), f32[64,16,128]{2,1,0:T(8,128)S(1)}, u32[]{:S(2)}, u32[]{:S(2)}) async-start(f32[64,16,128]{2,1,0:T(8,128)} %get-tuple-element.39), calls=%async_computation.3 | async-start | bytes 1048576 | tf_op jit(solution)/shard_map/all_to_all | solution.py:412
  114.2 37.6 %all-to-all-start.2 = ((f32[8,512,128]{2,1,0:T(8,128)}), f32[8,512,128]{2,1,0:T(8,128)S(1)}, u32[]{:S(2)}, u32[]{:S(2)}) async-start(f32[8,512,128]{2,1,0:T(8,128)} %get-tuple-element.37), calls=%async_computation.2 | async-start | bytes 4194304 | tf_op jit(solution)/shard_map/all_to_all | solution.py:449
  121.1 2.8 %collective-permute-start.16 = (f32[2,512,128]{2,1,0:T(8,128)S(1)}, f32[2,512,128]{2,1,0:T(8,128)S(1)}, u32[]{:S(2)}, u32[]{:S(2)}) collective-permute-start(f32[2,512,128]{2,1,0:T(8,128)S(1)} %follow.3.mine), channel_id=1, source_target_pairs={{0,1},{1,0},{2,3},{3,2},{4,5},{5,4},{6,7},{7,6},{8,9},{9,8},{10,11... | collective-permute-start | bytes 1572872 | tf_op jit(solution)/shard_map/ppermute | solution.py:416
  (16 other events, 82.4 us)

commit v4 on v3

--- a/solution.py
+++ b/solution.py
@@ -1,5 +1,3 @@
-import functools
-
 import jax
 import jax.numpy as jnp
 from jax import lax
@@ -86,42 +84,36 @@
     return high, (values - high.astype(F32)).astype(BF16)
 
 
-def mask_kernel(half, pattern, border, _, out, done):
+def mask_kernel(pattern, border, _, out, done):
     step = pl.program_id(0)
     done[...] = jnp.zeros_like(done)
-    depth = border.shape[1]
-    chunks, _, _, wide = out.shape
+    depth, width = border.shape[1:]
     per_scen = STEPS // pattern.shape[0]
     for e in range(depth // BLOCK):
-        rows = slice(e * BLOCK, (e + 1) * BLOCK)
         block = lax.rem(step, per_scen) * (depth // BLOCK) + e
-        for n in range(chunks):
-            for c in range(wide // BLOCK):
-                col = n * (wide // BLOCK) + c
-                weight = pattern[lax.div(step, per_scen), half * chunks * (wide // BLOCK) + col, block].astype(F32)
-                high, low = split(border[0, rows, col * BLOCK : (col + 1) * BLOCK] * weight)
-                lanes = slice(c * BLOCK, (c + 1) * BLOCK)
-                out[n, 0, rows, lanes] = high
-                out[n, 1, rows, lanes] = low
-
-
-def mask_parts(half, pattern, border, after):
+        at = e * BLOCK
+        for c in range(width // BLOCK):
+            lanes = slice(c * BLOCK, (c + 1) * BLOCK)
+            weight = pattern[lax.div(step, per_scen), c, block].astype(F32)
+            high, low = split(border[0, at : at + BLOCK, lanes] * weight)
+            out[0, at : at + BLOCK, lanes] = high
+            out[0, depth + at : depth + at + BLOCK, lanes] = low
+
+
+def mask_parts(pattern, border, after):
     scenarios, row_total, own_width = border.shape
-    rows = scenarios * row_total
-    depth = rows // STEPS
+    depth = scenarios * row_total // STEPS
     per_scen = row_total // depth
-    wide = 2 * BLOCK
-    chunks = own_width // 2 // wide
     return pl.pallas_call(
-        functools.partial(mask_kernel, half),
+        mask_kernel,
         grid=(STEPS,),
         in_specs=[
             pl.BlockSpec(memory_space=pltpu.SMEM),
-            pl.BlockSpec((1, depth, own_width // 2), lambda t: (t // per_scen, t % per_scen, half)),
+            pl.BlockSpec((1, depth, own_width), lambda t: (t // per_scen, t % per_scen, 0)),
             ANY,
         ],
-        out_specs=[pl.BlockSpec((chunks, 2, depth, wide), lambda t: (0, 0, t, 0)), DONE_SPEC],
-        out_shape=[jax.ShapeDtypeStruct((chunks, 2, rows, wide), BF16), DONE],
+        out_specs=[pl.BlockSpec((1, 2 * depth, own_width), lambda t: (t, 0, 0)), DONE_SPEC],
+        out_shape=[jax.ShapeDtypeStruct((STEPS, 2 * depth, own_width), BF16), DONE],
         compiler_params=WIDE_PARAMS,
         cost_estimate=SHORT,
         name="mask",
@@ -145,75 +137,72 @@
     )(first, value)
 
 
-def schur_kernel(part, masked_left, masked_right, slack, earlier, *refs):
-    count = len(refs) - 10
-    pieces, out, done = refs[:count], refs[count], refs[count + 1]
-    high, low, held, right, result, sems, right_sems, out_sem = refs[count + 2 :]
-    done[...] = jnp.zeros_like(done)
+def schur_kernel(masked, slack, _, *refs):
+    *pieces, out, done, high, low, held, sems = refs
+    step = pl.program_id(0)
+    depth = masked.shape[1] // 2
     blocks, width = held.shape[1:3]
-    sources = [half.at[n] for half in (masked_left, masked_right) for n in range(half.shape[0])]
-    loads = [
-        pltpu.make_async_copy(source, right.at[n % 2], right_sems.at[n % 2]) for n, source in enumerate(sources)
-    ]
-    copies = [
-        pltpu.make_async_copy(piece.at[pl.ds(0, blocks)], held.at[k], sems.at[k]) for k, piece in enumerate(pieces)
-    ]
-    for copy in copies:
-        copy.start()
-    loads[0].start()
-    for k, copy in enumerate(copies):
-        copy.wait()
-
-        def prepare(e, carry):
-            inverse = 1.0 / slack[pl.ds(e, 1), :]
-            lanes = pl.ds(pl.multiple_of(e * BLOCK, BLOCK), BLOCK)
-            rows = slice(k * width, (k + 1) * width)
-            high[rows, lanes], low[rows, lanes] = split(held[k, e] * inverse)
-            return carry
-
-        lax.fori_loop(0, blocks, prepare, 0, unroll=4)
+
+    @pl.when(step == 0)
+    def _():
+        done[...] = jnp.zeros_like(done)
+        out[...] = jnp.zeros_like(out)
+        copies = [
+            pltpu.make_async_copy(piece.at[pl.ds(0, blocks)], held.at[k], sems.at[k]) for k, piece in enumerate(pieces)
+        ]
+        for copy in copies:
+            copy.start()
+        for k, copy in enumerate(copies):
+            copy.wait()
+
+            def prepare(e, carry):
+                inverse = 1.0 / slack[pl.ds(e, 1), :]
+                lanes = pl.ds(pl.multiple_of(e * BLOCK, BLOCK), BLOCK)
+                rows = slice(k * width, (k + 1) * width)
+                high[rows, lanes], low[rows, lanes] = split(held[k, e] * inverse)
+                return carry
+
+            lax.fori_loop(0, blocks, prepare, 0, unroll=4)
+
+    now = pl.ds(pl.multiple_of(step * depth, depth), depth)
     dims = ((1,), (0,))
-    for n, load in enumerate(loads):
-        if n + 1 < len(loads):
-            loads[n + 1].start()
-        load.wait()
-        product = dot(high[...], right[n % 2, 0], dims, lax.Precision.DEFAULT)
-        product += dot(high[...], right[n % 2, 1], dims, lax.Precision.DEFAULT)
-        product += dot(low[...], right[n % 2, 0], dims, lax.Precision.DEFAULT)
-        result[2 * n] = product[:, :BLOCK]
-        result[2 * n + 1] = product[:, BLOCK:]
-    rows = result.shape[1]
-    copy = pltpu.make_async_copy(result, out.at[:, pl.ds(part * rows, rows)], out_sem)
-    copy.start()
-    copy.wait()
+    wide = 2 * BLOCK
+    for n in range(masked.shape[2] // wide):
+        lanes = slice(n * wide, (n + 1) * wide)
+        product = dot(high[:, now], masked[0, :depth, lanes], dims, lax.Precision.DEFAULT)
+        product += dot(high[:, now], masked[0, depth:, lanes], dims, lax.Precision.DEFAULT)
+        product += dot(low[:, now], masked[0, :depth, lanes], dims, lax.Precision.DEFAULT)
+        out[2 * n] += product[:, :BLOCK]
+        out[2 * n + 1] += product[:, BLOCK:]
 
 
 def schur_product(masked, slack, pieces, scens, part, earlier):
-    chunks, _, depth, wide = masked[0].shape
-    own_width = 2 * chunks * wide
+    steps, depth, own_width = masked.shape
     width = pieces[0].shape[1]
     rows = len(pieces) * width
-    whole = (scens, 2 * rows, own_width // scens)
+    total = steps * depth // 2
+    shape = (scens, rows, own_width // scens)
     return pl.pallas_call(
-        functools.partial(schur_kernel, part),
-        in_specs=[ANY, ANY, VMEM, ANY] + [ANY] * len(pieces),
-        out_specs=[ANY, VMEM],
-        out_shape=[jax.ShapeDtypeStruct(whole, F32), DONE],
-        input_output_aliases={3: 0} if part else {},
+        schur_kernel,
+        grid=(steps,),
+        in_specs=[
+            pl.BlockSpec((1, depth, own_width), lambda t: (t, 0, 0)),
+            pl.BlockSpec(slack.shape, lambda t: (0, 0)),
+        ]
+        + [ANY] * (1 + len(pieces)),
+        out_specs=[pl.BlockSpec(shape, lambda t: (0, part, 0)), DONE_SPEC],
+        out_shape=[jax.ShapeDtypeStruct((scens, 2 * rows, own_width // scens), F32), DONE],
+        input_output_aliases={2: 0} if part else {},
         scratch_shapes=[
-            pltpu.VMEM((rows, depth), BF16),
-            pltpu.VMEM((rows, depth), BF16),
-            pltpu.VMEM((len(pieces), depth // BLOCK, width, BLOCK), F32),
-            pltpu.VMEM((2, 2, depth, wide), BF16),
-            pltpu.VMEM((scens, rows, own_width // scens), F32),
+            pltpu.VMEM((rows, total), BF16),
+            pltpu.VMEM((rows, total), BF16),
+            pltpu.VMEM((len(pieces), total // BLOCK, width, BLOCK), F32),
             pltpu.SemaphoreType.DMA((len(pieces),)),
-            pltpu.SemaphoreType.DMA((2,)),
-            pltpu.SemaphoreType.DMA,
         ],
         compiler_params=WIDE_PARAMS,
         cost_estimate=SHORT,
         name="schur",
-    )(*masked, slack, earlier, *pieces)
+    )(masked, slack, earlier, *pieces)
 
 
 def eliminate(w):
@@ -367,9 +356,7 @@
     first = lax.ppermute(piece, ("x", "core"), first_way)
     second = lax.ppermute(piece, ("x", "core"), second_way)
     beside = lax.ppermute(piece, "z", SWAP)
-    masked_left, masked_done = mask_parts(0, pattern, border, row_blocks)
-    masked_right, masked_done = mask_parts(1, pattern, border, masked_done)
-    masked = (masked_left, masked_right)
+    masked, masked_done = mask_parts(pattern, border, row_blocks)
     first = follow(masked_done, first)
     opposite = lax.ppermute(first, ("x", "core"), first_way)
 

time: 158 us -> 146 us (0.924)
  Pallas kernels: 95.4 us -> 84.1 us
    pallas_call x4 -> x3, Pallas kernels: 58 us -> 46.6 us  [the longest x2 31.2 us: schur_product(): pl.pallas_call(schur_kernel, grid=(steps,), in_specs=[pl.BlockSpec((1, de...]
  transfers between devices with their start and end apart: 21 -> 21, of which waited for: 3 -> 3; matrix products, arithmetic and copies ran while one was open for 2% -> 3% of each run, Pallas kernels for 57% -> 53%
where the time goes in v4:
time: 146 us; the launch traced here: 145 us
  Pallas kernels  84.1 us (58%)
  starting transfers between devices  48.5 us (33%)
  local copies, waits for them, and re-layouts  6.71 us (5%)
  waiting for transfers between devices  2.65 us (2%)
  other arithmetic  2.18 us (1%)
    pallas_call x2, Pallas kernels, schur_product(): pl.pallas_call(schur_kernel, grid=(steps,), in_specs=[pl.BlockSpec((1, de...  31.2 us
    pallas_call x1, Pallas kernels, per_device(): pl.pallas_call(solve_kernel, grid=(1,), in_specs=[smem, smem, pl.BlockSpe...  24.5 us
    pallas_call x1, Pallas kernels, mask_parts(): pl.pallas_call(mask_kernel, grid=(STEPS,), in_specs=[pl.BlockSpec(memory_...  15.4 us
    all_to_all x1, starting transfers between devices, per_device(): lax.all_to_all(share, ALL_CHIPS, 0, 0, tiled=True).reshape(2, PW, BLOCK)  10.2 us
    all_to_all x1, starting transfers between devices, per_device(): lax.all_to_all(pair.reshape(chips, 2 * PW // chips, BLOCK), ALL_CHIPS, 0,...  8.48 us
    all_to_all x1, starting transfers between devices, per_device(): schur = lax.all_to_all(schur, 'scen', 0, 0, tiled=True)  6.24 us
    unnamed x38, local copies, waits for them, and re-layouts  5.24 us
    all_to_all x1, starting transfers between devices, per_device(): mine = lax.all_to_all(row_blocks, COL, 0, 0, tiled=True)  5.07 us
  transfers between devices with their start and end apart: 21, of which 3 were waited for; matrix products, arithmetic and copies ran while one was open for 3% of the time, Pallas kernels for 53%

profile of v4, /device:TPU:1, one launch (start us, length us, event | category | flops | bytes accessed | tf_op | source)
XLA Modules:
  0.0 145.0 jit_solution(1555133592151749906)
XLA Ops:
  0.6 2.9 %panel.1 = (f32[16,2,32,128]{3,2,1,0:T(8,128)}, f32[34,32,128]{2,1,0:T(8,128)}) custom-call(s32[2,8,16]{2,1,0:T(8,128)} %bitcast.26, f32[2,2048,1024]{2,1,0:T(8,128)} %border.3, f32[1024,256]{1,0:T(8,128)} %rhs.3), custom_call_target="tpu_custom_call" | custom-call | tf_op jit(solution)/shard_map/panel/pallas_call | solution.py:332
  3.5 3.3 %collective-permute-start.1 = (f32[34,32,128]{2,1,0:T(8,128)}, f32[34,32,128]{2,1,0:T(8,128)S(1)}, u32[]{:S(2)}, u32[]{:S(2)}) collective-permute-start(f32[34,32,128]{2,1,0:T(8,128)} %get-tuple-element.23.refs_0_), channel_id=1, source_target_pairs={{0,4},{1,13},{4,8},{5,1},{8,12},{9,5},{12,0},{13,9},{2,6},{3,15},{... | collective-permute-start | bytes 1671176 | tf_op jit(solution)/shard_map/ppermute | solution.py:356
  6.8 1.6 %collective-permute-start.4 = (f32[34,32,128]{2,1,0:T(8,128)}, f32[34,32,128]{2,1,0:T(8,128)S(1)}, u32[]{:S(2)}, u32[]{:S(2)}) collective-permute-start(f32[34,32,128]{2,1,0:T(8,128)} %get-tuple-element.23.refs_0_), channel_id=1, source_target_pairs={{0,2},{2,0},{1,3},{3,1},{4,6},{6,4},{5,7},{7,5},{8,10},{10,8},{9,1... | collective-permute-start | bytes 1671176 | tf_op jit(solution)/shard_map/ppermute | solution.py:358
  8.4 5.1 %all-to-all-start = ((f32[16,2,32,128]{3,2,1,0:T(8,128)}), f32[16,2,32,128]{3,2,1,0:T(8,128)S(1)}, u32[]{:S(2)}, u32[]{:S(2)}) async-start(f32[16,2,32,128]{3,2,1,0:T(8,128)} %get-tuple-element.20._), calls=%async_computation | async-start | bytes 1048576 | tf_op jit(solution)/shard_map/all_to_all | solution.py:352
  13.8 15.4 %mask.1 = (bf16[8,1024,1024]{2,1,0:T(8,128)(2,1)}, f32[8,128]{1,0:T(8,128)}) custom-call(s32[2,8,16]{2,1,0:T(8,128)} %bitcast.27, f32[2,2048,1024]{2,1,0:T(8,128)} %border.3, f32[16,2,32,128]{3,2,1,0:T(8,128)} %get-tuple-element.20._), custom_call_target="tpu_custom_call" | custom-call | flops 1048576 | bytes 65536 | tf_op jit(solution)/shard_map/mask/pallas_call | solution.py:107
  30.5 2.7 %collective-permute-start.10 = (f32[34,32,128]{2,1,0:T(8,128)S(1)}, f32[34,32,128]{2,1,0:T(8,128)}, u32[]{:S(2)}, u32[]{:S(2)}) collective-permute-start(f32[34,32,128]{2,1,0:T(8,128)S(1)} %follow.2.refs_2_), channel_id=1, source_target_pairs={{0,4},{1,13},{4,8},{5,1},{8,12},{9,5},{12,0},{13,9},{2,6},{3,15},{... | collective-permute-start | bytes 1671176 | tf_op jit(solution)/shard_map/ppermute | solution.py:361
  34.3 1.8 %pivot.1 = (f32[2,512,128]{2,1,0:T(8,128)S(1)}, f32[2,512,128]{2,1,0:T(8,128)S(1)}, f32[34,32,128]{2,1,0:T(8,128)S(1)}, f32[34,32,128]{2,1,0:T(8,128)S(1)}) custom-call(s32[1]{0:T(128)} %bitcast.19.core, f32[16,2,32,128]{3,2,1,0:T(8,128)S(1)} %all-to-all-done.mine, ...), custom_call_target="tpu_custom_call", output_to_operand_aliasing={{2}: (5, {}), {3}: (6, {})} | custom-call | flops 1048576 | bytes 65536 | tf_op jit(solution)/shard_map/pivot/pallas_call | solution.py:368
  37.2 1.0 collective-permute-done.7
  38.5 1.2 collective-permute-done.10.refs_4_.refs_12_
  39.8 3.2 %collective-permute-start.8 = (f32[34,32,128]{2,1,0:T(8,128)S(1)}, f32[34,32,128]{2,1,0:T(8,128)S(1)}, u32[]{:S(2)}, u32[]{:S(2)}) collective-permute-start(f32[34,32,128]{2,1,0:T(8,128)S(1)} %get-tuple-element.25.refs_6_), channel_id=1, source_target_pairs={{0,4},{1,13},{4,8},{5,1},{8,12},{9,5},{12,0},{13,9},{2,6},{3,15},{... | collective-permute-start | bytes 1671176 | tf_op jit(solution)/shard_map/ppermute | solution.py:383
  43.0 1.2 collective-permute-start.11
  44.2 0.9 add.201
  45.1 8.5 %all-to-all-start.1 = ((f32[64,16,128]{2,1,0:T(8,128)}), f32[64,16,128]{2,1,0:T(8,128)}, u32[]{:S(2)}, u32[]{:S(2)}) async-start(f32[64,16,128]{2,1,0:T(8,128)} %bitcast.25), calls=%async_computation.1 | async-start | bytes 1048576 | tf_op jit(solution)/shard_map/all_to_all | solution.py:381
  54.2 2.8 %collective-permute-start.14 = (f32[34,32,128]{2,1,0:T(8,128)}, f32[34,32,128]{2,1,0:T(8,128)S(1)}, u32[]{:S(2)}, u32[]{:S(2)}) collective-permute-start(f32[34,32,128]{2,1,0:T(8,128)} %collective-permute-done.10.refs_4_.refs_12_), channel_id=1, source_target_pairs={{0,1},{1,0},{2,3},{3,2},{4,5},{5,4},{6,7},{7,6},{8,9},{9,8},{10,11... | collective-permute-start | bytes 1671176 | tf_op jit(solution)/shard_map/ppermute | solution.py:315
  57.0 15.6 %schur.2 = (f32[8,512,128]{2,1,0:T(8,128)}, f32[8,128]{1,0:T(8,128)}) custom-call(bf16[8,1024,1024]{2,1,0:T(8,128)(2,1)} %get-tuple-element.21.masked, f32[32,128]{1,0:T(8,128)} %reshape.21.slack, f32[8,128]{1,0:T(8,128)} %get-tuple-element.22.refs_0_._, f32[34,32,128]{2,1,0:T(8,128)} %get-tuple-element.23.refs_0_, f32[34,32,128]{2,1,0:T(8,128)} %copy-done.14, ...), custom_call_target="tpu_custom_call" | custom-call | flops 1048576 | bytes 65536 | tf_op jit(solution)/shard_map/schur/pallas_call | solution.py:185
  73.4 1.9 %total.1 = (f32[64,16,128]{2,1,0:T(8,128)}, f32[34,32,128]{2,1,0:T(8,128)S(1)}, f32[34,32,128]{2,1,0:T(8,128)S(1)}, f32[34,32,128]{2,1,0:T(8,128)S(1)}) custom-call(f32[64,16,128]{2,1,0:T(8,128)} %all-to-all-done.1.pair, f32[8,128]{1,0:T(8,128)S(1)} %copy-done.12, ...), custom_call_target="tpu_custom_call", output_to_operand_aliasing={{1}: (2, {}), {2}: (3, {}), {3}: (4, {})} | custom-call | flops 1048576 | bytes 65536 | tf_op jit(solution)/shard_map/total/pallas_call | solution.py:389
  75.9 10.2 %all-to-all-start.3 = ((f32[64,16,128]{2,1,0:T(8,128)}), f32[64,16,128]{2,1,0:T(8,128)S(1)}, u32[]{:S(2)}, u32[]{:S(2)}) async-start(f32[64,16,128]{2,1,0:T(8,128)} %get-tuple-element.35), calls=%async_computation.3 | async-start | bytes 1048576 | tf_op jit(solution)/shard_map/all_to_all | solution.py:399
  87.2 15.6 %schur.3 = (f32[8,512,128]{2,1,0:T(8,128)}, f32[8,128]{1,0:T(8,128)}) custom-call(bf16[8,1024,1024]{2,1,0:T(8,128)(2,1)} %get-tuple-element.21.masked, f32[32,128]{1,0:T(8,128)} %reshape.21.slack, f32[8,512,128]{2,1,0:T(8,128)} %get-tuple-element.26._, f32[34,32,128]{2,1,0:T(8,128)} %copy-done.4, ...), custom_call_target="tpu_custom_call", output_to_operand_aliasing={{0}: (2, {})} | custom-call | flops 1048576 | bytes 65536 | tf_op jit(solution)/shard_map/schur/pallas_call | solution.py:185
  102.8 6.2 %all-to-all-start.2 = ((f32[8,512,128]{2,1,0:T(8,128)}), f32[8,512,128]{2,1,0:T(8,128)S(1)}, u32[]{:S(2)}, u32[]{:S(2)}) async-start(f32[8,512,128]{2,1,0:T(8,128)} %get-tuple-element.33), calls=%async_computation.2 | async-start | bytes 4194304 | tf_op jit(solution)/shard_map/all_to_all | solution.py:436
  109.1 1.3 collective-permute-start.16
  112.8 24.5 %solve.1 = (f32[512,256]{1,0:T(8,128)}, f32[512,256]{1,0:T(8,128)}) custom-call(s32[1]{0:T(128)} %bitcast.19.core, s32[16]{0:T(128)} %stack.79.order, f32[2,512,128]{2,1,0:T(8,128)} %copy-done.6, f32[2,512,128]{2,1,0:T(8,128)} %copy-done.17, f32[34,32,128]{2,1,0:T(8,128)} %get-tuple-element.23.refs_0_, f32[34,32,128]{2,1,0:T(8,128)} %copy-done.14, ...), custom_call_target="tpu_custom_call" | custom-call | flops 1048576 | bytes 65536 | tf_op jit(solution)/shard_map/solve/pallas_call | solution.py:414
  137.3 2.7 %directions.1 = f32[2,128,256]{2,1,0:T(8,128)} custom-call(f32[512,256]{1,0:T(8,128)} %get-tuple-element.36.sol, f32[16,2,32,128]{3,2,1,0:T(8,128)} %copy-done.7, f32[2,128]{1,0:T(2,128)} %copy-done.11, f32[2,128,256]{2,1,0:T(8,128)} %scen_rhs.1), custom_call_target="tpu_custom_call" | custom-call | flops 1048576 | bytes 65536 | tf_op jit(solution)/shard_map/directions/pallas_call | solution.py:438
  139.9 1.3 copy-done.13
  141.3 3.7 %reduced.1 = f32[1,128,256]{2,1,0:T(8,128)} custom-call(s32[2]{0:T(128)} %pad_add_fusion.place, s32[16]{0:T(128)} %stack.79.order, f32[8,512,128]{2,1,0:T(8,128)} %copy-done.13, f32[512,256]{1,0:T(8,128)} %get-tuple-element.36.sol, f32[512,256]{1,0:T(8,128)} %get-tuple-element.37.fwd, f32[1024,256]{1,0:T(8,128)} %rhs.3), custom_call_target="tpu_custom_call" | custom-call | flops 1048576 | bytes 65536 | tf_op jit(solution)/shard_map/reduced/pallas_call | solution.py:450
  (75 shorter events, 9.3 us)
Async XLA Ops:
  3.5 26.4 %collective-permute-start.1 = (f32[34,32,128]{2,1,0:T(8,128)}, f32[34,32,128]{2,1,0:T(8,128)S(1)}, u32[]{:S(2)}, u32[]{:S(2)}) collective-permute-start(f32[34,32,128]{2,1,0:T(8,128)} %get-tuple-element.23.refs_0_), channel_id=1, source_target_pairs={{0,4},{1,13},{4,8},{5,1},{8,12},{9,5},{12,0},{13,9},{2,6},{3,15},{... | collective-permute-start | bytes 1671176 | tf_op jit(solution)/shard_map/ppermute | solution.py:356
  6.8 26.8 %collective-permute-start.4 = (f32[34,32,128]{2,1,0:T(8,128)}, f32[34,32,128]{2,1,0:T(8,128)S(1)}, u32[]{:S(2)}, u32[]{:S(2)}) collective-permute-start(f32[34,32,128]{2,1,0:T(8,128)} %get-tuple-element.23.refs_0_), channel_id=1, source_target_pairs={{0,2},{2,0},{1,3},{3,1},{4,6},{6,4},{5,7},{7,5},{8,10},{10,8},{9,1... | collective-permute-start | bytes 1671176 | tf_op jit(solution)/shard_map/ppermute | solution.py:358
  8.4 25.2 %collective-permute-start.3 = (f32[34,32,128]{2,1,0:T(8,128)}, f32[34,32,128]{2,1,0:T(8,128)S(1)}, u32[]{:S(2)}, u32[]{:S(2)}) collective-permute-start(f32[34,32,128]{2,1,0:T(8,128)} %get-tuple-element.23.refs_0_), channel_id=1, source_target_pairs={{4,0},{13,1},{8,4},{1,5},{12,8},{5,9},{0,12},{9,13},{6,2},{15,3},{... | collective-permute-start | bytes 1671176 | tf_op jit(solution)/shard_map/ppermute | solution.py:357
  8.4 25.1 %all-to-all-start = ((f32[16,2,32,128]{3,2,1,0:T(8,128)}), f32[16,2,32,128]{3,2,1,0:T(8,128)S(1)}, u32[]{:S(2)}, u32[]{:S(2)}) async-start(f32[16,2,32,128]{3,2,1,0:T(8,128)} %get-tuple-element.20._), calls=%async_computation | async-start | bytes 1048576 | tf_op jit(solution)/shard_map/all_to_all | solution.py:352
  13.5 23.3 %collective-permute-start = (f32[34,32,128]{2,1,0:T(8,128)}, f32[34,32,128]{2,1,0:T(8,128)S(1)}, u32[]{:S(2)}, u32[]{:S(2)}) collective-permute-start(f32[34,32,128]{2,1,0:T(8,128)} %get-tuple-element.23.refs_0_), channel_id=1, source_target_pairs={{0,1},{1,0},{2,3},{3,2},{4,5},{5,4},{6,7},{7,6},{8,9},{9,8},{10,11... | collective-permute-start | bytes 1671176 | tf_op jit(solution)/shard_map/ppermute | solution.py:315
  13.8 19.5 %copy-start.18 = (f32[2,2048]{1,0:T(2,128)S(1)}, f32[2,2048]{1,0:T(2,128)}, u32[]{:S(2)}) copy-start(f32[2,2048]{1,0:T(2,128)} %param.8) | copy-start | bytes 49156
  30.5 9.2 %collective-permute-start.10 = (f32[34,32,128]{2,1,0:T(8,128)S(1)}, f32[34,32,128]{2,1,0:T(8,128)}, u32[]{:S(2)}, u32[]{:S(2)}) collective-permute-start(f32[34,32,128]{2,1,0:T(8,128)S(1)} %follow.2.refs_2_), channel_id=1, source_target_pairs={{0,4},{1,13},{4,8},{5,1},{8,12},{9,5},{12,0},{13,9},{2,6},{3,15},{... | collective-permute-start | bytes 1671176 | tf_op jit(solution)/shard_map/ppermute | solution.py:361
  33.3 9.7 %collective-permute-start.2 = (f32[34,32,128]{2,1,0:T(8,128)S(1)}, f32[34,32,128]{2,1,0:T(8,128)}, u32[]{:S(2)}, u32[]{:S(2)}) collective-permute-start(f32[34,32,128]{2,1,0:T(8,128)S(1)} %follow.2.refs_2_), channel_id=1, source_target_pairs={{0,1},{1,0},{2,3},{3,2},{4,5},{5,4},{6,7},{7,6},{8,9},{9,8},{10,11... | collective-permute-start | bytes 1671176 | tf_op jit(solution)/shard_map/ppermute | solution.py:315
  36.2 20.8 %copy-start = (f32[34,32,128]{2,1,0:T(8,128)}, f32[34,32,128]{2,1,0:T(8,128)S(1)}, u32[]{:S(2)}) copy-start(f32[34,32,128]{2,1,0:T(8,128)S(1)} %get-tuple-element.25.refs_6_) | copy-start | bytes 1671172
  36.2 20.8 %copy-start.1 = (f32[34,32,128]{2,1,0:T(8,128)}, f32[34,32,128]{2,1,0:T(8,128)S(1)}, u32[]{:S(2)}) copy-start(f32[34,32,128]{2,1,0:T(8,128)S(1)} %get-tuple-element.24.refs_4_) | copy-start | bytes 1671172
  36.2 2.0 %collective-permute-start.7 = (f32[2,512,128]{2,1,0:T(8,128)S(1)}, f32[2,512,128]{2,1,0:T(8,128)S(1)}, u32[]{:S(2)}, u32[]{:S(2)}) collective-permute-start(f32[2,512,128]{2,1,0:T(8,128)S(1)} %get-tuple-element.28), channel_id=1, source_target_pairs={{0,1},{1,0},{2,3},{3,2},{4,5},{5,4},{6,7},{7,6},{8,9},{9,8},{10,11... | collective-permute-start | bytes 1572872 | tf_op jit(solution)/shard_map/ppermute | solution.py:380
  36.7 17.5 %collective-permute-start.5 = (f32[34,32,128]{2,1,0:T(8,128)S(1)}, f32[34,32,128]{2,1,0:T(8,128)}, u32[]{:S(2)}, u32[]{:S(2)}) collective-permute-start(f32[34,32,128]{2,1,0:T(8,128)S(1)} %get-tuple-element.24.refs_4_), channel_id=1, source_target_pairs={{0,1},{1,0},{2,3},{3,2},{4,5},{5,4},{6,7},{7,6},{8,9},{9,8},{10,11... | collective-permute-start | bytes 1671176 | tf_op jit(solution)/shard_map/ppermute | solution.py:315
  36.8 20.2 %collective-permute-start.6 = (f32[34,32,128]{2,1,0:T(8,128)S(1)}, f32[34,32,128]{2,1,0:T(8,128)}, u32[]{:S(2)}, u32[]{:S(2)}) collective-permute-start(f32[34,32,128]{2,1,0:T(8,128)S(1)} %get-tuple-element.25.refs_6_), channel_id=1, source_target_pairs={{0,1},{1,0},{2,3},{3,2},{4,5},{5,4},{6,7},{7,6},{8,9},{9,8},{10,11... | collective-permute-start | bytes 1671176 | tf_op jit(solution)/shard_map/ppermute | solution.py:315
  38.2 34.5 %collective-permute-start.9 = (f32[34,32,128]{2,1,0:T(8,128)S(1)}, f32[34,32,128]{2,1,0:T(8,128)S(1)}, u32[]{:S(2)}, u32[]{:S(2)}) collective-permute-start(f32[34,32,128]{2,1,0:T(8,128)S(1)} %get-tuple-element.25.refs_6_), channel_id=1, source_target_pairs={{4,0},{13,1},{8,4},{1,5},{12,8},{5,9},{0,12},{9,13},{6,2},{15,3},{... | collective-permute-start | bytes 1671176 | tf_op jit(solution)/shard_map/ppermute | solution.py:384
  39.8 32.9 %collective-permute-start.8 = (f32[34,32,128]{2,1,0:T(8,128)S(1)}, f32[34,32,128]{2,1,0:T(8,128)S(1)}, u32[]{:S(2)}, u32[]{:S(2)}) collective-permute-start(f32[34,32,128]{2,1,0:T(8,128)S(1)} %get-tuple-element.25.refs_6_), channel_id=1, source_target_pairs={{0,4},{1,13},{4,8},{5,1},{8,12},{9,5},{12,0},{13,9},{2,6},{3,15},{... | collective-permute-start | bytes 1671176 | tf_op jit(solution)/shard_map/ppermute | solution.py:383
  43.0 29.7 %collective-permute-start.11 = (f32[34,32,128]{2,1,0:T(8,128)}, f32[34,32,128]{2,1,0:T(8,128)S(1)}, u32[]{:S(2)}, u32[]{:S(2)}) collective-permute-start(f32[34,32,128]{2,1,0:T(8,128)} %collective-permute-done.10.refs_4_.refs_12_), channel_id=1, source_target_pairs={{0,2},{2,0},{1,3},{3,1},{4,6},{6,4},{5,7},{7,5},{8,10},{10,8},{9,1... | collective-permute-start | bytes 1671176 | tf_op jit(solution)/shard_map/ppermute | solution.py:382
  45.1 27.6 %all-to-all-start.1 = ((f32[64,16,128]{2,1,0:T(8,128)}), f32[64,16,128]{2,1,0:T(8,128)}, u32[]{:S(2)}, u32[]{:S(2)}) async-start(f32[64,16,128]{2,1,0:T(8,128)} %bitcast.25), calls=%async_computation.1 | async-start | bytes 1048576 | tf_op jit(solution)/shard_map/all_to_all | solution.py:381
  54.2 32.0 %collective-permute-start.14 = (f32[34,32,128]{2,1,0:T(8,128)}, f32[34,32,128]{2,1,0:T(8,128)S(1)}, u32[]{:S(2)}, u32[]{:S(2)}) collective-permute-start(f32[34,32,128]{2,1,0:T(8,128)} %collective-permute-done.10.refs_4_.refs_12_), channel_id=1, source_target_pairs={{0,1},{1,0},{2,3},{3,2},{4,5},{5,4},{6,7},{7,6},{8,9},{9,8},{10,11... | collective-permute-start | bytes 1671176 | tf_op jit(solution)/shard_map/ppermute | solution.py:315
  75.3 10.9 %collective-permute-start.12 = (f32[34,32,128]{2,1,0:T(8,128)S(1)}, f32[34,32,128]{2,1,0:T(8,128)S(1)}, u32[]{:S(2)}, u32[]{:S(2)}) collective-permute-start(f32[34,32,128]{2,1,0:T(8,128)S(1)} %get-tuple-element.30.refs_0_.refs_8_), channel_id=1, source_target_pairs={{0,1},{1,0},{2,3},{3,2},{4,5},{5,4},{6,7},{7,6},{8,9},{9,8},{10,11... | collective-permute-start | bytes 1671176 | tf_op jit(solution)/shard_map/ppermute | solution.py:315
  75.3 10.9 %collective-permute-start.13 = (f32[34,32,128]{2,1,0:T(8,128)S(1)}, f32[34,32,128]{2,1,0:T(8,128)}, u32[]{:S(2)}, u32[]{:S(2)}) collective-permute-start(f32[34,32,128]{2,1,0:T(8,128)S(1)} %get-tuple-element.31.refs_2_.refs_10_), channel_id=1, source_target_pairs={{0,1},{1,0},{2,3},{3,2},{4,5},{5,4},{6,7},{7,6},{8,9},{9,8},{10,11... | collective-permute-start | bytes 1671176 | tf_op jit(solution)/shard_map/ppermute | solution.py:315
  75.8 10.4 %collective-permute-start.15 = (f32[34,32,128]{2,1,0:T(8,128)S(1)}, f32[34,32,128]{2,1,0:T(8,128)}, u32[]{:S(2)}, u32[]{:S(2)}) collective-permute-start(f32[34,32,128]{2,1,0:T(8,128)S(1)} %get-tuple-element.32.refs_6_.refs_14_), channel_id=1, source_target_pairs={{0,1},{1,0},{2,3},{3,2},{4,5},{5,4},{6,7},{7,6},{8,9},{9,8},{10,11... | collective-permute-start | bytes 1671176 | tf_op jit(solution)/shard_map/ppermute | solution.py:315
  75.9 26.9 %all-to-all-start.3 = ((f32[64,16,128]{2,1,0:T(8,128)}), f32[64,16,128]{2,1,0:T(8,128)S(1)}, u32[]{:S(2)}, u32[]{:S(2)}) async-start(f32[64,16,128]{2,1,0:T(8,128)} %get-tuple-element.35), calls=%async_computation.3 | async-start | bytes 1048576 | tf_op jit(solution)/shard_map/all_to_all | solution.py:399
  102.8 37.1 %all-to-all-start.2 = ((f32[8,512,128]{2,1,0:T(8,128)}), f32[8,512,128]{2,1,0:T(8,128)S(1)}, u32[]{:S(2)}, u32[]{:S(2)}) async-start(f32[8,512,128]{2,1,0:T(8,128)} %get-tuple-element.33), calls=%async_computation.2 | async-start | bytes 4194304 | tf_op jit(solution)/shard_map/all_to_all | solution.py:436
  109.1 2.9 %collective-permute-start.16 = (f32[2,512,128]{2,1,0:T(8,128)S(1)}, f32[2,512,128]{2,1,0:T(8,128)S(1)}, u32[]{:S(2)}, u32[]{:S(2)}) collective-permute-start(f32[2,512,128]{2,1,0:T(8,128)S(1)} %follow.3.mine), channel_id=1, source_target_pairs={{0,1},{1,0},{2,3},{3,2},{4,5},{5,4},{6,7},{7,6},{8,9},{9,8},{10,11... | collective-permute-start | bytes 1572872 | tf_op jit(solution)/shard_map/ppermute | solution.py:403
  (16 other events, 79.7 us)

commit v5 on v4

--- a/solution.py
+++ b/solution.py
@@ -138,67 +138,57 @@
 
 
 def schur_kernel(masked, slack, _, *refs):
-    *pieces, out, done, high, low, held, sems = refs
+    *pieces, out, done, left = refs
     step = pl.program_id(0)
-    depth = masked.shape[1] // 2
-    blocks, width = held.shape[1:3]
+    done[...] = jnp.zeros_like(done)
+    count, width = pieces[0].shape[:2]
+    depth = count * BLOCK
+    per_scen = slack.shape[1] // depth
+    for e in range(count):
+        at = e * BLOCK
+        first = pl.multiple_of(lax.rem(step, per_scen) * depth + at, BLOCK)
+        both = slack[:, pl.ds(first, BLOCK)]
+        inverse = 1.0 / jnp.where(step < per_scen, both[0:1], both[1:2])
+        for k, piece in enumerate(pieces):
+            high, low = split(piece[e] * inverse)
+            rows = slice(k * width, (k + 1) * width)
+            left[rows, at : at + BLOCK] = high
+            left[rows, depth + at : depth + at + BLOCK] = high
+            left[rows, 2 * depth + at : 2 * depth + at + BLOCK] = low
 
     @pl.when(step == 0)
     def _():
-        done[...] = jnp.zeros_like(done)
         out[...] = jnp.zeros_like(out)
-        copies = [
-            pltpu.make_async_copy(piece.at[pl.ds(0, blocks)], held.at[k], sems.at[k]) for k, piece in enumerate(pieces)
-        ]
-        for copy in copies:
-            copy.start()
-        for k, copy in enumerate(copies):
-            copy.wait()
-
-            def prepare(e, carry):
-                inverse = 1.0 / slack[pl.ds(e, 1), :]
-                lanes = pl.ds(pl.multiple_of(e * BLOCK, BLOCK), BLOCK)
-                rows = slice(k * width, (k + 1) * width)
-                high[rows, lanes], low[rows, lanes] = split(held[k, e] * inverse)
-                return carry
-
-            lax.fori_loop(0, blocks, prepare, 0, unroll=4)
-
-    now = pl.ds(pl.multiple_of(step * depth, depth), depth)
+
+    wide = 2 * BLOCK
     dims = ((1,), (0,))
-    wide = 2 * BLOCK
     for n in range(masked.shape[2] // wide):
         lanes = slice(n * wide, (n + 1) * wide)
-        product = dot(high[:, now], masked[0, :depth, lanes], dims, lax.Precision.DEFAULT)
-        product += dot(high[:, now], masked[0, depth:, lanes], dims, lax.Precision.DEFAULT)
-        product += dot(low[:, now], masked[0, :depth, lanes], dims, lax.Precision.DEFAULT)
+        product = dot(left[:, : 2 * depth], masked[0, :, lanes], dims, lax.Precision.DEFAULT)
+        product += dot(left[:, 2 * depth :], masked[0, :depth, lanes], dims, lax.Precision.DEFAULT)
         out[2 * n] += product[:, :BLOCK]
         out[2 * n + 1] += product[:, BLOCK:]
 
 
 def schur_product(masked, slack, pieces, scens, part, earlier):
     steps, depth, own_width = masked.shape
+    depth //= 2
     width = pieces[0].shape[1]
     rows = len(pieces) * width
-    total = steps * depth // 2
     shape = (scens, rows, own_width // scens)
     return pl.pallas_call(
         schur_kernel,
         grid=(steps,),
         in_specs=[
-            pl.BlockSpec((1, depth, own_width), lambda t: (t, 0, 0)),
+            pl.BlockSpec((1, 2 * depth, own_width), lambda t: (t, 0, 0)),
             pl.BlockSpec(slack.shape, lambda t: (0, 0)),
+            ANY,
         ]
-        + [ANY] * (1 + len(pieces)),
+        + [pl.BlockSpec((depth // BLOCK, width, BLOCK), lambda t: (t, 0, 0))] * len(pieces),
         out_specs=[pl.BlockSpec(shape, lambda t: (0, part, 0)), DONE_SPEC],
         out_shape=[jax.ShapeDtypeStruct((scens, 2 * rows, own_width // scens), F32), DONE],
         input_output_aliases={2: 0} if part else {},
-        scratch_shapes=[
-            pltpu.VMEM((rows, total), BF16),
-            pltpu.VMEM((rows, total), BF16),
-            pltpu.VMEM((len(pieces), total // BLOCK, width, BLOCK), F32),
-            pltpu.SemaphoreType.DMA((len(pieces),)),
-        ],
+        scratch_shapes=[pltpu.VMEM((rows, 3 * depth), BF16)],
         compiler_params=WIDE_PARAMS,
         cost_estimate=SHORT,
         name="schur",
@@ -212,10 +202,11 @@
         left, right = w[first : first + SLAB, :BLOCK], w[first : first + SLAB, BLOCK:]
         lower, upper = [], []
         for k in range(SLAB):
-            scale = lax.rsqrt(cols[k][k : k + 1, :])
-            square = scale * scale
+            pivot = cols[k][k : k + 1, :]
+            scale = lax.rsqrt(pivot)
+            inverse = 1.0 / pivot
             for m in range(k + 1, SLAB):
-                cols[m] = cols[m] - cols[k] * (cols[k][m : m + 1, :] * square)
+                cols[m] = cols[m] - cols[k] * (cols[k][m : m + 1, :] * inverse)
             low = cols[k] * scale
             u0 = left[k : k + 1, :] * scale
             u1 = right[k : k + 1, :] * scale
@@ -253,24 +244,19 @@
     shape = (BLOCK, BLOCK)
     eye = (lax.broadcasted_iota(jnp.int32, shape, 0) == lax.broadcasted_iota(jnp.int32, shape, 1)).astype(F32)
 
-    def outer(step, carry):
-        here = pl.ds(pl.multiple_of(step * BLOCK, BLOCK), BLOCK)
+    for step in range(steps):
+        after = (step + 1) * BLOCK
+        here = slice(step * BLOCK, after)
         w[:, :BLOCK] = m[here, here]
         w[:, BLOCK:] = eye
         eliminate(w)
         inverse = w[:, BLOCK:]
         linv[step] = inverse
-        m[here, :] = dot_nn(inverse, m[here, :])
-
-        def update(later, inner):
-            there = pl.ds(pl.multiple_of(later * BLOCK, BLOCK), BLOCK)
-            m[there, :] = m[there, :] - dot_tn(m[here, there], m[here, :])
-            return inner
-
-        lax.fori_loop(step + 1, steps, update, 0)
-        return carry
-
-    lax.fori_loop(0, steps, outer, 0)
+        m[here, after:] = dot_nn(inverse, m[here, after:])
+        for later in range(step + 1, steps):
+            first = later * BLOCK
+            there = slice(first, first + BLOCK)
+            m[there, first:] = m[there, first:] - dot_tn(m[here, there], m[here, first:])
     fwd[...] = m[:, size:]
     for step in reversed(range(steps)):
         rows = slice(step * BLOCK, (step + 1) * BLOCK)
@@ -382,13 +368,12 @@
     opposite_beside = lax.ppermute(opposite, "z", SWAP)
     first_beside = lax.ppermute(beside, ("x", "core"), first_way)
     second_beside = lax.ppermute(beside, ("x", "core"), second_way)
-    slack_rows = slack.reshape(own * blocks, BLOCK)
     near_pieces = with_other_core([piece, first, second, beside])
-    schur, near_done = schur_product(masked, slack_rows, near_pieces, scens, 0, masked_done)
+    schur, near_done = schur_product(masked, slack, near_pieces, scens, 0, masked_done)
 
     share, first_beside, second_beside, opposite_beside = pl.pallas_call(
         total_kernel,
-        in_specs=[VMEM] + [ANY] * 4,
+        in_specs=[VMEM, ANY] + [ANY] * 3,
         out_specs=[VMEM] + [ANY] * 3,
         out_shape=[shape_of(v) for v in (pair, first_beside, second_beside, opposite_beside)],
         input_output_aliases={2: 1, 3: 2, 4: 3},
@@ -398,7 +383,7 @@
     )(pair, near_done, first_beside, second_beside, opposite_beside)
     half = lax.all_to_all(share, ALL_CHIPS, 0, 0, tiled=True).reshape(2, PW, BLOCK)
     far_pieces = with_other_core([first_beside, second_beside, opposite, opposite_beside])
-    schur, far_done = schur_product(masked, slack_rows, far_pieces, scens, 1, schur)
+    schur, far_done = schur_product(masked, slack, far_pieces, scens, 1, schur)
     half = follow(far_done, half)
     other = lax.ppermute(half, "core", SWAP)
 

time: 146 us -> 138 us (0.945)
  Pallas kernels: 84.1 us -> 76.2 us
    pallas_call x3, Pallas kernels: 33.2 us -> 29 us  [the longest x2 27.1 us: schur_product(): pl.pallas_call(schur_kernel, grid=(steps,), in_specs=[pl.BlockSpec((1, 2...]
    pallas_call x1, Pallas kernels: 24.5 us -> 20.8 us  [per_device(): pl.pallas_call(solve_kernel, grid=(1,), in_specs=[smem, smem, pl.BlockSpe...]
    unnamed x38 -> x36, local copies, waits for them, and re-layouts: 5.24 us -> 5.23 us
  transfers between devices with their start and end apart: 21 -> 21, of which waited for: 3 -> 4; matrix products, arithmetic and copies ran while one was open for 3% -> 3% of each run, Pallas kernels for 53% -> 51%
where the time goes in v5:
time: 138 us; the launch traced here: 137 us
  Pallas kernels  76.2 us (55%)
  starting transfers between devices  48.1 us (35%)
  local copies, waits for them, and re-layouts  6.74 us (5%)
  waiting for transfers between devices  3.23 us (2%)
  other arithmetic  2.14 us (2%)
    pallas_call x2, Pallas kernels, schur_product(): pl.pallas_call(schur_kernel, grid=(steps,), in_specs=[pl.BlockSpec((1, 2...  27.1 us
    pallas_call x1, Pallas kernels, per_device(): pl.pallas_call(solve_kernel, grid=(1,), in_specs=[smem, smem, pl.BlockSpe...  20.8 us
    pallas_call x1, Pallas kernels, mask_parts(): pl.pallas_call(mask_kernel, grid=(STEPS,), in_specs=[pl.BlockSpec(memory_...  15.3 us
    all_to_all x1, starting transfers between devices, per_device(): lax.all_to_all(share, ALL_CHIPS, 0, 0, tiled=True).reshape(2, PW, BLOCK)  10.1 us
    all_to_all x1, starting transfers between devices, per_device(): lax.all_to_all(pair.reshape(chips, 2 * PW // chips, BLOCK), ALL_CHIPS, 0,...  8.48 us
    all_to_all x1, starting transfers between devices, per_device(): schur = lax.all_to_all(schur, 'scen', 0, 0, tiled=True)  6.42 us
    unnamed x36, local copies, waits for them, and re-layouts  5.23 us
    all_to_all x1, starting transfers between devices, per_device(): mine = lax.all_to_all(row_blocks, COL, 0, 0, tiled=True)  5.07 us
  transfers between devices with their start and end apart: 21, of which 4 were waited for; matrix products, arithmetic and copies ran while one was open for 3% of the time, Pallas kernels for 51%

profile of v5, /device:TPU:1, one launch (start us, length us, event | category | flops | bytes accessed | tf_op | source)
XLA Modules:
  0.0 137.3 jit_solution(15111746742429731878)
XLA Ops:
  0.6 2.8 %panel.1 = (f32[16,2,32,128]{3,2,1,0:T(8,128)}, f32[34,32,128]{2,1,0:T(8,128)}) custom-call(s32[2,8,16]{2,1,0:T(8,128)} %bitcast.26, f32[2,2048,1024]{2,1,0:T(8,128)} %border.3, f32[1024,256]{1,0:T(8,128)} %rhs.3), custom_call_target="tpu_custom_call" | custom-call | tf_op jit(solution)/shard_map/panel/pallas_call | solution.py:318
  3.5 3.3 %collective-permute-start.1 = (f32[34,32,128]{2,1,0:T(8,128)}, f32[34,32,128]{2,1,0:T(8,128)S(1)}, u32[]{:S(2)}, u32[]{:S(2)}) collective-permute-start(f32[34,32,128]{2,1,0:T(8,128)} %get-tuple-element.23.refs_0_), channel_id=1, source_target_pairs={{0,4},{1,13},{4,8},{5,1},{8,12},{9,5},{12,0},{13,9},{2,6},{3,15},{... | collective-permute-start | bytes 1671176 | tf_op jit(solution)/shard_map/ppermute | solution.py:342
  6.8 1.6 %collective-permute-start.4 = (f32[34,32,128]{2,1,0:T(8,128)}, f32[34,32,128]{2,1,0:T(8,128)S(1)}, u32[]{:S(2)}, u32[]{:S(2)}) collective-permute-start(f32[34,32,128]{2,1,0:T(8,128)} %get-tuple-element.23.refs_0_), channel_id=1, source_target_pairs={{0,2},{2,0},{1,3},{3,1},{4,6},{6,4},{5,7},{7,5},{8,10},{10,8},{9,1... | collective-permute-start | bytes 1671176 | tf_op jit(solution)/shard_map/ppermute | solution.py:344
  8.4 5.1 %all-to-all-start = ((f32[16,2,32,128]{3,2,1,0:T(8,128)}), f32[16,2,32,128]{3,2,1,0:T(8,128)S(1)}, u32[]{:S(2)}, u32[]{:S(2)}) async-start(f32[16,2,32,128]{3,2,1,0:T(8,128)} %get-tuple-element.20._), calls=%async_computation | async-start | bytes 1048576 | tf_op jit(solution)/shard_map/all_to_all | solution.py:338
  13.8 15.3 %mask.1 = (bf16[8,1024,1024]{2,1,0:T(8,128)(2,1)}, f32[8,128]{1,0:T(8,128)}) custom-call(s32[2,8,16]{2,1,0:T(8,128)} %bitcast.27, f32[2,2048,1024]{2,1,0:T(8,128)} %border.3, f32[16,2,32,128]{3,2,1,0:T(8,128)} %get-tuple-element.20._), custom_call_target="tpu_custom_call" | custom-call | flops 1048576 | bytes 65536 | tf_op jit(solution)/shard_map/mask/pallas_call | solution.py:107
  30.5 2.7 %collective-permute-start.10 = (f32[34,32,128]{2,1,0:T(8,128)S(1)}, f32[34,32,128]{2,1,0:T(8,128)}, u32[]{:S(2)}, u32[]{:S(2)}) collective-permute-start(f32[34,32,128]{2,1,0:T(8,128)S(1)} %follow.2.refs_2_), channel_id=1, source_target_pairs={{0,4},{1,13},{4,8},{5,1},{8,12},{9,5},{12,0},{13,9},{2,6},{3,15},{... | collective-permute-start | bytes 1671176 | tf_op jit(solution)/shard_map/ppermute | solution.py:347
  34.9 1.8 %pivot.1 = (f32[2,512,128]{2,1,0:T(8,128)S(1)}, f32[2,512,128]{2,1,0:T(8,128)S(1)}, f32[34,32,128]{2,1,0:T(8,128)S(1)}, f32[34,32,128]{2,1,0:T(8,128)S(1)}) custom-call(s32[1]{0:T(128)} %bitcast.19.core, f32[16,2,32,128]{3,2,1,0:T(8,128)S(1)} %all-to-all-done.mine, ...), custom_call_target="tpu_custom_call", output_to_operand_aliasing={{2}: (5, {}), {3}: (6, {})} | custom-call | flops 1048576 | bytes 65536 | tf_op jit(solution)/shard_map/pivot/pallas_call | solution.py:354
  37.8 1.0 collective-permute-done.7
  39.7 3.2 %collective-permute-start.8 = (f32[34,32,128]{2,1,0:T(8,128)S(1)}, f32[34,32,128]{2,1,0:T(8,128)S(1)}, u32[]{:S(2)}, u32[]{:S(2)}) collective-permute-start(f32[34,32,128]{2,1,0:T(8,128)S(1)} %get-tuple-element.25.refs_6_), channel_id=1, source_target_pairs={{0,4},{1,13},{4,8},{5,1},{8,12},{9,5},{12,0},{13,9},{2,6},{3,15},{... | collective-permute-start | bytes 1671176 | tf_op jit(solution)/shard_map/ppermute | solution.py:369
  42.9 1.2 collective-permute-start.11
  44.1 0.9 add.201
  45.0 8.5 %all-to-all-start.1 = ((f32[64,16,128]{2,1,0:T(8,128)}), f32[64,16,128]{2,1,0:T(8,128)}, u32[]{:S(2)}, u32[]{:S(2)}) async-start(f32[64,16,128]{2,1,0:T(8,128)} %bitcast.25), calls=%async_computation.1 | async-start | bytes 1048576 | tf_op jit(solution)/shard_map/all_to_all | solution.py:367
  53.5 2.2 %collective-permute-start.14 = (f32[34,32,128]{2,1,0:T(8,128)}, f32[34,32,128]{2,1,0:T(8,128)S(1)}, u32[]{:S(2)}, u32[]{:S(2)}) collective-permute-start(f32[34,32,128]{2,1,0:T(8,128)} %collective-permute-done.10.refs_4_.refs_12_), channel_id=1, source_target_pairs={{0,1},{1,0},{2,3},{3,2},{4,5},{5,4},{6,7},{7,6},{8,9},{9,8},{10,11... | collective-permute-start | bytes 1671176 | tf_op jit(solution)/shard_map/ppermute | solution.py:301
  55.8 13.5 %schur.2 = (f32[8,512,128]{2,1,0:T(8,128)}, f32[8,128]{1,0:T(8,128)}) custom-call(bf16[8,1024,1024]{2,1,0:T(8,128)(2,1)} %get-tuple-element.21.masked, f32[2,2048]{1,0:T(2,128)} %slack.3, f32[8,128]{1,0:T(8,128)} %get-tuple-element.22.refs_0_._, f32[34,32,128]{2,1,0:T(8,128)} %get-tuple-element.23.refs_0_, f32[34,32,128]{2,1,0:T(8,128)} %copy-done.14, ...), custom_call_target="tpu_custom_call" | custom-call | flops 1048576 | bytes 65536 | tf_op jit(solution)/shard_map/schur/pallas_call | solution.py:179
  70.1 1.9 %total.1 = (f32[64,16,128]{2,1,0:T(8,128)}, f32[34,32,128]{2,1,0:T(8,128)S(1)}, f32[34,32,128]{2,1,0:T(8,128)S(1)}, f32[34,32,128]{2,1,0:T(8,128)S(1)}) custom-call(f32[64,16,128]{2,1,0:T(8,128)} %all-to-all-done.1.pair, f32[8,128]{1,0:T(8,128)S(1)} %copy-done.12, ...), custom_call_target="tpu_custom_call", output_to_operand_aliasing={{1}: (2, {}), {2}: (3, {}), {3}: (4, {})} | custom-call | flops 1048576 | bytes 65536 | tf_op jit(solution)/shard_map/total/pallas_call | solution.py:374
  72.6 10.1 %all-to-all-start.3 = ((f32[64,16,128]{2,1,0:T(8,128)}), f32[64,16,128]{2,1,0:T(8,128)S(1)}, u32[]{:S(2)}, u32[]{:S(2)}) async-start(f32[64,16,128]{2,1,0:T(8,128)} %get-tuple-element.35), calls=%async_computation.3 | async-start | bytes 1048576 | tf_op jit(solution)/shard_map/all_to_all | solution.py:384
  83.7 13.5 %schur.3 = (f32[8,512,128]{2,1,0:T(8,128)}, f32[8,128]{1,0:T(8,128)}) custom-call(bf16[8,1024,1024]{2,1,0:T(8,128)(2,1)} %get-tuple-element.21.masked, f32[2,2048]{1,0:T(2,128)} %slack.3, f32[8,512,128]{2,1,0:T(8,128)} %get-tuple-element.26._, f32[34,32,128]{2,1,0:T(8,128)} %copy-done.4, f32[34,32,128]{2,1,0:T(8,128)} %copy-done.16, ...), custom_call_target="tpu_custom_call", output_to_operand_aliasing={{0}: (2, {})} | custom-call | flops 1048576 | bytes 65536 | tf_op jit(solution)/shard_map/schur/pallas_call | solution.py:179
  97.3 6.4 %all-to-all-start.2 = ((f32[8,512,128]{2,1,0:T(8,128)}), f32[8,512,128]{2,1,0:T(8,128)S(1)}, u32[]{:S(2)}, u32[]{:S(2)}) async-start(f32[8,512,128]{2,1,0:T(8,128)} %get-tuple-element.33), calls=%async_computation.2 | async-start | bytes 4194304 | tf_op jit(solution)/shard_map/all_to_all | solution.py:421
  103.7 1.5 %collective-permute-start.16 = (f32[2,512,128]{2,1,0:T(8,128)S(1)}, f32[2,512,128]{2,1,0:T(8,128)S(1)}, u32[]{:S(2)}, u32[]{:S(2)}) collective-permute-start(f32[2,512,128]{2,1,0:T(8,128)S(1)} %follow.3.mine), channel_id=1, source_target_pairs={{0,1},{1,0},{2,3},{3,2},{4,5},{5,4},{6,7},{7,6},{8,9},{9,8},{10,11... | collective-permute-start | bytes 1572872 | tf_op jit(solution)/shard_map/ppermute | solution.py:388
  107.6 20.8 %solve.1 = (f32[512,256]{1,0:T(8,128)}, f32[512,256]{1,0:T(8,128)}) custom-call(s32[1]{0:T(128)} %bitcast.19.core, s32[16]{0:T(128)} %stack.79.order, f32[2,512,128]{2,1,0:T(8,128)} %copy-done.6, f32[2,512,128]{2,1,0:T(8,128)} %copy-done.17, f32[34,32,128]{2,1,0:T(8,128)} %get-tuple-element.23.refs_0_, f32[34,32,128]{2,1,0:T(8,128)} %copy-done.14, ...), custom_call_target="tpu_custom_call" | custom-call | flops 1048576 | bytes 65536 | tf_op jit(solution)/shard_map/solve/pallas_call | solution.py:399
  128.4 2.7 %directions.1 = f32[2,128,256]{2,1,0:T(8,128)} custom-call(f32[512,256]{1,0:T(8,128)} %get-tuple-element.36.sol, f32[16,2,32,128]{3,2,1,0:T(8,128)} %copy-done.7, f32[2,128]{1,0:T(2,128)} %copy-done.11, f32[2,128,256]{2,1,0:T(8,128)} %scen_rhs.1), custom_call_target="tpu_custom_call" | custom-call | flops 1048576 | bytes 65536 | tf_op jit(solution)/shard_map/directions/pallas_call | solution.py:423
  131.0 1.2 all-to-all-done.2.schur
  132.2 1.3 copy-done.13
  133.6 3.7 %reduced.1 = f32[1,128,256]{2,1,0:T(8,128)} custom-call(s32[2]{0:T(128)} %pad_add_fusion.place, s32[16]{0:T(128)} %stack.79.order, f32[8,512,128]{2,1,0:T(8,128)} %copy-done.13, f32[512,256]{1,0:T(8,128)} %get-tuple-element.36.sol, f32[512,256]{1,0:T(8,128)} %get-tuple-element.37.fwd, f32[1024,256]{1,0:T(8,128)} %rhs.3), custom_call_target="tpu_custom_call" | custom-call | flops 1048576 | bytes 65536 | tf_op jit(solution)/shard_map/reduced/pallas_call | solution.py:435
  (72 shorter events, 9.9 us)
Async XLA Ops:
  3.5 26.4 %collective-permute-start.1 = (f32[34,32,128]{2,1,0:T(8,128)}, f32[34,32,128]{2,1,0:T(8,128)S(1)}, u32[]{:S(2)}, u32[]{:S(2)}) collective-permute-start(f32[34,32,128]{2,1,0:T(8,128)} %get-tuple-element.23.refs_0_), channel_id=1, source_target_pairs={{0,4},{1,13},{4,8},{5,1},{8,12},{9,5},{12,0},{13,9},{2,6},{3,15},{... | collective-permute-start | bytes 1671176 | tf_op jit(solution)/shard_map/ppermute | solution.py:342
  6.8 27.4 %collective-permute-start.4 = (f32[34,32,128]{2,1,0:T(8,128)}, f32[34,32,128]{2,1,0:T(8,128)S(1)}, u32[]{:S(2)}, u32[]{:S(2)}) collective-permute-start(f32[34,32,128]{2,1,0:T(8,128)} %get-tuple-element.23.refs_0_), channel_id=1, source_target_pairs={{0,2},{2,0},{1,3},{3,1},{4,6},{6,4},{5,7},{7,5},{8,10},{10,8},{9,1... | collective-permute-start | bytes 1671176 | tf_op jit(solution)/shard_map/ppermute | solution.py:344
  8.4 25.7 %collective-permute-start.3 = (f32[34,32,128]{2,1,0:T(8,128)}, f32[34,32,128]{2,1,0:T(8,128)S(1)}, u32[]{:S(2)}, u32[]{:S(2)}) collective-permute-start(f32[34,32,128]{2,1,0:T(8,128)} %get-tuple-element.23.refs_0_), channel_id=1, source_target_pairs={{4,0},{13,1},{8,4},{1,5},{12,8},{5,9},{0,12},{9,13},{6,2},{15,3},{... | collective-permute-start | bytes 1671176 | tf_op jit(solution)/shard_map/ppermute | solution.py:343
  8.4 25.7 %all-to-all-start = ((f32[16,2,32,128]{3,2,1,0:T(8,128)}), f32[16,2,32,128]{3,2,1,0:T(8,128)S(1)}, u32[]{:S(2)}, u32[]{:S(2)}) async-start(f32[16,2,32,128]{3,2,1,0:T(8,128)} %get-tuple-element.20._), calls=%async_computation | async-start | bytes 1048576 | tf_op jit(solution)/shard_map/all_to_all | solution.py:338
  13.5 23.9 %collective-permute-start = (f32[34,32,128]{2,1,0:T(8,128)}, f32[34,32,128]{2,1,0:T(8,128)S(1)}, u32[]{:S(2)}, u32[]{:S(2)}) collective-permute-start(f32[34,32,128]{2,1,0:T(8,128)} %get-tuple-element.23.refs_0_), channel_id=1, source_target_pairs={{0,1},{1,0},{2,3},{3,2},{4,5},{5,4},{6,7},{7,6},{8,9},{9,8},{10,11... | collective-permute-start | bytes 1671176 | tf_op jit(solution)/shard_map/ppermute | solution.py:301
  30.5 14.5 %copy-start.2 = (f32[34,32,128]{2,1,0:T(8,128)}, f32[34,32,128]{2,1,0:T(8,128)S(1)}, u32[]{:S(2)}) copy-start(f32[34,32,128]{2,1,0:T(8,128)S(1)} %follow.2.refs_2_) | copy-start | bytes 1671172
  30.5 9.2 %collective-permute-start.10 = (f32[34,32,128]{2,1,0:T(8,128)S(1)}, f32[34,32,128]{2,1,0:T(8,128)}, u32[]{:S(2)}, u32[]{:S(2)}) collective-permute-start(f32[34,32,128]{2,1,0:T(8,128)S(1)} %follow.2.refs_2_), channel_id=1, source_target_pairs={{0,4},{1,13},{4,8},{5,1},{8,12},{9,5},{12,0},{13,9},{2,6},{3,15},{... | collective-permute-start | bytes 1671176 | tf_op jit(solution)/shard_map/ppermute | solution.py:347
  33.2 9.7 %collective-permute-start.2 = (f32[34,32,128]{2,1,0:T(8,128)S(1)}, f32[34,32,128]{2,1,0:T(8,128)}, u32[]{:S(2)}, u32[]{:S(2)}) collective-permute-start(f32[34,32,128]{2,1,0:T(8,128)S(1)} %follow.2.refs_2_), channel_id=1, source_target_pairs={{0,1},{1,0},{2,3},{3,2},{4,5},{5,4},{6,7},{7,6},{8,9},{9,8},{10,11... | collective-permute-start | bytes 1671176 | tf_op jit(solution)/shard_map/ppermute | solution.py:301
  36.7 19.1 %copy-start = (f32[34,32,128]{2,1,0:T(8,128)}, f32[34,32,128]{2,1,0:T(8,128)S(1)}, u32[]{:S(2)}) copy-start(f32[34,32,128]{2,1,0:T(8,128)S(1)} %get-tuple-element.25.refs_6_) | copy-start | bytes 1671172
  36.7 19.1 %copy-start.1 = (f32[34,32,128]{2,1,0:T(8,128)}, f32[34,32,128]{2,1,0:T(8,128)S(1)}, u32[]{:S(2)}) copy-start(f32[34,32,128]{2,1,0:T(8,128)S(1)} %get-tuple-element.24.refs_4_) | copy-start | bytes 1671172
  36.7 2.0 %collective-permute-start.7 = (f32[2,512,128]{2,1,0:T(8,128)S(1)}, f32[2,512,128]{2,1,0:T(8,128)S(1)}, u32[]{:S(2)}, u32[]{:S(2)}) collective-permute-start(f32[2,512,128]{2,1,0:T(8,128)S(1)} %get-tuple-element.28), channel_id=1, source_target_pairs={{0,1},{1,0},{2,3},{3,2},{4,5},{5,4},{6,7},{7,6},{8,9},{9,8},{10,11... | collective-permute-start | bytes 1572872 | tf_op jit(solution)/shard_map/ppermute | solution.py:366
  37.2 16.3 %collective-permute-start.5 = (f32[34,32,128]{2,1,0:T(8,128)S(1)}, f32[34,32,128]{2,1,0:T(8,128)}, u32[]{:S(2)}, u32[]{:S(2)}) collective-permute-start(f32[34,32,128]{2,1,0:T(8,128)S(1)} %get-tuple-element.24.refs_4_), channel_id=1, source_target_pairs={{0,1},{1,0},{2,3},{3,2},{4,5},{5,4},{6,7},{7,6},{8,9},{9,8},{10,11... | collective-permute-start | bytes 1671176 | tf_op jit(solution)/shard_map/ppermute | solution.py:301
  37.3 18.4 %collective-permute-start.6 = (f32[34,32,128]{2,1,0:T(8,128)S(1)}, f32[34,32,128]{2,1,0:T(8,128)}, u32[]{:S(2)}, u32[]{:S(2)}) collective-permute-start(f32[34,32,128]{2,1,0:T(8,128)S(1)} %get-tuple-element.25.refs_6_), channel_id=1, source_target_pairs={{0,1},{1,0},{2,3},{3,2},{4,5},{5,4},{6,7},{7,6},{8,9},{9,8},{10,11... | collective-permute-start | bytes 1671176 | tf_op jit(solution)/shard_map/ppermute | solution.py:301
  38.8 30.6 %collective-permute-start.9 = (f32[34,32,128]{2,1,0:T(8,128)S(1)}, f32[34,32,128]{2,1,0:T(8,128)S(1)}, u32[]{:S(2)}, u32[]{:S(2)}) collective-permute-start(f32[34,32,128]{2,1,0:T(8,128)S(1)} %get-tuple-element.25.refs_6_), channel_id=1, source_target_pairs={{4,0},{13,1},{8,4},{1,5},{12,8},{5,9},{0,12},{9,13},{6,2},{15,3},{... | collective-permute-start | bytes 1671176 | tf_op jit(solution)/shard_map/ppermute | solution.py:370
  39.7 29.6 %collective-permute-start.8 = (f32[34,32,128]{2,1,0:T(8,128)S(1)}, f32[34,32,128]{2,1,0:T(8,128)S(1)}, u32[]{:S(2)}, u32[]{:S(2)}) collective-permute-start(f32[34,32,128]{2,1,0:T(8,128)S(1)} %get-tuple-element.25.refs_6_), channel_id=1, source_target_pairs={{0,4},{1,13},{4,8},{5,1},{8,12},{9,5},{12,0},{13,9},{2,6},{3,15},{... | collective-permute-start | bytes 1671176 | tf_op jit(solution)/shard_map/ppermute | solution.py:369
  42.9 26.4 %collective-permute-start.11 = (f32[34,32,128]{2,1,0:T(8,128)}, f32[34,32,128]{2,1,0:T(8,128)S(1)}, u32[]{:S(2)}, u32[]{:S(2)}) collective-permute-start(f32[34,32,128]{2,1,0:T(8,128)} %collective-permute-done.10.refs_4_.refs_12_), channel_id=1, source_target_pairs={{0,2},{2,0},{1,3},{3,1},{4,6},{6,4},{5,7},{7,5},{8,10},{10,8},{9,1... | collective-permute-start | bytes 1671176 | tf_op jit(solution)/shard_map/ppermute | solution.py:368
  45.0 24.3 %all-to-all-start.1 = ((f32[64,16,128]{2,1,0:T(8,128)}), f32[64,16,128]{2,1,0:T(8,128)}, u32[]{:S(2)}, u32[]{:S(2)}) async-start(f32[64,16,128]{2,1,0:T(8,128)} %bitcast.25), calls=%async_computation.1 | async-start | bytes 1048576 | tf_op jit(solution)/shard_map/all_to_all | solution.py:367
  53.5 29.1 %collective-permute-start.14 = (f32[34,32,128]{2,1,0:T(8,128)}, f32[34,32,128]{2,1,0:T(8,128)S(1)}, u32[]{:S(2)}, u32[]{:S(2)}) collective-permute-start(f32[34,32,128]{2,1,0:T(8,128)} %collective-permute-done.10.refs_4_.refs_12_), channel_id=1, source_target_pairs={{0,1},{1,0},{2,3},{3,2},{4,5},{5,4},{6,7},{7,6},{8,9},{9,8},{10,11... | collective-permute-start | bytes 1671176 | tf_op jit(solution)/shard_map/ppermute | solution.py:301
  72.0 10.7 %collective-permute-start.12 = (f32[34,32,128]{2,1,0:T(8,128)S(1)}, f32[34,32,128]{2,1,0:T(8,128)S(1)}, u32[]{:S(2)}, u32[]{:S(2)}) collective-permute-start(f32[34,32,128]{2,1,0:T(8,128)S(1)} %get-tuple-element.30.refs_0_.refs_8_), channel_id=1, source_target_pairs={{0,1},{1,0},{2,3},{3,2},{4,5},{5,4},{6,7},{7,6},{8,9},{9,8},{10,11... | collective-permute-start | bytes 1671176 | tf_op jit(solution)/shard_map/ppermute | solution.py:301
  72.1 10.7 %collective-permute-start.13 = (f32[34,32,128]{2,1,0:T(8,128)S(1)}, f32[34,32,128]{2,1,0:T(8,128)}, u32[]{:S(2)}, u32[]{:S(2)}) collective-permute-start(f32[34,32,128]{2,1,0:T(8,128)S(1)} %get-tuple-element.31.refs_2_.refs_10_), channel_id=1, source_target_pairs={{0,1},{1,0},{2,3},{3,2},{4,5},{5,4},{6,7},{7,6},{8,9},{9,8},{10,11... | collective-permute-start | bytes 1671176 | tf_op jit(solution)/shard_map/ppermute | solution.py:301
  72.5 10.2 %collective-permute-start.15 = (f32[34,32,128]{2,1,0:T(8,128)S(1)}, f32[34,32,128]{2,1,0:T(8,128)}, u32[]{:S(2)}, u32[]{:S(2)}) collective-permute-start(f32[34,32,128]{2,1,0:T(8,128)S(1)} %get-tuple-element.32.refs_6_.refs_14_), channel_id=1, source_target_pairs={{0,1},{1,0},{2,3},{3,2},{4,5},{5,4},{6,7},{7,6},{8,9},{9,8},{10,11... | collective-permute-start | bytes 1671176 | tf_op jit(solution)/shard_map/ppermute | solution.py:301
  72.6 24.6 %all-to-all-start.3 = ((f32[64,16,128]{2,1,0:T(8,128)}), f32[64,16,128]{2,1,0:T(8,128)S(1)}, u32[]{:S(2)}, u32[]{:S(2)}) async-start(f32[64,16,128]{2,1,0:T(8,128)} %get-tuple-element.35), calls=%async_computation.3 | async-start | bytes 1048576 | tf_op jit(solution)/shard_map/all_to_all | solution.py:384
  97.3 35.0 %all-to-all-start.2 = ((f32[8,512,128]{2,1,0:T(8,128)}), f32[8,512,128]{2,1,0:T(8,128)S(1)}, u32[]{:S(2)}, u32[]{:S(2)}) async-start(f32[8,512,128]{2,1,0:T(8,128)} %get-tuple-element.33), calls=%async_computation.2 | async-start | bytes 4194304 | tf_op jit(solution)/shard_map/all_to_all | solution.py:421
  103.7 3.1 %collective-permute-start.16 = (f32[2,512,128]{2,1,0:T(8,128)S(1)}, f32[2,512,128]{2,1,0:T(8,128)S(1)}, u32[]{:S(2)}, u32[]{:S(2)}) collective-permute-start(f32[2,512,128]{2,1,0:T(8,128)S(1)} %follow.3.mine), channel_id=1, source_target_pairs={{0,1},{1,0},{2,3},{3,2},{4,5},{5,4},{6,7},{7,6},{8,9},{9,8},{10,11... | collective-permute-start | bytes 1572872 | tf_op jit(solution)/shard_map/ppermute | solution.py:388
  (15 other events, 64.3 us)

commit v6 on v5

--- a/solution.py
+++ b/solution.py
@@ -55,17 +55,18 @@
             all_out[2 * blocks + h] = rhs[:, h * BLOCK : (h + 1) * BLOCK]
 
 
-def pivot_kernel(core, mine, slack, diag, *refs):
+def pivot_kernel(place, mine, slack, diag, *refs):
     kept, sent, right = refs[3], refs[4], refs[-1]
     size = diag.shape[1]
     for s in range(2):
         right[:, s * BLOCK : (s + 1) * BLOCK] = mine[:, s].reshape(size, BLOCK)
-    left = jnp.concatenate([right[:, s * BLOCK : (s + 1) * BLOCK] / slack[s : s + 1, :] for s in range(2)], axis=1)
+    own_slack = slack[:, pl.ds(pl.multiple_of(place[1] * BLOCK, BLOCK), BLOCK)]
+    left = jnp.concatenate([right[:, s * BLOCK : (s + 1) * BLOCK] / own_slack[s : s + 1] for s in range(2)], axis=1)
     rows = lax.broadcasted_iota(jnp.int32, (size, BLOCK), 0)
     cols = lax.broadcasted_iota(jnp.int32, (size, BLOCK), 1)
-    for out, place in ((kept, core[0]), (sent, 1 - core[0])):
+    for out, core in ((kept, place[2]), (sent, 1 - place[2])):
         for q in range(2):
-            first = pl.multiple_of((q + 2 * place) * BLOCK, BLOCK)
+            first = pl.multiple_of((q + 2 * core) * BLOCK, BLOCK)
             piece = dot_nt(left, right[pl.ds(first, BLOCK), :])
             out[q] = piece + jnp.where(rows == cols + first, diag[:, pl.ds(first, BLOCK)], 0.0)
 
@@ -201,21 +202,31 @@
         cols = [jnp.broadcast_to(w[first:, first + k : first + k + 1], (height, BLOCK)) for k in range(SLAB)]
         left, right = w[first : first + SLAB, :BLOCK], w[first : first + SLAB, BLOCK:]
         lower, upper = [], []
-        for k in range(SLAB):
-            pivot = cols[k][k : k + 1, :]
-            scale = lax.rsqrt(pivot)
-            inverse = 1.0 / pivot
-            for m in range(k + 1, SLAB):
-                cols[m] = cols[m] - cols[k] * (cols[k][m : m + 1, :] * inverse)
-            low = cols[k] * scale
-            u0 = left[k : k + 1, :] * scale
-            u1 = right[k : k + 1, :] * scale
-            if k + 1 < SLAB:
-                left = left - low[:SLAB] * u0
-                right = right - low[:SLAB] * u1
-            w[first + k : first + k + 1, BLOCK:] = u1
-            lower.append(low)
-            upper.append((u0, u1))
+        for k in range(0, SLAB, 2):
+            c0, c1 = cols[k], cols[k + 1]
+            a00, a10, a11 = c0[k : k + 1, :], c0[k + 1 : k + 2, :], c1[k + 1 : k + 2, :]
+            inv0 = 1.0 / a00
+            inv1 = a00 * (1.0 / (a00 * a11 - a10 * a10))
+            ratio = a10 * inv0
+            c1 = c1 - c0 * ratio
+            for m in range(k + 2, SLAB):
+                f0 = c0[m : m + 1, :] * inv0
+                f1 = (cols[k + 1][m : m + 1, :] - c0[m : m + 1, :] * ratio) * inv1
+                cols[m] = cols[m] - c0 * f0 - c1 * f1
+            s0 = lax.rsqrt(a00)
+            s1 = lax.rsqrt(a11 - a10 * ratio)
+            low0, low1 = c0 * s0, c1 * s1
+            l0, l1 = left[k : k + 1, :], left[k + 1 : k + 2, :]
+            r0, r1 = right[k : k + 1, :], right[k + 1 : k + 2, :]
+            l0, l1 = l0 * s0, (l1 - l0 * ratio) * s1
+            r0, r1 = r0 * s0, (r1 - r0 * ratio) * s1
+            if k + 2 < SLAB:
+                left = left - low0[:SLAB] * l0 - low1[:SLAB] * l1
+                right = right - low0[:SLAB] * r0 - low1[:SLAB] * r1
+            w[first + k:first + k + 1, BLOCK:] = r0
+            w[first + k + 1:first + k + 2, BLOCK:] = r1
+            lower += [low0, low1]
+            upper += [(l0, r0), (l1, r1)]
         if height > SLAB:
             rest0, rest1 = w[first + SLAB :, :BLOCK], w[first + SLAB :, BLOCK:]
             for k in range(SLAB):
@@ -225,22 +236,22 @@
             w[first + SLAB :, BLOCK:] = rest1
 
 
-def rows_of(order, k, width):
-    return pl.ds(pl.multiple_of(order[k] * width, width), width)
-
-
-def solve_kernel(core, order, mine, other, *refs):
+def rows_of(place, k, width):
+    return pl.ds(pl.multiple_of(place[3 + k] * width, width), width)
+
+
+def solve_kernel(place, mine, other, *refs):
     *pieces, _, fwd, sol, m, w, linv = refs
     size = fwd.shape[0]
     steps = size // BLOCK
     width = pieces[0].shape[1]
     for q in range(2):
-        here = pl.ds(pl.multiple_of((q + 2 * core[0]) * BLOCK, BLOCK), BLOCK)
+        here = pl.ds(pl.multiple_of((q + 2 * place[2]) * BLOCK, BLOCK), BLOCK)
         m[:, here] = mine[q]
-        here = pl.ds(pl.multiple_of((q + 2 * (1 - core[0])) * BLOCK, BLOCK), BLOCK)
+        here = pl.ds(pl.multiple_of((q + 2 * (1 - place[2])) * BLOCK, BLOCK), BLOCK)
         m[:, here] = other[q]
         for k, piece in enumerate(pieces):
-            m[rows_of(order, k, width), size + q * BLOCK : size + (q + 1) * BLOCK] = piece[q]
+            m[rows_of(place, k, width), size + q * BLOCK : size + (q + 1) * BLOCK] = piece[q]
     shape = (BLOCK, BLOCK)
     eye = (lax.broadcasted_iota(jnp.int32, shape, 0) == lax.broadcasted_iota(jnp.int32, shape, 1)).astype(F32)
 
@@ -267,22 +278,23 @@
         sol[rows, :] = dot_tn(linv[step], total)
 
 
-def directions_kernel(sol, mine, slack, scen_rhs, directions):
+def directions_kernel(place, sol, mine, slack, scen_rhs, directions):
     size = sol.shape[0]
     solved = sol[...]
+    own_slack = slack[:, pl.ds(pl.multiple_of(place[1] * BLOCK, BLOCK), BLOCK)]
     for s in range(2):
         moved = dot_tn(mine[:, s].reshape(size, BLOCK), solved)
-        divisor = jnp.broadcast_to(slack[s : s + 1, :], (BLOCK, BLOCK)).T
+        divisor = jnp.broadcast_to(own_slack[s : s + 1], (BLOCK, BLOCK)).T
         for h in range(moved.shape[1] // BLOCK):
             lanes = slice(h * BLOCK, (h + 1) * BLOCK)
             directions[s, :, lanes] = (scen_rhs[s, :, lanes] - moved[:, lanes]) / divisor
 
 
-def reduced_kernel(place, order, schur, sol, fwd, rhs, reduced, moved_sol):
-    pieces = order.shape[0]
+def reduced_kernel(place, schur, sol, fwd, rhs, reduced, moved_sol):
+    pieces = place.shape[0] - 3
     width = sol.shape[0] // pieces
     for k in range(pieces):
-        moved_sol[k * width : (k + 1) * width, :] = sol[rows_of(order, k, width), :]
+        moved_sol[k * width : (k + 1) * width, :] = sol[rows_of(place, k, width), :]
     total = schur[0]
     for k in range(1, schur.shape[0]):
         total = total + schur[k]
@@ -290,7 +302,7 @@
 
     @pl.when(place[0] == 0)
     def _():
-        reduced[0, :width] = fwd[rows_of(place, 1, width), :]
+        reduced[0, :width] = fwd[rows_of(place, -2, width), :]
 
 
 def shape_of(value):
@@ -346,10 +358,16 @@
     first = follow(masked_done, first)
     opposite = lax.ppermute(first, ("x", "core"), first_way)
 
-    slack_mine = lax.dynamic_slice_in_dim(slack, col_index * BLOCK, BLOCK, 1)
     diag = jnp.where(scen_index == 0, first_diag[:width], 0.0)
     diag = lax.dynamic_update_slice_in_dim(jnp.zeros((PW,), F32), diag, col_index * width, 0).reshape(1, PW)
-    core = core_index.reshape(1).astype(jnp.int32)
+    x, z = lax.axis_index("x"), lax.axis_index("z")
+    place = [scen_index, col_index, core_index]
+    for step, side in ((0, 0), (-1, 0), (1, 0), (0, 1), (-1, 1), (1, 1), (2, 0), (2, 1)):
+        for other_core in range(2):
+            c = core_index if other_core == 0 else 1 - core_index
+            chip_x = lax.rem(x + along + step * (1 - 2 * c), along)
+            place.append((chip_x * 2 + lax.rem(z + side, 2)) * 2 + c)
+    place = jnp.stack(place).astype(jnp.int32)
     half_shape = jax.ShapeDtypeStruct((2, PW, BLOCK), F32)
     kept, sent, second, beside = pl.pallas_call(
         pivot_kernel,
@@ -361,7 +379,7 @@
         compiler_params=PARAMS,
         cost_estimate=SHORT,
         name="pivot",
-    )(core, mine, slack_mine, diag, masked_done, second, beside)
+    )(place, mine, slack, diag, masked_done, second, beside)
 
     pair = kept + lax.ppermute(sent, "core", SWAP)
     pair = lax.all_to_all(pair.reshape(chips, 2 * PW // chips, BLOCK), ALL_CHIPS, 0, 0, tiled=True)
@@ -387,20 +405,11 @@
     half = follow(far_done, half)
     other = lax.ppermute(half, "core", SWAP)
 
-    x, z = lax.axis_index("x"), lax.axis_index("z")
-    order = []
-    for step, side in ((0, 0), (-1, 0), (1, 0), (0, 1), (-1, 1), (1, 1), (2, 0), (2, 1)):
-        for other_core in range(2):
-            c = core_index if other_core == 0 else 1 - core_index
-            chip_x = lax.rem(x + along + step * (1 - 2 * c), along)
-            order.append((chip_x * 2 + lax.rem(z + side, 2)) * 2 + c)
-    order = jnp.stack(order).astype(jnp.int32)
     pieces = near_pieces + far_pieces
     fwd, sol = pl.pallas_call(
         solve_kernel,
         grid=(1,),
         in_specs=[
-            smem,
             smem,
             pl.BlockSpec((2, PW, BLOCK), lambda t: (0, 0, 0)),
             pl.BlockSpec((2, PW, BLOCK), lambda t: (0, 0, 0)),
@@ -417,25 +426,24 @@
         compiler_params=WIDE_PARAMS,
         cost_estimate=SHORT,
         name="solve",
-    )(core, order, half, other, *pieces, far_done)
+    )(place, half, other, *pieces, far_done)
     schur = lax.all_to_all(schur, "scen", 0, 0, tiled=True)
 
     directions = pl.pallas_call(
         directions_kernel,
-        in_specs=[VMEM] * 4,
+        in_specs=[smem] + [VMEM] * 4,
         out_specs=VMEM,
         out_shape=shape_of(scen_rhs),
         compiler_params=WIDE_PARAMS,
         cost_estimate=SHORT,
         name="directions",
-    )(sol, mine, slack_mine, scen_rhs)
-
-    place = jnp.stack([scen_index, col_index]).astype(jnp.int32)
+    )(place, sol, mine, slack, scen_rhs)
+
     own_share = own_width // scens
     reduced = pl.pallas_call(
         reduced_kernel,
         grid_spec=pltpu.PrefetchScalarGridSpec(
-            num_scalar_prefetch=2,
+            num_scalar_prefetch=1,
             grid=(1,),
             in_specs=[
                 pl.BlockSpec(schur.shape, lambda t, *_: (0, 0, 0)),
@@ -447,10 +455,10 @@
             scratch_shapes=[pltpu.VMEM((PW, nrhs), F32)],
         ),
         out_shape=jax.ShapeDtypeStruct((1, own_share, nrhs), F32),
-        compiler_params=WIDE_PARAMS,
+        compiler_params=PARAMS,
         cost_estimate=SHORT,
         name="reduced",
-    )(place, order, schur, sol, fwd, rhs)
+    )(place, schur, sol, fwd, rhs)
     return reduced, directions
 
 

time: 138 us -> 137 us (level)
  Pallas kernels: 76.2 us -> 74.1 us
  waiting for transfers between devices: 3.23 us -> 5.19 us
    pallas_call x1, Pallas kernels: 3.72 us -> 1.74 us  [per_device(): pl.pallas_call(reduced_kernel, grid_spec=pltpu.PrefetchScalarGridSpec(num...]
    unnamed x36 -> x38, local copies, waits for them, and re-layouts: 5.23 us -> 5.12 us
  transfers between devices with their start and end apart: 21 -> 21, of which waited for: 4 -> 4; matrix products, arithmetic and copies ran while one was open for 3% -> 1% of each run, Pallas kernels for 51% -> 51%
where the time goes in v6:
time: 137 us; the launch traced here: 135 us
  Pallas kernels  74.1 us (54%)
  starting transfers between devices  48.2 us (35%)
  local copies, waits for them, and re-layouts  5.42 us (4%)
  waiting for transfers between devices  5.19 us (4%)
  other arithmetic  1.59 us (1%)
    pallas_call x2, Pallas kernels, schur_product(): pl.pallas_call(schur_kernel, grid=(steps,), in_specs=[pl.BlockSpec((1, 2...  27.1 us
    pallas_call x1, Pallas kernels, per_device(): pl.pallas_call(solve_kernel, grid=(1,), in_specs=[smem, pl.BlockSpec((2,...  19.9 us
    pallas_call x1, Pallas kernels, mask_parts(): pl.pallas_call(mask_kernel, grid=(STEPS,), in_specs=[pl.BlockSpec(memory_...  15.4 us
    all_to_all x1, starting transfers between devices, per_device(): lax.all_to_all(share, ALL_CHIPS, 0, 0, tiled=True).reshape(2, PW, BLOCK)  10.1 us
    all_to_all x1, starting transfers between devices, per_device(): lax.all_to_all(pair.reshape(chips, 2 * PW // chips, BLOCK), ALL_CHIPS, 0,...  8.48 us
    all_to_all x1, starting transfers between devices, per_device(): schur = lax.all_to_all(schur, 'scen', 0, 0, tiled=True)  6.42 us
    unnamed x38, local copies, waits for them, and re-layouts  5.12 us
    all_to_all x1, starting transfers between devices, per_device(): mine = lax.all_to_all(row_blocks, COL, 0, 0, tiled=True)  5.07 us
  transfers between devices with their start and end apart: 21, of which 4 were waited for; matrix products, arithmetic and copies ran while one was open for 1% of the time, Pallas kernels for 51%

profile of v6, /device:TPU:1, one launch (start us, length us, event | category | flops | bytes accessed | tf_op | source)
XLA Modules:
  0.0 135.4 jit_solution(1639463536239317963)
XLA Ops:
  0.6 2.9 %panel.1 = (f32[16,2,32,128]{3,2,1,0:T(8,128)}, f32[34,32,128]{2,1,0:T(8,128)}) custom-call(s32[2,8,16]{2,1,0:T(8,128)} %bitcast.26, f32[2,2048,1024]{2,1,0:T(8,128)} %border.3, f32[1024,256]{1,0:T(8,128)} %rhs.3), custom_call_target="tpu_custom_call" | custom-call | tf_op jit(solution)/shard_map/panel/pallas_call | solution.py:330
  3.5 3.3 %collective-permute-start.1 = (f32[34,32,128]{2,1,0:T(8,128)}, f32[34,32,128]{2,1,0:T(8,128)S(1)}, u32[]{:S(2)}, u32[]{:S(2)}) collective-permute-start(f32[34,32,128]{2,1,0:T(8,128)} %get-tuple-element.23.refs_0_), channel_id=1, source_target_pairs={{0,4},{1,13},{4,8},{5,1},{8,12},{9,5},{12,0},{13,9},{2,6},{3,15},{... | collective-permute-start | bytes 1671176 | tf_op jit(solution)/shard_map/ppermute | solution.py:354
  6.8 1.6 %collective-permute-start.4 = (f32[34,32,128]{2,1,0:T(8,128)}, f32[34,32,128]{2,1,0:T(8,128)S(1)}, u32[]{:S(2)}, u32[]{:S(2)}) collective-permute-start(f32[34,32,128]{2,1,0:T(8,128)} %get-tuple-element.23.refs_0_), channel_id=1, source_target_pairs={{0,2},{2,0},{1,3},{3,1},{4,6},{6,4},{5,7},{7,5},{8,10},{10,8},{9,1... | collective-permute-start | bytes 1671176 | tf_op jit(solution)/shard_map/ppermute | solution.py:356
  8.4 5.1 %all-to-all-start = ((f32[16,2,32,128]{3,2,1,0:T(8,128)}), f32[16,2,32,128]{3,2,1,0:T(8,128)S(1)}, u32[]{:S(2)}, u32[]{:S(2)}) async-start(f32[16,2,32,128]{3,2,1,0:T(8,128)} %get-tuple-element.20._), calls=%async_computation | async-start | bytes 1048576 | tf_op jit(solution)/shard_map/all_to_all | solution.py:350
  13.8 15.4 %mask.1 = (bf16[8,1024,1024]{2,1,0:T(8,128)(2,1)}, f32[8,128]{1,0:T(8,128)}) custom-call(s32[2,8,16]{2,1,0:T(8,128)} %bitcast.27, f32[2,2048,1024]{2,1,0:T(8,128)} %border.3, f32[16,2,32,128]{3,2,1,0:T(8,128)} %get-tuple-element.20._), custom_call_target="tpu_custom_call" | custom-call | flops 1048576 | bytes 65536 | tf_op jit(solution)/shard_map/mask/pallas_call | solution.py:108
  29.9 2.7 %collective-permute-start.10 = (f32[34,32,128]{2,1,0:T(8,128)S(1)}, f32[34,32,128]{2,1,0:T(8,128)}, u32[]{:S(2)}, u32[]{:S(2)}) collective-permute-start(f32[34,32,128]{2,1,0:T(8,128)S(1)} %follow.2.refs_2_), channel_id=1, source_target_pairs={{0,4},{1,13},{4,8},{5,1},{8,12},{9,5},{12,0},{13,9},{2,6},{3,15},{... | collective-permute-start | bytes 1671176 | tf_op jit(solution)/shard_map/ppermute | solution.py:359
  33.6 2.4 %pivot.1 = (f32[2,512,128]{2,1,0:T(8,128)S(1)}, f32[2,512,128]{2,1,0:T(8,128)S(1)}, f32[34,32,128]{2,1,0:T(8,128)S(1)}, f32[34,32,128]{2,1,0:T(8,128)S(1)}) custom-call(s32[19]{0:T(128)S(1)} %stack.79.place, f32[16,2,32,128]{3,2,1,0:T(8,128)S(1)} %all-to-all-done.mine, f32[2,2048]{1,0:T(2,128)S(1)} %copy-done.11, ...), custom_call_target="tpu_custom_call", output_to_operand_aliasing={{2}: (5, {}), {3}: (6, {})} | custom-call | flops 1048576 | bytes 65536 | tf_op jit(solution)/shard_map/pivot/pallas_call | solution.py:372
  39.1 3.2 %collective-permute-start.8 = (f32[34,32,128]{2,1,0:T(8,128)S(1)}, f32[34,32,128]{2,1,0:T(8,128)S(1)}, u32[]{:S(2)}, u32[]{:S(2)}) collective-permute-start(f32[34,32,128]{2,1,0:T(8,128)S(1)} %get-tuple-element.25.refs_6_), channel_id=1, source_target_pairs={{0,4},{1,13},{4,8},{5,1},{8,12},{9,5},{12,0},{13,9},{2,6},{3,15},{... | collective-permute-start | bytes 1671176 | tf_op jit(solution)/shard_map/ppermute | solution.py:387
  42.3 1.2 collective-permute-start.11
  44.4 8.5 %all-to-all-start.1 = ((f32[64,16,128]{2,1,0:T(8,128)}), f32[64,16,128]{2,1,0:T(8,128)}, u32[]{:S(2)}, u32[]{:S(2)}) async-start(f32[64,16,128]{2,1,0:T(8,128)} %bitcast.25), calls=%async_computation.1 | async-start | bytes 1048576 | tf_op jit(solution)/shard_map/all_to_all | solution.py:385
  52.9 2.3 %collective-permute-start.14 = (f32[34,32,128]{2,1,0:T(8,128)}, f32[34,32,128]{2,1,0:T(8,128)}, u32[]{:S(2)}, u32[]{:S(2)}) collective-permute-start(f32[34,32,128]{2,1,0:T(8,128)} %collective-permute-done.10.refs_4_.refs_12_), channel_id=1, source_target_pairs={{0,1},{1,0},{2,3},{3,2},{4,5},{5,4},{6,7},{7,6},{8,9},{9,8},{10,11... | collective-permute-start | bytes 1671176 | tf_op jit(solution)/shard_map/ppermute | solution.py:313
  55.2 13.6 %schur.2 = (f32[8,512,128]{2,1,0:T(8,128)}, f32[8,128]{1,0:T(8,128)}) custom-call(bf16[8,1024,1024]{2,1,0:T(8,128)(2,1)} %get-tuple-element.21.masked, f32[2,2048]{1,0:T(2,128)} %slack.7, f32[8,128]{1,0:T(8,128)} %get-tuple-element.22.refs_0_._, f32[34,32,128]{2,1,0:T(8,128)} %get-tuple-element.23.refs_0_, f32[34,32,128]{2,1,0:T(8,128)} %collective-permute-done.refs_1_, ...), custom_call_target="tpu_custom_call" | custom-call | flops 1048576 | bytes 65536 | tf_op jit(solution)/shard_map/schur/pallas_call | solution.py:180
  69.5 1.9 %total.1 = (f32[64,16,128]{2,1,0:T(8,128)}, f32[34,32,128]{2,1,0:T(8,128)S(1)}, f32[34,32,128]{2,1,0:T(8,128)S(1)}, f32[34,32,128]{2,1,0:T(8,128)S(1)}) custom-call(f32[64,16,128]{2,1,0:T(8,128)} %all-to-all-done.1.pair, f32[8,128]{1,0:T(8,128)S(1)} %copy-done.16, ...), custom_call_target="tpu_custom_call", output_to_operand_aliasing={{1}: (2, {}), {2}: (3, {}), {3}: (4, {})} | custom-call | flops 1048576 | bytes 65536 | tf_op jit(solution)/shard_map/total/pallas_call | solution.py:392
  72.1 10.1 %all-to-all-start.3 = ((f32[64,16,128]{2,1,0:T(8,128)}), f32[64,16,128]{2,1,0:T(8,128)S(1)}, u32[]{:S(2)}, u32[]{:S(2)}) async-start(f32[64,16,128]{2,1,0:T(8,128)} %get-tuple-element.35), calls=%async_computation.3 | async-start | bytes 1048576 | tf_op jit(solution)/shard_map/all_to_all | solution.py:402
  83.0 13.6 %schur.3 = (f32[8,512,128]{2,1,0:T(8,128)}, f32[8,128]{1,0:T(8,128)}) custom-call(bf16[8,1024,1024]{2,1,0:T(8,128)(2,1)} %get-tuple-element.21.masked, f32[2,2048]{1,0:T(2,128)} %slack.7, f32[8,512,128]{2,1,0:T(8,128)} %get-tuple-element.26._, f32[34,32,128]{2,1,0:T(8,128)} %copy-done.3, f32[34,32,128]{2,1,0:T(8,128)} %copy-done.17, ...), custom_call_target="tpu_custom_call", output_to_operand_aliasing={{0}: (2, {})} | custom-call | flops 1048576 | bytes 65536 | tf_op jit(solution)/shard_map/schur/pallas_call | solution.py:180
  96.6 6.4 %all-to-all-start.2 = ((f32[8,512,128]{2,1,0:T(8,128)}), f32[8,512,128]{2,1,0:T(8,128)S(1)}, u32[]{:S(2)}, u32[]{:S(2)}) async-start(f32[8,512,128]{2,1,0:T(8,128)} %get-tuple-element.33), calls=%async_computation.2 | async-start | bytes 4194304 | tf_op jit(solution)/shard_map/all_to_all | solution.py:430
  103.0 1.5 %collective-permute-start.16 = (f32[2,512,128]{2,1,0:T(8,128)S(1)}, f32[2,512,128]{2,1,0:T(8,128)S(1)}, u32[]{:S(2)}, u32[]{:S(2)}) collective-permute-start(f32[2,512,128]{2,1,0:T(8,128)S(1)} %follow.3.mine), channel_id=1, source_target_pairs={{0,1},{1,0},{2,3},{3,2},{4,5},{5,4},{6,7},{7,6},{8,9},{9,8},{10,11... | collective-permute-start | bytes 1572872 | tf_op jit(solution)/shard_map/ppermute | solution.py:406
  104.6 1.5 %collective-permute-done.16.other = f32[2,512,128]{2,1,0:T(8,128)S(1)} collective-permute-done((f32[2,512,128]{2,1,0:T(8,128)S(1)}, f32[2,512,128]{2,1,0:T(8,128)S(1)}, u32[]{:S(2)}, u32[]{:S(2)}) %collective-permute-start.16) | collective-permute-done | bytes 524320 | tf_op jit(solution)/shard_map/ppermute | solution.py:406
  106.9 19.9 %solve.1 = (f32[512,256]{1,0:T(8,128)}, f32[512,256]{1,0:T(8,128)}) custom-call(s32[19]{0:T(128)} %copy-done.14, f32[2,512,128]{2,1,0:T(8,128)} %copy-done.7, f32[2,512,128]{2,1,0:T(8,128)} %copy-done.18, f32[34,32,128]{2,1,0:T(8,128)} %get-tuple-element.23.refs_0_, f32[34,32,128]{2,1,0:T(8,128)} %collective-permute-done.refs_1_, f32[34,32,128]{2,1,0:T(8,128)} %copy-done.5, ...), custom_call_target="tpu_custom_call" | custom-call | flops 1048576 | bytes 65536 | tf_op jit(solution)/shard_map/solve/pallas_call | solution.py:409
  126.8 2.8 %directions.1 = f32[2,128,256]{2,1,0:T(8,128)} custom-call(s32[19]{0:T(128)} %copy-done.14, f32[512,256]{1,0:T(8,128)} %get-tuple-element.36.sol, f32[16,2,32,128]{3,2,1,0:T(8,128)} %copy-done.6, f32[2,2048]{1,0:T(2,128)} %slack.7, f32[2,128,256]{2,1,0:T(8,128)} %scen_rhs.1), custom_call_target="tpu_custom_call" | custom-call | flops 1048576 | bytes 65536 | tf_op jit(solution)/shard_map/directions/pallas_call | solution.py:432
  129.6 1.9 %all-to-all-done.2.schur = f32[8,512,128]{2,1,0:T(8,128)S(1)} async-done(((f32[8,512,128]{2,1,0:T(8,128)}), f32[8,512,128]{2,1,0:T(8,128)S(1)}, u32[]{:S(2)}, u32[]{:S(2)}) %all-to-all-start.2) | async-done | bytes 2097184 | tf_op jit(solution)/shard_map/all_to_all | solution.py:430
  131.6 1.0 copy-done.9
  132.6 1.0 copy-done.10
  133.6 1.7 %reduced.1 = f32[1,128,256]{2,1,0:T(8,128)} custom-call(s32[19]{0:T(128)S(1)} %copy-done.15, f32[8,512,128]{2,1,0:T(8,128)S(1)} %all-to-all-done.2.schur, f32[512,256]{1,0:T(8,128)S(1)} %copy-done.9, f32[512,256]{1,0:T(8,128)S(1)} %copy-done.10, f32[1024,256]{1,0:T(8,128)S(1)} %copy-done.8), custom_call_target="tpu_custom_call" | custom-call | flops 1048576 | bytes 65536 | tf_op jit(solution)/shard_map/reduced/pallas_call | solution.py:443
  (72 shorter events, 8.9 us)
Async XLA Ops:
  3.5 25.7 %collective-permute-start.1 = (f32[34,32,128]{2,1,0:T(8,128)}, f32[34,32,128]{2,1,0:T(8,128)S(1)}, u32[]{:S(2)}, u32[]{:S(2)}) collective-permute-start(f32[34,32,128]{2,1,0:T(8,128)} %get-tuple-element.23.refs_0_), channel_id=1, source_target_pairs={{0,4},{1,13},{4,8},{5,1},{8,12},{9,5},{12,0},{13,9},{2,6},{3,15},{... | collective-permute-start | bytes 1671176 | tf_op jit(solution)/shard_map/ppermute | solution.py:354
  6.8 26.8 %collective-permute-start.4 = (f32[34,32,128]{2,1,0:T(8,128)}, f32[34,32,128]{2,1,0:T(8,128)S(1)}, u32[]{:S(2)}, u32[]{:S(2)}) collective-permute-start(f32[34,32,128]{2,1,0:T(8,128)} %get-tuple-element.23.refs_0_), channel_id=1, source_target_pairs={{0,2},{2,0},{1,3},{3,1},{4,6},{6,4},{5,7},{7,5},{8,10},{10,8},{9,1... | collective-permute-start | bytes 1671176 | tf_op jit(solution)/shard_map/ppermute | solution.py:356
  8.4 25.2 %collective-permute-start.3 = (f32[34,32,128]{2,1,0:T(8,128)}, f32[34,32,128]{2,1,0:T(8,128)S(1)}, u32[]{:S(2)}, u32[]{:S(2)}) collective-permute-start(f32[34,32,128]{2,1,0:T(8,128)} %get-tuple-element.23.refs_0_), channel_id=1, source_target_pairs={{4,0},{13,1},{8,4},{1,5},{12,8},{5,9},{0,12},{9,13},{6,2},{15,3},{... | collective-permute-start | bytes 1671176 | tf_op jit(solution)/shard_map/ppermute | solution.py:355
  8.4 25.2 %all-to-all-start = ((f32[16,2,32,128]{3,2,1,0:T(8,128)}), f32[16,2,32,128]{3,2,1,0:T(8,128)S(1)}, u32[]{:S(2)}, u32[]{:S(2)}) async-start(f32[16,2,32,128]{3,2,1,0:T(8,128)} %get-tuple-element.20._), calls=%async_computation | async-start | bytes 1048576 | tf_op jit(solution)/shard_map/all_to_all | solution.py:350
  13.5 23.1 %collective-permute-start = (f32[34,32,128]{2,1,0:T(8,128)}, f32[34,32,128]{2,1,0:T(8,128)}, u32[]{:S(2)}, u32[]{:S(2)}) collective-permute-start(f32[34,32,128]{2,1,0:T(8,128)} %get-tuple-element.23.refs_0_), channel_id=1, source_target_pairs={{0,1},{1,0},{2,3},{3,2},{4,5},{5,4},{6,7},{7,6},{8,9},{9,8},{10,11... | collective-permute-start | bytes 1671176 | tf_op jit(solution)/shard_map/ppermute | solution.py:313
  13.8 19.8 %copy-start.11 = (f32[2,2048]{1,0:T(2,128)S(1)}, f32[2,2048]{1,0:T(2,128)}, u32[]{:S(2)}) copy-start(f32[2,2048]{1,0:T(2,128)} %slack.7) | copy-start | bytes 49156
  29.9 9.2 %collective-permute-start.10 = (f32[34,32,128]{2,1,0:T(8,128)S(1)}, f32[34,32,128]{2,1,0:T(8,128)}, u32[]{:S(2)}, u32[]{:S(2)}) collective-permute-start(f32[34,32,128]{2,1,0:T(8,128)S(1)} %follow.2.refs_2_), channel_id=1, source_target_pairs={{0,4},{1,13},{4,8},{5,1},{8,12},{9,5},{12,0},{13,9},{2,6},{3,15},{... | collective-permute-start | bytes 1671176 | tf_op jit(solution)/shard_map/ppermute | solution.py:359
  32.6 9.7 %collective-permute-start.2 = (f32[34,32,128]{2,1,0:T(8,128)S(1)}, f32[34,32,128]{2,1,0:T(8,128)}, u32[]{:S(2)}, u32[]{:S(2)}) collective-permute-start(f32[34,32,128]{2,1,0:T(8,128)S(1)} %follow.2.refs_2_), channel_id=1, source_target_pairs={{0,1},{1,0},{2,3},{3,2},{4,5},{5,4},{6,7},{7,6},{8,9},{9,8},{10,11... | collective-permute-start | bytes 1671176 | tf_op jit(solution)/shard_map/ppermute | solution.py:313
  36.0 19.2 %copy-start = (f32[34,32,128]{2,1,0:T(8,128)}, f32[34,32,128]{2,1,0:T(8,128)S(1)}, u32[]{:S(2)}) copy-start(f32[34,32,128]{2,1,0:T(8,128)S(1)} %get-tuple-element.25.refs_6_) | copy-start | bytes 1671172
  36.1 2.0 %collective-permute-start.7 = (f32[2,512,128]{2,1,0:T(8,128)S(1)}, f32[2,512,128]{2,1,0:T(8,128)S(1)}, u32[]{:S(2)}, u32[]{:S(2)}) collective-permute-start(f32[2,512,128]{2,1,0:T(8,128)S(1)} %get-tuple-element.28), channel_id=1, source_target_pairs={{0,1},{1,0},{2,3},{3,2},{4,5},{5,4},{6,7},{7,6},{8,9},{9,8},{10,11... | collective-permute-start | bytes 1572872 | tf_op jit(solution)/shard_map/ppermute | solution.py:384
  36.5 16.4 %collective-permute-start.5 = (f32[34,32,128]{2,1,0:T(8,128)S(1)}, f32[34,32,128]{2,1,0:T(8,128)}, u32[]{:S(2)}, u32[]{:S(2)}) collective-permute-start(f32[34,32,128]{2,1,0:T(8,128)S(1)} %get-tuple-element.24.refs_4_), channel_id=1, source_target_pairs={{0,1},{1,0},{2,3},{3,2},{4,5},{5,4},{6,7},{7,6},{8,9},{9,8},{10,11... | collective-permute-start | bytes 1671176 | tf_op jit(solution)/shard_map/ppermute | solution.py:313
  36.6 18.5 %collective-permute-start.6 = (f32[34,32,128]{2,1,0:T(8,128)S(1)}, f32[34,32,128]{2,1,0:T(8,128)}, u32[]{:S(2)}, u32[]{:S(2)}) collective-permute-start(f32[34,32,128]{2,1,0:T(8,128)S(1)} %get-tuple-element.25.refs_6_), channel_id=1, source_target_pairs={{0,1},{1,0},{2,3},{3,2},{4,5},{5,4},{6,7},{7,6},{8,9},{9,8},{10,11... | collective-permute-start | bytes 1671176 | tf_op jit(solution)/shard_map/ppermute | solution.py:313
  38.1 30.7 %collective-permute-start.9 = (f32[34,32,128]{2,1,0:T(8,128)S(1)}, f32[34,32,128]{2,1,0:T(8,128)S(1)}, u32[]{:S(2)}, u32[]{:S(2)}) collective-permute-start(f32[34,32,128]{2,1,0:T(8,128)S(1)} %get-tuple-element.25.refs_6_), channel_id=1, source_target_pairs={{4,0},{13,1},{8,4},{1,5},{12,8},{5,9},{0,12},{9,13},{6,2},{15,3},{... | collective-permute-start | bytes 1671176 | tf_op jit(solution)/shard_map/ppermute | solution.py:388
  39.1 29.7 %collective-permute-start.8 = (f32[34,32,128]{2,1,0:T(8,128)S(1)}, f32[34,32,128]{2,1,0:T(8,128)S(1)}, u32[]{:S(2)}, u32[]{:S(2)}) collective-permute-start(f32[34,32,128]{2,1,0:T(8,128)S(1)} %get-tuple-element.25.refs_6_), channel_id=1, source_target_pairs={{0,4},{1,13},{4,8},{5,1},{8,12},{9,5},{12,0},{13,9},{2,6},{3,15},{... | collective-permute-start | bytes 1671176 | tf_op jit(solution)/shard_map/ppermute | solution.py:387
  42.3 26.5 %collective-permute-start.11 = (f32[34,32,128]{2,1,0:T(8,128)}, f32[34,32,128]{2,1,0:T(8,128)S(1)}, u32[]{:S(2)}, u32[]{:S(2)}) collective-permute-start(f32[34,32,128]{2,1,0:T(8,128)} %collective-permute-done.10.refs_4_.refs_12_), channel_id=1, source_target_pairs={{0,2},{2,0},{1,3},{3,1},{4,6},{6,4},{5,7},{7,5},{8,10},{10,8},{9,1... | collective-permute-start | bytes 1671176 | tf_op jit(solution)/shard_map/ppermute | solution.py:386
  44.4 24.4 %all-to-all-start.1 = ((f32[64,16,128]{2,1,0:T(8,128)}), f32[64,16,128]{2,1,0:T(8,128)}, u32[]{:S(2)}, u32[]{:S(2)}) async-start(f32[64,16,128]{2,1,0:T(8,128)} %bitcast.25), calls=%async_computation.1 | async-start | bytes 1048576 | tf_op jit(solution)/shard_map/all_to_all | solution.py:385
  52.9 29.2 %collective-permute-start.14 = (f32[34,32,128]{2,1,0:T(8,128)}, f32[34,32,128]{2,1,0:T(8,128)}, u32[]{:S(2)}, u32[]{:S(2)}) collective-permute-start(f32[34,32,128]{2,1,0:T(8,128)} %collective-permute-done.10.refs_4_.refs_12_), channel_id=1, source_target_pairs={{0,1},{1,0},{2,3},{3,2},{4,5},{5,4},{6,7},{7,6},{8,9},{9,8},{10,11... | collective-permute-start | bytes 1671176 | tf_op jit(solution)/shard_map/ppermute | solution.py:313
  71.5 10.7 %collective-permute-start.12 = (f32[34,32,128]{2,1,0:T(8,128)S(1)}, f32[34,32,128]{2,1,0:T(8,128)S(1)}, u32[]{:S(2)}, u32[]{:S(2)}) collective-permute-start(f32[34,32,128]{2,1,0:T(8,128)S(1)} %get-tuple-element.30.refs_0_.refs_8_), channel_id=1, source_target_pairs={{0,1},{1,0},{2,3},{3,2},{4,5},{5,4},{6,7},{7,6},{8,9},{9,8},{10,11... | collective-permute-start | bytes 1671176 | tf_op jit(solution)/shard_map/ppermute | solution.py:313
  71.5 10.7 %collective-permute-start.13 = (f32[34,32,128]{2,1,0:T(8,128)S(1)}, f32[34,32,128]{2,1,0:T(8,128)}, u32[]{:S(2)}, u32[]{:S(2)}) collective-permute-start(f32[34,32,128]{2,1,0:T(8,128)S(1)} %get-tuple-element.31.refs_2_.refs_10_), channel_id=1, source_target_pairs={{0,1},{1,0},{2,3},{3,2},{4,5},{5,4},{6,7},{7,6},{8,9},{9,8},{10,11... | collective-permute-start | bytes 1671176 | tf_op jit(solution)/shard_map/ppermute | solution.py:313
  72.0 10.2 %collective-permute-start.15 = (f32[34,32,128]{2,1,0:T(8,128)S(1)}, f32[34,32,128]{2,1,0:T(8,128)}, u32[]{:S(2)}, u32[]{:S(2)}) collective-permute-start(f32[34,32,128]{2,1,0:T(8,128)S(1)} %get-tuple-element.32.refs_6_.refs_14_), channel_id=1, source_target_pairs={{0,1},{1,0},{2,3},{3,2},{4,5},{5,4},{6,7},{7,6},{8,9},{9,8},{10,11... | collective-permute-start | bytes 1671176 | tf_op jit(solution)/shard_map/ppermute | solution.py:313
  72.1 24.5 %all-to-all-start.3 = ((f32[64,16,128]{2,1,0:T(8,128)}), f32[64,16,128]{2,1,0:T(8,128)S(1)}, u32[]{:S(2)}, u32[]{:S(2)}) async-start(f32[64,16,128]{2,1,0:T(8,128)} %get-tuple-element.35), calls=%async_computation.3 | async-start | bytes 1048576 | tf_op jit(solution)/shard_map/all_to_all | solution.py:402
  96.6 35.0 %all-to-all-start.2 = ((f32[8,512,128]{2,1,0:T(8,128)}), f32[8,512,128]{2,1,0:T(8,128)S(1)}, u32[]{:S(2)}, u32[]{:S(2)}) async-start(f32[8,512,128]{2,1,0:T(8,128)} %get-tuple-element.33), calls=%async_computation.2 | async-start | bytes 4194304 | tf_op jit(solution)/shard_map/all_to_all | solution.py:430
  103.0 28.5 %copy-start.15 = (s32[19]{0:T(128)S(1)}, s32[19]{0:T(128)}, u32[]{:S(2)}) copy-start(s32[19]{0:T(128)} %copy-done.14) | copy-start | bytes 232
  103.0 3.1 %collective-permute-start.16 = (f32[2,512,128]{2,1,0:T(8,128)S(1)}, f32[2,512,128]{2,1,0:T(8,128)S(1)}, u32[]{:S(2)}, u32[]{:S(2)}) collective-permute-start(f32[2,512,128]{2,1,0:T(8,128)S(1)} %follow.3.mine), channel_id=1, source_target_pairs={{0,1},{1,0},{2,3},{3,2},{4,5},{5,4},{6,7},{7,6},{8,9},{9,8},{10,11... | collective-permute-start | bytes 1572872 | tf_op jit(solution)/shard_map/ppermute | solution.py:406
  (16 other events, 97.4 us)

commit v7 on v6

--- a/solution.py
+++ b/solution.py
@@ -57,7 +57,14 @@
 
 def pivot_kernel(place, mine, slack, diag, *refs):
     kept, sent, right = refs[3], refs[4], refs[-1]
-    size = diag.shape[1]
+    size = right.shape[0]
+    width = mine.shape[2]
+    per_block = BLOCK // width
+    shift = lax.rem(place[1], per_block) * width
+    lanes = lax.broadcasted_iota(jnp.int32, diag.shape, 1)
+    own_lanes = (lanes >= shift) & (lanes < shift + width) & (place[0] == 0)
+    own_diag = jnp.where(own_lanes, pltpu.roll(jnp.broadcast_to(diag[0:1, :], diag.shape), shift, axis=1), 0.0)[0:1]
+    own_block = lax.div(place[1], per_block) * BLOCK
     for s in range(2):
         right[:, s * BLOCK : (s + 1) * BLOCK] = mine[:, s].reshape(size, BLOCK)
     own_slack = slack[:, pl.ds(pl.multiple_of(place[1] * BLOCK, BLOCK), BLOCK)]
@@ -68,7 +75,7 @@
         for q in range(2):
             first = pl.multiple_of((q + 2 * core) * BLOCK, BLOCK)
             piece = dot_nt(left, right[pl.ds(first, BLOCK), :])
-            out[q] = piece + jnp.where(rows == cols + first, diag[:, pl.ds(first, BLOCK)], 0.0)
+            out[q] = piece + jnp.where((rows == cols + first) & (first == own_block), own_diag, 0.0)
 
 
 def total_kernel(pair, *refs):
@@ -241,8 +248,8 @@
 
 
 def solve_kernel(place, mine, other, *refs):
-    *pieces, _, fwd, sol, m, w, linv = refs
-    size = fwd.shape[0]
+    *pieces, _, sol, m, w, linv = refs
+    size = m.shape[0]
     steps = size // BLOCK
     width = pieces[0].shape[1]
     for q in range(2):
@@ -268,19 +275,19 @@
             first = later * BLOCK
             there = slice(first, first + BLOCK)
             m[there, first:] = m[there, first:] - dot_tn(m[here, there], m[here, first:])
-    fwd[...] = m[:, size:]
+    sol[size:, :] = m[rows_of(place, -2, width), size:]
     for step in reversed(range(steps)):
         rows = slice(step * BLOCK, (step + 1) * BLOCK)
         total = m[rows, size:]
         if step + 1 < steps:
             after = (step + 1) * BLOCK
-            total = total - dot_nn(m[rows, after:size], sol[after:, :])
+            total = total - dot_nn(m[rows, after:size], sol[after:size, :])
         sol[rows, :] = dot_tn(linv[step], total)
 
 
 def directions_kernel(place, sol, mine, slack, scen_rhs, directions):
-    size = sol.shape[0]
-    solved = sol[...]
+    size = mine.shape[0] * mine.shape[2]
+    solved = sol[:size, :]
     own_slack = slack[:, pl.ds(pl.multiple_of(place[1] * BLOCK, BLOCK), BLOCK)]
     for s in range(2):
         moved = dot_tn(mine[:, s].reshape(size, BLOCK), solved)
@@ -290,9 +297,9 @@
             directions[s, :, lanes] = (scen_rhs[s, :, lanes] - moved[:, lanes]) / divisor
 
 
-def reduced_kernel(place, schur, sol, fwd, rhs, reduced, moved_sol):
+def reduced_kernel(place, schur, sol, rhs, reduced, moved_sol):
     pieces = place.shape[0] - 3
-    width = sol.shape[0] // pieces
+    width = moved_sol.shape[0] // pieces
     for k in range(pieces):
         moved_sol[k * width : (k + 1) * width, :] = sol[rows_of(place, k, width), :]
     total = schur[0]
@@ -302,7 +309,7 @@
 
     @pl.when(place[0] == 0)
     def _():
-        reduced[0, :width] = fwd[rows_of(place, -2, width), :]
+        reduced[0, :width] = sol[pieces * width :, :]
 
 
 def shape_of(value):
@@ -358,8 +365,7 @@
     first = follow(masked_done, first)
     opposite = lax.ppermute(first, ("x", "core"), first_way)
 
-    diag = jnp.where(scen_index == 0, first_diag[:width], 0.0)
-    diag = lax.dynamic_update_slice_in_dim(jnp.zeros((PW,), F32), diag, col_index * width, 0).reshape(1, PW)
+    diag = first_diag.reshape(-1, BLOCK)
     x, z = lax.axis_index("x"), lax.axis_index("z")
     place = [scen_index, col_index, core_index]
     for step, side in ((0, 0), (-1, 0), (1, 0), (0, 1), (-1, 1), (1, 1), (2, 0), (2, 1)):
@@ -406,7 +412,7 @@
     other = lax.ppermute(half, "core", SWAP)
 
     pieces = near_pieces + far_pieces
-    fwd, sol = pl.pallas_call(
+    sol = pl.pallas_call(
         solve_kernel,
         grid=(1,),
         in_specs=[
@@ -416,8 +422,8 @@
         ]
         + [pl.BlockSpec((2, width, BLOCK), lambda t: (own * blocks // 2, 0, 0))] * len(pieces)
         + [ANY],
-        out_specs=[pl.BlockSpec((PW, nrhs), lambda t: (0, 0))] * 2,
-        out_shape=[jax.ShapeDtypeStruct((PW, nrhs), F32)] * 2,
+        out_specs=pl.BlockSpec((PW + width, nrhs), lambda t: (0, 0)),
+        out_shape=jax.ShapeDtypeStruct((PW + width, nrhs), F32),
         scratch_shapes=[
             pltpu.VMEM((PW, PW + nrhs), F32),
             pltpu.VMEM((BLOCK, 2 * BLOCK), F32),
@@ -447,8 +453,7 @@
             grid=(1,),
             in_specs=[
                 pl.BlockSpec(schur.shape, lambda t, *_: (0, 0, 0)),
-                pl.BlockSpec((PW, nrhs), lambda t, *_: (0, 0)),
-                pl.BlockSpec((PW, nrhs), lambda t, *_: (0, 0)),
+                pl.BlockSpec((PW + width, nrhs), lambda t, *_: (0, 0)),
                 pl.BlockSpec((own_share, nrhs), lambda t, place, *_: (place[0], 0)),
             ],
             out_specs=pl.BlockSpec((1, own_share, nrhs), lambda t, *_: (0, 0, 0)),
@@ -458,7 +463,7 @@
         compiler_params=PARAMS,
         cost_estimate=SHORT,
         name="reduced",
-    )(place, schur, sol, fwd, rhs)
+    )(place, schur, sol, rhs)
     return reduced, directions
 
 

time: 137 us -> 136 us (level)
  no operation moved by 1% of the time
where the time goes in v7:
time: 136 us; the launch traced here: 135 us
  Pallas kernels  74 us (54%)
  starting transfers between devices  49.1 us (36%)
  waiting for transfers between devices  6.05 us (4%)
  local copies, waits for them, and re-layouts  4.2 us (3%)
    pallas_call x2, Pallas kernels, schur_product(): pl.pallas_call(schur_kernel, grid=(steps,), in_specs=[pl.BlockSpec((1, 2...  27.1 us
    pallas_call x1, Pallas kernels, per_device(): pl.pallas_call(solve_kernel, grid=(1,), in_specs=[smem, pl.BlockSpec((2,...  19.9 us
    pallas_call x1, Pallas kernels, mask_parts(): pl.pallas_call(mask_kernel, grid=(STEPS,), in_specs=[pl.BlockSpec(memory_...  15.3 us
    all_to_all x1, starting transfers between devices, per_device(): lax.all_to_all(share, ALL_CHIPS, 0, 0, tiled=True).reshape(2, PW, BLOCK)  10.1 us
    all_to_all x1, starting transfers between devices, per_device(): lax.all_to_all(pair.reshape(chips, 2 * PW // chips, BLOCK), ALL_CHIPS, 0,...  8.48 us
    all_to_all x1, starting transfers between devices, per_device(): schur = lax.all_to_all(schur, 'scen', 0, 0, tiled=True)  6.42 us
    all_to_all x1, starting transfers between devices, per_device(): mine = lax.all_to_all(row_blocks, COL, 0, 0, tiled=True)  5.07 us
    ppermute x8, starting transfers between devices, with_other_core(): lax.ppermute(piece, 'core', SWAP)  4.58 us
  transfers between devices with their start and end apart: 21, of which 4 were waited for; matrix products, arithmetic and copies ran while one was open for 1% of the time, Pallas kernels for 51%

profile of v7, /device:TPU:1, one launch (start us, length us, event | category | flops | bytes accessed | tf_op | source)
XLA Modules:
  0.0 135.2 jit_solution(10519379992430206532)
XLA Ops:
  0.6 2.8 %panel.1 = (f32[16,2,32,128]{3,2,1,0:T(8,128)}, f32[34,32,128]{2,1,0:T(8,128)}) custom-call(s32[2,8,16]{2,1,0:T(8,128)} %bitcast.26, f32[2,2048,1024]{2,1,0:T(8,128)} %border.3, f32[1024,256]{1,0:T(8,128)} %rhs.3), custom_call_target="tpu_custom_call" | custom-call | tf_op jit(solution)/shard_map/panel/pallas_call | solution.py:337
  3.5 3.3 %collective-permute-start.1 = (f32[34,32,128]{2,1,0:T(8,128)}, f32[34,32,128]{2,1,0:T(8,128)S(1)}, u32[]{:S(2)}, u32[]{:S(2)}) collective-permute-start(f32[34,32,128]{2,1,0:T(8,128)} %get-tuple-element.21.refs_0_), channel_id=1, source_target_pairs={{0,4},{1,13},{4,8},{5,1},{8,12},{9,5},{12,0},{13,9},{2,6},{3,15},{... | collective-permute-start | bytes 1671176 | tf_op jit(solution)/shard_map/ppermute | solution.py:361
  6.8 1.6 %collective-permute-start.4 = (f32[34,32,128]{2,1,0:T(8,128)}, f32[34,32,128]{2,1,0:T(8,128)S(1)}, u32[]{:S(2)}, u32[]{:S(2)}) collective-permute-start(f32[34,32,128]{2,1,0:T(8,128)} %get-tuple-element.21.refs_0_), channel_id=1, source_target_pairs={{0,2},{2,0},{1,3},{3,1},{4,6},{6,4},{5,7},{7,5},{8,10},{10,8},{9,1... | collective-permute-start | bytes 1671176 | tf_op jit(solution)/shard_map/ppermute | solution.py:363
  8.4 5.1 %all-to-all-start = ((f32[16,2,32,128]{3,2,1,0:T(8,128)}), f32[16,2,32,128]{3,2,1,0:T(8,128)S(1)}, u32[]{:S(2)}, u32[]{:S(2)}) async-start(f32[16,2,32,128]{3,2,1,0:T(8,128)} %get-tuple-element.18._), calls=%async_computation | async-start | bytes 1048576 | tf_op jit(solution)/shard_map/all_to_all | solution.py:357
  13.8 15.3 %mask.1 = (bf16[8,1024,1024]{2,1,0:T(8,128)(2,1)}, f32[8,128]{1,0:T(8,128)}) custom-call(s32[2,8,16]{2,1,0:T(8,128)} %bitcast.27, f32[2,2048,1024]{2,1,0:T(8,128)} %border.3, f32[16,2,32,128]{3,2,1,0:T(8,128)} %get-tuple-element.18._), custom_call_target="tpu_custom_call" | custom-call | flops 1048576 | bytes 65536 | tf_op jit(solution)/shard_map/mask/pallas_call | solution.py:115
  29.8 2.8 %collective-permute-start.10 = (f32[34,32,128]{2,1,0:T(8,128)S(1)}, f32[34,32,128]{2,1,0:T(8,128)}, u32[]{:S(2)}, u32[]{:S(2)}) collective-permute-start(f32[34,32,128]{2,1,0:T(8,128)S(1)} %follow.2.refs_2_), channel_id=1, source_target_pairs={{0,4},{1,13},{4,8},{5,1},{8,12},{9,5},{12,0},{13,9},{2,6},{3,15},{... | collective-permute-start | bytes 1671176 | tf_op jit(solution)/shard_map/ppermute | solution.py:366
  32.8 2.4 %pivot.1 = (f32[2,512,128]{2,1,0:T(8,128)S(1)}, f32[2,512,128]{2,1,0:T(8,128)S(1)}, f32[34,32,128]{2,1,0:T(8,128)S(1)}, f32[34,32,128]{2,1,0:T(8,128)S(1)}) custom-call(s32[19]{0:T(128)S(1)} %stack.79.place, f32[16,2,32,128]{3,2,1,0:T(8,128)S(1)} %all-to-all-done.mine, f32[2,2048]{1,0:T(2,128)S(1)} %copy-done.10, ...), custom_call_target="tpu_custom_call", output_to_operand_aliasing={{2}: (5, {}), {3}: (6, {})} | custom-call | flops 1048576 | bytes 65536 | tf_op jit(solution)/shard_map/pivot/pallas_call | solution.py:378
  37.6 1.5 %collective-permute-done.10.refs_4_.refs_12_ = f32[34,32,128]{2,1,0:T(8,128)} collective-permute-done((f32[34,32,128]{2,1,0:T(8,128)S(1)}, f32[34,32,128]{2,1,0:T(8,128)}, u32[]{:S(2)}, u32[]{:S(2)}) %collective-permute-start.10) | collective-permute-done | bytes 557088 | tf_op jit(solution)/shard_map/ppermute | solution.py:366
  39.1 3.2 %collective-permute-start.8 = (f32[34,32,128]{2,1,0:T(8,128)S(1)}, f32[34,32,128]{2,1,0:T(8,128)S(1)}, u32[]{:S(2)}, u32[]{:S(2)}) collective-permute-start(f32[34,32,128]{2,1,0:T(8,128)S(1)} %get-tuple-element.23.refs_6_), channel_id=1, source_target_pairs={{0,4},{1,13},{4,8},{5,1},{8,12},{9,5},{12,0},{13,9},{2,6},{3,15},{... | collective-permute-start | bytes 1671176 | tf_op jit(solution)/shard_map/ppermute | solution.py:393
  42.4 1.2 collective-permute-start.11
  44.4 8.5 %all-to-all-start.1 = ((f32[64,16,128]{2,1,0:T(8,128)}), f32[64,16,128]{2,1,0:T(8,128)}, u32[]{:S(2)}, u32[]{:S(2)}) async-start(f32[64,16,128]{2,1,0:T(8,128)} %bitcast.25), calls=%async_computation.1 | async-start | bytes 1048576 | tf_op jit(solution)/shard_map/all_to_all | solution.py:391
  52.9 3.2 %collective-permute-start.14 = (f32[34,32,128]{2,1,0:T(8,128)}, f32[34,32,128]{2,1,0:T(8,128)}, u32[]{:S(2)}, u32[]{:S(2)}) collective-permute-start(f32[34,32,128]{2,1,0:T(8,128)} %collective-permute-done.10.refs_4_.refs_12_), channel_id=1, source_target_pairs={{0,1},{1,0},{2,3},{3,2},{4,5},{5,4},{6,7},{7,6},{8,9},{9,8},{10,11... | collective-permute-start | bytes 1671176 | tf_op jit(solution)/shard_map/ppermute | solution.py:320
  56.1 13.5 %schur.2 = (f32[8,512,128]{2,1,0:T(8,128)}, f32[8,128]{1,0:T(8,128)}) custom-call(bf16[8,1024,1024]{2,1,0:T(8,128)(2,1)} %get-tuple-element.19.masked, f32[2,2048]{1,0:T(2,128)} %slack.7, f32[8,128]{1,0:T(8,128)} %get-tuple-element.20.refs_0_._, f32[34,32,128]{2,1,0:T(8,128)} %get-tuple-element.21.refs_0_, f32[34,32,128]{2,1,0:T(8,128)} %collective-permute-done.refs_1_, ...), custom_call_target="tpu_custom_call" | custom-call | flops 1048576 | bytes 65536 | tf_op jit(solution)/shard_map/schur/pallas_call | solution.py:187
  70.4 1.9 %total.1 = (f32[64,16,128]{2,1,0:T(8,128)}, f32[34,32,128]{2,1,0:T(8,128)S(1)}, f32[34,32,128]{2,1,0:T(8,128)S(1)}, f32[34,32,128]{2,1,0:T(8,128)S(1)}) custom-call(f32[64,16,128]{2,1,0:T(8,128)} %all-to-all-done.1.pair, f32[8,128]{1,0:T(8,128)S(1)} %copy-done.16, ...), custom_call_target="tpu_custom_call", output_to_operand_aliasing={{1}: (2, {}), {2}: (3, {}), {3}: (4, {})} | custom-call | flops 1048576 | bytes 65536 | tf_op jit(solution)/shard_map/total/pallas_call | solution.py:398
  72.9 10.1 %all-to-all-start.3 = ((f32[64,16,128]{2,1,0:T(8,128)}), f32[64,16,128]{2,1,0:T(8,128)S(1)}, u32[]{:S(2)}, u32[]{:S(2)}) async-start(f32[64,16,128]{2,1,0:T(8,128)} %get-tuple-element.33), calls=%async_computation.3 | async-start | bytes 1048576 | tf_op jit(solution)/shard_map/all_to_all | solution.py:408
  83.9 13.5 %schur.3 = (f32[8,512,128]{2,1,0:T(8,128)}, f32[8,128]{1,0:T(8,128)}) custom-call(bf16[8,1024,1024]{2,1,0:T(8,128)(2,1)} %get-tuple-element.19.masked, f32[2,2048]{1,0:T(2,128)} %slack.7, f32[8,512,128]{2,1,0:T(8,128)} %get-tuple-element.24._, f32[34,32,128]{2,1,0:T(8,128)} %copy-done.3, f32[34,32,128]{2,1,0:T(8,128)} %copy-done.17, ...), custom_call_target="tpu_custom_call", output_to_operand_aliasing={{0}: (2, {})} | custom-call | flops 1048576 | bytes 65536 | tf_op jit(solution)/shard_map/schur/pallas_call | solution.py:187
  97.4 6.4 %all-to-all-start.2 = ((f32[8,512,128]{2,1,0:T(8,128)}), f32[8,512,128]{2,1,0:T(8,128)S(1)}, u32[]{:S(2)}, u32[]{:S(2)}) async-start(f32[8,512,128]{2,1,0:T(8,128)} %get-tuple-element.31), calls=%async_computation.2 | async-start | bytes 4194304 | tf_op jit(solution)/shard_map/all_to_all | solution.py:436
  103.9 1.5 %collective-permute-start.16 = (f32[2,512,128]{2,1,0:T(8,128)S(1)}, f32[2,512,128]{2,1,0:T(8,128)S(1)}, u32[]{:S(2)}, u32[]{:S(2)}) collective-permute-start(f32[2,512,128]{2,1,0:T(8,128)S(1)} %follow.3.mine), channel_id=1, source_target_pairs={{0,1},{1,0},{2,3},{3,2},{4,5},{5,4},{6,7},{7,6},{8,9},{9,8},{10,11... | collective-permute-start | bytes 1572872 | tf_op jit(solution)/shard_map/ppermute | solution.py:412
  105.4 1.5 %collective-permute-done.16.other = f32[2,512,128]{2,1,0:T(8,128)S(1)} collective-permute-done((f32[2,512,128]{2,1,0:T(8,128)S(1)}, f32[2,512,128]{2,1,0:T(8,128)S(1)}, u32[]{:S(2)}, u32[]{:S(2)}) %collective-permute-start.16) | collective-permute-done | bytes 524320 | tf_op jit(solution)/shard_map/ppermute | solution.py:412
  107.8 19.9 %solve.1.sol = f32[544,256]{1,0:T(8,128)} custom-call(s32[19]{0:T(128)} %copy-done.13, f32[2,512,128]{2,1,0:T(8,128)} %copy-done.7, f32[2,512,128]{2,1,0:T(8,128)} %copy-done.18, f32[34,32,128]{2,1,0:T(8,128)} %get-tuple-element.21.refs_0_, f32[34,32,128]{2,1,0:T(8,128)} %collective-permute-done.refs_1_, f32[34,32,128]{2,1,0:T(8,128)} %copy-done.5, ...), custom_call_target="tpu_custom_call" | custom-call | flops 1048576 | bytes 65536 | tf_op jit(solution)/shard_map/solve/pallas_call | solution.py:415
  127.7 2.8 %directions.1 = f32[2,128,256]{2,1,0:T(8,128)} custom-call(s32[19]{0:T(128)} %copy-done.13, f32[544,256]{1,0:T(8,128)} %solve.1.sol, f32[16,2,32,128]{3,2,1,0:T(8,128)} %copy-done.8, f32[2,2048]{1,0:T(2,128)} %slack.7, f32[2,128,256]{2,1,0:T(8,128)} %scen_rhs.1), custom_call_target="tpu_custom_call" | custom-call | flops 1048576 | bytes 65536 | tf_op jit(solution)/shard_map/directions/pallas_call | solution.py:438
  130.5 1.9 %all-to-all-done.2.schur = f32[8,512,128]{2,1,0:T(8,128)S(1)} async-done(((f32[8,512,128]{2,1,0:T(8,128)}), f32[8,512,128]{2,1,0:T(8,128)S(1)}, u32[]{:S(2)}, u32[]{:S(2)}) %all-to-all-start.2) | async-done | bytes 2097184 | tf_op jit(solution)/shard_map/all_to_all | solution.py:436
  132.4 1.1 copy-done.6
  133.5 1.7 %reduced.1 = f32[1,128,256]{2,1,0:T(8,128)} custom-call(s32[19]{0:T(128)S(1)} %copy-done.14, f32[8,512,128]{2,1,0:T(8,128)S(1)} %all-to-all-done.2.schur, f32[544,256]{1,0:T(8,128)S(1)} %copy-done.6, f32[1024,256]{1,0:T(8,128)S(1)} %copy-done.9), custom_call_target="tpu_custom_call" | custom-call | flops 1048576 | bytes 65536 | tf_op jit(solution)/shard_map/reduced/pallas_call | solution.py:449
  (69 shorter events, 7.3 us)
Async XLA Ops:
  3.5 25.7 %collective-permute-start.1 = (f32[34,32,128]{2,1,0:T(8,128)}, f32[34,32,128]{2,1,0:T(8,128)S(1)}, u32[]{:S(2)}, u32[]{:S(2)}) collective-permute-start(f32[34,32,128]{2,1,0:T(8,128)} %get-tuple-element.21.refs_0_), channel_id=1, source_target_pairs={{0,4},{1,13},{4,8},{5,1},{8,12},{9,5},{12,0},{13,9},{2,6},{3,15},{... | collective-permute-start | bytes 1671176 | tf_op jit(solution)/shard_map/ppermute | solution.py:361
  6.8 26.0 %collective-permute-start.4 = (f32[34,32,128]{2,1,0:T(8,128)}, f32[34,32,128]{2,1,0:T(8,128)S(1)}, u32[]{:S(2)}, u32[]{:S(2)}) collective-permute-start(f32[34,32,128]{2,1,0:T(8,128)} %get-tuple-element.21.refs_0_), channel_id=1, source_target_pairs={{0,2},{2,0},{1,3},{3,1},{4,6},{6,4},{5,7},{7,5},{8,10},{10,8},{9,1... | collective-permute-start | bytes 1671176 | tf_op jit(solution)/shard_map/ppermute | solution.py:363
  8.4 24.4 %collective-permute-start.3 = (f32[34,32,128]{2,1,0:T(8,128)}, f32[34,32,128]{2,1,0:T(8,128)S(1)}, u32[]{:S(2)}, u32[]{:S(2)}) collective-permute-start(f32[34,32,128]{2,1,0:T(8,128)} %get-tuple-element.21.refs_0_), channel_id=1, source_target_pairs={{4,0},{13,1},{8,4},{1,5},{12,8},{5,9},{0,12},{9,13},{6,2},{15,3},{... | collective-permute-start | bytes 1671176 | tf_op jit(solution)/shard_map/ppermute | solution.py:362
  8.4 24.4 %all-to-all-start = ((f32[16,2,32,128]{3,2,1,0:T(8,128)}), f32[16,2,32,128]{3,2,1,0:T(8,128)S(1)}, u32[]{:S(2)}, u32[]{:S(2)}) async-start(f32[16,2,32,128]{3,2,1,0:T(8,128)} %get-tuple-element.18._), calls=%async_computation | async-start | bytes 1048576 | tf_op jit(solution)/shard_map/all_to_all | solution.py:357
  13.5 22.4 %collective-permute-start = (f32[34,32,128]{2,1,0:T(8,128)}, f32[34,32,128]{2,1,0:T(8,128)}, u32[]{:S(2)}, u32[]{:S(2)}) collective-permute-start(f32[34,32,128]{2,1,0:T(8,128)} %get-tuple-element.21.refs_0_), channel_id=1, source_target_pairs={{0,1},{1,0},{2,3},{3,2},{4,5},{5,4},{6,7},{7,6},{8,9},{9,8},{10,11... | collective-permute-start | bytes 1671176 | tf_op jit(solution)/shard_map/ppermute | solution.py:320
  29.8 9.3 %collective-permute-start.10 = (f32[34,32,128]{2,1,0:T(8,128)S(1)}, f32[34,32,128]{2,1,0:T(8,128)}, u32[]{:S(2)}, u32[]{:S(2)}) collective-permute-start(f32[34,32,128]{2,1,0:T(8,128)S(1)} %follow.2.refs_2_), channel_id=1, source_target_pairs={{0,4},{1,13},{4,8},{5,1},{8,12},{9,5},{12,0},{13,9},{2,6},{3,15},{... | collective-permute-start | bytes 1671176 | tf_op jit(solution)/shard_map/ppermute | solution.py:366
  32.6 9.7 %collective-permute-start.2 = (f32[34,32,128]{2,1,0:T(8,128)S(1)}, f32[34,32,128]{2,1,0:T(8,128)}, u32[]{:S(2)}, u32[]{:S(2)}) collective-permute-start(f32[34,32,128]{2,1,0:T(8,128)S(1)} %follow.2.refs_2_), channel_id=1, source_target_pairs={{0,1},{1,0},{2,3},{3,2},{4,5},{5,4},{6,7},{7,6},{8,9},{9,8},{10,11... | collective-permute-start | bytes 1671176 | tf_op jit(solution)/shard_map/ppermute | solution.py:320
  35.2 20.9 %copy-start = (f32[34,32,128]{2,1,0:T(8,128)}, f32[34,32,128]{2,1,0:T(8,128)S(1)}, u32[]{:S(2)}) copy-start(f32[34,32,128]{2,1,0:T(8,128)S(1)} %get-tuple-element.23.refs_6_) | copy-start | bytes 1671172
  35.2 20.9 %copy-start.1 = (f32[34,32,128]{2,1,0:T(8,128)}, f32[34,32,128]{2,1,0:T(8,128)S(1)}, u32[]{:S(2)}) copy-start(f32[34,32,128]{2,1,0:T(8,128)S(1)} %get-tuple-element.22.refs_4_) | copy-start | bytes 1671172
  35.2 2.1 %collective-permute-start.7 = (f32[2,512,128]{2,1,0:T(8,128)S(1)}, f32[2,512,128]{2,1,0:T(8,128)S(1)}, u32[]{:S(2)}, u32[]{:S(2)}) collective-permute-start(f32[2,512,128]{2,1,0:T(8,128)S(1)} %get-tuple-element.26), channel_id=1, source_target_pairs={{0,1},{1,0},{2,3},{3,2},{4,5},{5,4},{6,7},{7,6},{8,9},{9,8},{10,11... | collective-permute-start | bytes 1572872 | tf_op jit(solution)/shard_map/ppermute | solution.py:390
  35.8 17.1 %collective-permute-start.5 = (f32[34,32,128]{2,1,0:T(8,128)S(1)}, f32[34,32,128]{2,1,0:T(8,128)}, u32[]{:S(2)}, u32[]{:S(2)}) collective-permute-start(f32[34,32,128]{2,1,0:T(8,128)S(1)} %get-tuple-element.22.refs_4_), channel_id=1, source_target_pairs={{0,1},{1,0},{2,3},{3,2},{4,5},{5,4},{6,7},{7,6},{8,9},{9,8},{10,11... | collective-permute-start | bytes 1671176 | tf_op jit(solution)/shard_map/ppermute | solution.py:320
  35.9 20.2 %collective-permute-start.6 = (f32[34,32,128]{2,1,0:T(8,128)S(1)}, f32[34,32,128]{2,1,0:T(8,128)}, u32[]{:S(2)}, u32[]{:S(2)}) collective-permute-start(f32[34,32,128]{2,1,0:T(8,128)S(1)} %get-tuple-element.23.refs_6_), channel_id=1, source_target_pairs={{0,1},{1,0},{2,3},{3,2},{4,5},{5,4},{6,7},{7,6},{8,9},{9,8},{10,11... | collective-permute-start | bytes 1671176 | tf_op jit(solution)/shard_map/ppermute | solution.py:320
  37.3 32.3 %collective-permute-start.9 = (f32[34,32,128]{2,1,0:T(8,128)S(1)}, f32[34,32,128]{2,1,0:T(8,128)S(1)}, u32[]{:S(2)}, u32[]{:S(2)}) collective-permute-start(f32[34,32,128]{2,1,0:T(8,128)S(1)} %get-tuple-element.23.refs_6_), channel_id=1, source_target_pairs={{4,0},{13,1},{8,4},{1,5},{12,8},{5,9},{0,12},{9,13},{6,2},{15,3},{... | collective-permute-start | bytes 1671176 | tf_op jit(solution)/shard_map/ppermute | solution.py:394
  39.1 30.6 %collective-permute-start.8 = (f32[34,32,128]{2,1,0:T(8,128)S(1)}, f32[34,32,128]{2,1,0:T(8,128)S(1)}, u32[]{:S(2)}, u32[]{:S(2)}) collective-permute-start(f32[34,32,128]{2,1,0:T(8,128)S(1)} %get-tuple-element.23.refs_6_), channel_id=1, source_target_pairs={{0,4},{1,13},{4,8},{5,1},{8,12},{9,5},{12,0},{13,9},{2,6},{3,15},{... | collective-permute-start | bytes 1671176 | tf_op jit(solution)/shard_map/ppermute | solution.py:393
  42.4 27.4 %collective-permute-start.11 = (f32[34,32,128]{2,1,0:T(8,128)}, f32[34,32,128]{2,1,0:T(8,128)S(1)}, u32[]{:S(2)}, u32[]{:S(2)}) collective-permute-start(f32[34,32,128]{2,1,0:T(8,128)} %collective-permute-done.10.refs_4_.refs_12_), channel_id=1, source_target_pairs={{0,2},{2,0},{1,3},{3,1},{4,6},{6,4},{5,7},{7,5},{8,10},{10,8},{9,1... | collective-permute-start | bytes 1671176 | tf_op jit(solution)/shard_map/ppermute | solution.py:392
  44.4 25.2 %all-to-all-start.1 = ((f32[64,16,128]{2,1,0:T(8,128)}), f32[64,16,128]{2,1,0:T(8,128)}, u32[]{:S(2)}, u32[]{:S(2)}) async-start(f32[64,16,128]{2,1,0:T(8,128)} %bitcast.25), calls=%async_computation.1 | async-start | bytes 1048576 | tf_op jit(solution)/shard_map/all_to_all | solution.py:391
  52.9 30.1 %collective-permute-start.14 = (f32[34,32,128]{2,1,0:T(8,128)}, f32[34,32,128]{2,1,0:T(8,128)}, u32[]{:S(2)}, u32[]{:S(2)}) collective-permute-start(f32[34,32,128]{2,1,0:T(8,128)} %collective-permute-done.10.refs_4_.refs_12_), channel_id=1, source_target_pairs={{0,1},{1,0},{2,3},{3,2},{4,5},{5,4},{6,7},{7,6},{8,9},{9,8},{10,11... | collective-permute-start | bytes 1671176 | tf_op jit(solution)/shard_map/ppermute | solution.py:320
  72.3 10.7 %collective-permute-start.12 = (f32[34,32,128]{2,1,0:T(8,128)S(1)}, f32[34,32,128]{2,1,0:T(8,128)S(1)}, u32[]{:S(2)}, u32[]{:S(2)}) collective-permute-start(f32[34,32,128]{2,1,0:T(8,128)S(1)} %get-tuple-element.28.refs_0_.refs_8_), channel_id=1, source_target_pairs={{0,1},{1,0},{2,3},{3,2},{4,5},{5,4},{6,7},{7,6},{8,9},{9,8},{10,11... | collective-permute-start | bytes 1671176 | tf_op jit(solution)/shard_map/ppermute | solution.py:320
  72.4 10.7 %collective-permute-start.13 = (f32[34,32,128]{2,1,0:T(8,128)S(1)}, f32[34,32,128]{2,1,0:T(8,128)}, u32[]{:S(2)}, u32[]{:S(2)}) collective-permute-start(f32[34,32,128]{2,1,0:T(8,128)S(1)} %get-tuple-element.29.refs_2_.refs_10_), channel_id=1, source_target_pairs={{0,1},{1,0},{2,3},{3,2},{4,5},{5,4},{6,7},{7,6},{8,9},{9,8},{10,11... | collective-permute-start | bytes 1671176 | tf_op jit(solution)/shard_map/ppermute | solution.py:320
  72.9 10.2 %collective-permute-start.15 = (f32[34,32,128]{2,1,0:T(8,128)S(1)}, f32[34,32,128]{2,1,0:T(8,128)}, u32[]{:S(2)}, u32[]{:S(2)}) collective-permute-start(f32[34,32,128]{2,1,0:T(8,128)S(1)} %get-tuple-element.30.refs_6_.refs_14_), channel_id=1, source_target_pairs={{0,1},{1,0},{2,3},{3,2},{4,5},{5,4},{6,7},{7,6},{8,9},{9,8},{10,11... | collective-permute-start | bytes 1671176 | tf_op jit(solution)/shard_map/ppermute | solution.py:320
  72.9 24.5 %all-to-all-start.3 = ((f32[64,16,128]{2,1,0:T(8,128)}), f32[64,16,128]{2,1,0:T(8,128)S(1)}, u32[]{:S(2)}, u32[]{:S(2)}) async-start(f32[64,16,128]{2,1,0:T(8,128)} %get-tuple-element.33), calls=%async_computation.3 | async-start | bytes 1048576 | tf_op jit(solution)/shard_map/all_to_all | solution.py:408
  97.4 35.0 %all-to-all-start.2 = ((f32[8,512,128]{2,1,0:T(8,128)}), f32[8,512,128]{2,1,0:T(8,128)S(1)}, u32[]{:S(2)}, u32[]{:S(2)}) async-start(f32[8,512,128]{2,1,0:T(8,128)} %get-tuple-element.31), calls=%async_computation.2 | async-start | bytes 4194304 | tf_op jit(solution)/shard_map/all_to_all | solution.py:436
  103.9 28.5 %copy-start.14 = (s32[19]{0:T(128)S(1)}, s32[19]{0:T(128)}, u32[]{:S(2)}) copy-start(s32[19]{0:T(128)} %copy-done.13) | copy-start | bytes 232
  103.9 3.1 %collective-permute-start.16 = (f32[2,512,128]{2,1,0:T(8,128)S(1)}, f32[2,512,128]{2,1,0:T(8,128)S(1)}, u32[]{:S(2)}, u32[]{:S(2)}) collective-permute-start(f32[2,512,128]{2,1,0:T(8,128)S(1)} %follow.3.mine), channel_id=1, source_target_pairs={{0,1},{1,0},{2,3},{3,2},{4,5},{5,4},{6,7},{7,6},{8,9},{9,8},{10,11... | collective-permute-start | bytes 1572872 | tf_op jit(solution)/shard_map/ppermute | solution.py:412
  (16 other events, 116.9 us)
